TPU v7x, 128 devices: a whole 4x4x4 slice. The times are simulated.
128 devices in a mesh: row: 8 (over z, x_lo), col: 8 (over y, x_hi), rep: 2 (over core).
Axes of the slice: x: 4 (x_hi: 2, x_lo: 2; x = x_hi * 2 + x_lo), y: 4, z: 4, core: 2. Of those that a mesh axis runs over, the one named last changes fastest.
Arguments:
- row_embed: float32 [8192, 512], P(('row', 'col')), may hold values from -1.2 to 1.2
- col_embed: float32 [512, 8192], P('row', 'col'), may hold values from -1.2 to 1.2
- counts: int32 [2, 16, 4096, 4096], P(None, 'rep', 'row', 'col'), may hold values from 0 to 192, as said below
- block_rows: int32 [2, 16, 8, 8], P(None, 'rep', 'row', 'col'), may hold values from 0 to 1
- block_cols: int32 [2, 16, 8, 8], P(None, 'rep', 'row', 'col'), may hold values from 0 to 1
- row_marginals: int32 [8192], P('row'), may hold values from 131072 to 6094848
- col_marginals: int32 [8192], P('col'), may hold values from 13107 to 406323
Outputs:
- new_row_embed: float32 [8192, 512], P(('row', 'col'))
- new_col_embed: float32 [512, 8192], P('row', 'col')
Inputs may be any that keep to these rules, and one draw needn't show every extreme that they name: `counts`: zero in about a third of the entries.
All inputs are finite; a program needn't handle non-finite values.
Results may differ from a plain program's by a relative error of at most 0.0054.
Values may be sent and summed in bfloat16 or wider, within the bound.
No kernel may reach another device: no remote copies, remote signals or barrier semaphores. Data moves between devices by JAX's collectives and lax.ppermute only.
A program may use at most 128 MiB of HBM per device.

v0:
```python
import jax
import jax.numpy as jnp
from jax import lax
from jax.sharding import PartitionSpec as P


def block_grad(dots, x, log_rows, log_cols, log_total):
    base = log_total - log_rows[:, None] - log_cols[None, :]
    xf = x.astype(jnp.float32)
    seen = x > 0
    weight = 0.1 + 0.25 * jnp.sqrt(xf)
    fitted = weight * (dots - jnp.log(jnp.maximum(xf, 1.0)) - base)
    hinge = jax.nn.sigmoid(dots - base)
    return jnp.where(seen, fitted, hinge).astype(jnp.bfloat16)


def per_device(row_embed, col_embed, counts, block_rows, block_cols, row_marginals, col_marginals):
    local_total = jnp.sum(row_marginals.astype(jnp.float32))
    log_total = jnp.log(lax.psum(local_total, "row"))
    log_rows = jnp.log(row_marginals.astype(jnp.float32))
    log_cols = jnp.log(col_marginals.astype(jnp.float32))
    block = counts.shape[2]
    slots = counts.shape[1]
    for step in range(counts.shape[0]):
        slab_w = lax.all_gather(row_embed.astype(jnp.bfloat16), "col", axis=0, tiled=True)
        slab_c = lax.all_gather(col_embed.astype(jnp.bfloat16), "row", axis=0, tiled=True)
        counts_step = counts[step]
        rows_step = block_rows[step, :, 0, 0]
        cols_step = block_cols[step, :, 0, 0]

        def add_block(slot, totals):
            total_w, total_c = totals
            first_row = rows_step[slot] * block
            first_col = cols_step[slot] * block
            wblock = lax.dynamic_slice_in_dim(slab_w, first_row, block, 0)
            cblock = lax.dynamic_slice_in_dim(slab_c, first_col, block, 1)
            dots = jnp.dot(wblock, cblock, preferred_element_type=jnp.float32)
            x = lax.dynamic_index_in_dim(counts_step, slot, 0, keepdims=False)
            grad = block_grad(
                dots,
                x,
                lax.dynamic_slice_in_dim(log_rows, first_row, block),
                lax.dynamic_slice_in_dim(log_cols, first_col, block),
                log_total,
            )
            grad_w = lax.dot_general(
                grad, cblock, (((1,), (1,)), ((), ())), preferred_element_type=jnp.float32
            )
            grad_c = lax.dot_general(
                wblock, grad, (((0,), (0,)), ((), ())), preferred_element_type=jnp.float32
            )
            old_w = lax.dynamic_slice_in_dim(total_w, first_row, block, 0)
            total_w = lax.dynamic_update_slice_in_dim(total_w, old_w + grad_w, first_row, 0)
            old_c = lax.dynamic_slice_in_dim(total_c, first_col, block, 1)
            total_c = lax.dynamic_update_slice_in_dim(total_c, old_c + grad_c, first_col, 1)
            return (total_w, total_c)

        empty_w = jnp.zeros(slab_w.shape, jnp.float32)
        empty_c = jnp.zeros(slab_c.shape, jnp.float32)
        part_w, part_c = lax.fori_loop(0, slots, add_block, (empty_w, empty_c))
        share_w = lax.psum_scatter(part_w, "col", scatter_dimension=0, tiled=True)
        share_c = lax.psum_scatter(part_c, "row", scatter_dimension=0, tiled=True)
        share_w, share_c = lax.psum((share_w, share_c), "rep")
        row_embed = row_embed - 0.002 * share_w
        col_embed = col_embed - 0.002 * share_c
    return (row_embed, col_embed)


def solution(mesh):
    return jax.shard_map(
        per_device,
        mesh=mesh,
        in_specs=(
            P(("row", "col"), None),
            P("row", "col"),
            P(None, "rep", "row", "col"),
            P(None, "rep", "row", "col"),
            P(None, "rep", "row", "col"),
            P("row"),
            P("col"),
        ),
        out_specs=(P(("row", "col"), None), P("row", "col")),
        check_vma=False,
    )
```

profile of v0, /device:TPU:1, one launch (start us, length us, event | category | flops | bytes accessed | tf_op | source)
XLA Modules:
  0.0 643.9 jit_solution(5022801956698893873)
XLA Ops:
  7.2 1.6 convert_element_type.49
  8.9 1.6 convert_element_type.50
  11.9 18.8 %psum.35 = f32[]{:T(128)} all-reduce(f32[]{:T(128)} %get-tuple-element.427), channel_id=1, replica_groups=mesh['row'=8,'col'=8,'rep'=2] {'row'}, use_global_device_ids=true, to_apply=%region_1.0 | all-reduce | flops 1 | bytes 8 | tf_op jit(solution)/shard_map/psum | solution.py:19
  32.8 11.0 %slice_bitcast_fusion.1 = (s32[8,512,512]{2,1,0:T(8,128)}, s32[8,512,512]{2,1,0:T(8,128)}) fusion(s32[2,8,512,512]{3,2,1,0:T(8,128)} %param.13), kind=kLoop, calls=%fused_computation.47 | loop fusion | bytes 33554432 | tf_op jit(solution)/shard_map/squeeze | solution.py:27
  43.8 15.2 %all-gather.5.cloned.1.call-done = bf16[1024,512]{1,0:T(8,128)(2,1)} async-done(((bf16[128,512]{1,0:T(8,128)(2,1)}), bf16[1024,512]{1,0:T(8,128)(2,1)}) %all-gather.5.cloned.1.call-update) | async-done | bytes 1048592 | tf_op jit(solution)/shard_map/all_gather | solution.py:25
  59.0 38.4 %all-gather.7.cloned.1.call-done = bf16[512,1024]{1,0:T(8,128)(2,1)} async-done(((bf16[64,1024]{1,0:T(8,128)(2,1)}), bf16[512,1024]{1,0:T(8,128)(2,1)}) %all-gather.7.cloned.1.call-update) | async-done | bytes 1048592 | tf_op jit(solution)/shard_map/all_gather | solution.py:26
  97.7 1.6 broadcast.99.clone
  99.3 61.5 %while.30 = (s32[]{:T(128)}, f32[1024,512]{1,0:T(8,128)S(1)}, f32[512,1024]{1,0:T(8,128)}, s32[8]{0:T(128)S(1)}, s32[8,512,512]{2,1,0:T(8,128)}, /*index=5*/bf16...) while((s32[]{:T(128)}, f32[1024,512]{1,0:T(8,128)S(1)}, ...), condition=%wide.region_3.4_spmd, body=%wide.region_2.3_spmd.sunk | while | flops 809763328 | bytes 29897592 | solution.py:60
  101.9 2.6 fusion.68
  109.6 2.6 fusion.68
  117.3 2.6 fusion.68
  120.5 1.4 copy-done.5
  125.0 2.6 fusion.68
  132.7 2.6 fusion.68
  140.4 2.6 fusion.68
  148.1 2.6 fusion.68
  155.7 2.6 fusion.68
  160.8 1.4 copy-done.3
  162.8 77.1 %reduce-scatter.5.cloned.1.call-done = f32[128,512]{1,0:T(8,128)} async-done(((f32[1024,512]{1,0:T(8,128)}), f32[128,512]{1,0:T(8,128)}) %reduce-scatter.5.cloned.1.call-update) | async-done | bytes 262160 | tf_op jit(solution)/shard_map/reduce_scatter | solution.py:61
  239.9 55.0 %reduce-scatter.7.cloned.1.call-done = f32[64,1024]{1,0:T(8,128)} async-done(((f32[512,1024]{1,0:T(8,128)}), f32[64,1024]{1,0:T(8,128)}) %reduce-scatter.7.cloned.1.call-update) | async-done | bytes 262160 | tf_op jit(solution)/shard_map/reduce_scatter | solution.py:62
  295.0 26.4 %all-reduce.7.cloned.1.call-done = (f32[128,512]{1,0:T(8,128)}, f32[64,1024]{1,0:T(8,128)}) async-done(((f32[128,512]{1,0:T(8,128)}, f32[64,1024]{1,0:T(8,128)}), (f32[128,512]{1,0:T(8,128)}, f32[64,1024]{1,0:T(8,128)})) %all-reduce.7.cloned.1.call-update) | async-done | bytes 524304 | tf_op jit(solution)/shard_map/psum | solution.py:63
  321.4 1.6 fusion.39
  323.1 1.6 fusion.38
  324.8 35.6 %all-gather.11.cloned.1.call-done = bf16[512,1024]{1,0:T(8,128)(2,1)} async-done(((bf16[64,1024]{1,0:T(8,128)(2,1)}), bf16[512,1024]{1,0:T(8,128)(2,1)}) %all-gather.11.cloned.1.call-update) | async-done | bytes 1048592 | tf_op jit(solution)/shard_map/all_gather | solution.py:26
  360.5 52.1 %all-gather.9.cloned.1.call-done = bf16[1024,512]{1,0:T(8,128)(2,1)} async-done(((bf16[128,512]{1,0:T(8,128)(2,1)}), bf16[1024,512]{1,0:T(8,128)(2,1)}) %all-gather.9.cloned.1.call-update) | async-done | bytes 1048592 | tf_op jit(solution)/shard_map/all_gather | solution.py:25
  412.8 1.6 broadcast.99
  414.5 61.7 %while.31 = (s32[]{:T(128)}, f32[1024,512]{1,0:T(8,128)S(1)}, f32[512,1024]{1,0:T(8,128)}, s32[8]{0:T(128)S(1)}, s32[8,512,512]{2,1,0:T(8,128)}, /*index=5*/bf16...) while((s32[]{:T(128)}, f32[1024,512]{1,0:T(8,128)S(1)}, ...), condition=%wide.region_9.10_spmd, body=%wide.region_8.9_spmd.sunk | while | flops 809763328 | bytes 29897592 | solution.py:60
  417.1 2.6 fusion.77
  420.3 1.4 copy-done.2
  424.8 2.6 fusion.77
  428.0 1.4 copy-done.2
  432.5 2.6 fusion.77
  435.7 1.4 copy-done.2
  440.2 2.6 fusion.77
  443.4 1.4 copy-done.2
  448.0 2.6 fusion.77
  451.1 1.4 copy-done.2
  455.7 2.6 fusion.77
  458.8 1.4 copy-done.2
  463.4 2.6 fusion.77
  466.6 1.4 copy-done.2
  471.1 2.6 fusion.77
  474.3 1.4 copy-done.2
  477.6 51.5 %reduce-scatter.11.cloned.1.call-done = f32[64,1024]{1,0:T(8,128)} async-done(((f32[512,1024]{1,0:T(8,128)}), f32[64,1024]{1,0:T(8,128)}) %reduce-scatter.11.cloned.1.call-update) | async-done | bytes 262160 | tf_op jit(solution)/shard_map/reduce_scatter | solution.py:62
  529.1 77.0 %reduce-scatter.9.cloned.1.call-done = f32[128,512]{1,0:T(8,128)} async-done(((f32[1024,512]{1,0:T(8,128)}), f32[128,512]{1,0:T(8,128)}) %reduce-scatter.9.cloned.1.call-update) | async-done | bytes 262160 | tf_op jit(solution)/shard_map/reduce_scatter | solution.py:61
  606.1 27.5 %all-reduce.5.cloned.1.call-done = (f32[128,512]{1,0:T(8,128)}, f32[64,1024]{1,0:T(8,128)}) async-done(((f32[128,512]{1,0:T(8,128)}, f32[64,1024]{1,0:T(8,128)}), (f32[128,512]{1,0:T(8,128)}, f32[64,1024]{1,0:T(8,128)})) %all-reduce.5.cloned.1.call-update) | async-done | bytes 524304 | tf_op jit(solution)/shard_map/psum | solution.py:63
  633.7 1.7 multiply_subtract_fusion
  635.4 1.7 multiply_subtract_fusion.1
  (225 shorter events, 53.0 us)
Async XLA Ops:
  7.2 51.8 %all-gather.5.cloned.1.call-start = ((), (), s32[]{:S(2)}) async-start(), calls=%async_computation.4 | async-start | bytes 1179648 | tf_op jit(solution)/shard_map/all_gather | solution.py:25
  8.9 88.6 %all-gather.7.cloned.1.call-start = ((), (), s32[]{:S(2)}) async-start(), calls=%async_computation.5 | async-start | bytes 1179648 | tf_op jit(solution)/shard_map/all_gather | solution.py:26
  10.6 229.3 %reduce-scatter.5.cloned.1.call-start = ((), (), s32[]{:S(2)}) async-start(), calls=%async_computation.6 | async-start | bytes 2359296 | tf_op jit(solution)/shard_map/reduce_scatter | solution.py:61
  101.9 2.6 copy-start.4
  104.6 1.9 copy-start.8
  109.6 2.6 copy-start.4
  112.2 1.9 copy-start.8
  117.3 2.6 copy-start.4
  119.9 1.9 copy-start.8
  125.0 2.6 copy-start.4
  127.6 1.9 copy-start.8
  132.7 2.6 copy-start.4
  135.3 1.9 copy-start.8
  140.4 2.6 copy-start.4
  143.0 1.9 copy-start.8
  148.1 2.6 copy-start.4
  150.7 1.9 copy-start.8
  155.7 2.6 copy-start.4
  158.4 1.9 copy-start.8
  160.8 160.6 %copy-start.10 = (f32[64,1024]{1,0:T(8,128)S(1)}, f32[64,1024]{1,0:T(8,128)}, u32[]{:S(2)}) copy-start(f32[64,1024]{1,0:T(8,128)} %param.12) | copy-start | bytes 786436
  162.2 160.9 %copy-start.11 = (f32[128,512]{1,0:T(8,128)S(1)}, f32[128,512]{1,0:T(8,128)}, u32[]{:S(2)}) copy-start(f32[128,512]{1,0:T(8,128)} %param.11) | copy-start | bytes 786436
  162.2 132.7 %reduce-scatter.7.cloned.1.call-start = ((), (), s32[]{:S(2)}) async-start(), calls=%async_computation.8 | async-start | bytes 2359296 | tf_op jit(solution)/shard_map/reduce_scatter | solution.py:62
  162.8 158.6 %all-reduce.7.cloned.1.call-start = ((), (), s32[]{:S(2)}) async-start(), calls=%async_computation.13 | async-start | bytes 1048576 | tf_op jit(solution)/shard_map/psum | solution.py:63
  294.9 65.5 %all-gather.11.cloned.1.call-start = ((), (), s32[]{:S(2)}) async-start(), calls=%async_computation.9 | async-start | bytes 1179648 | tf_op jit(solution)/shard_map/all_gather | solution.py:26
  323.1 89.5 %all-gather.9.cloned.1.call-start = ((), (), s32[]{:S(2)}) async-start(), calls=%async_computation.7 | async-start | bytes 1179648 | tf_op jit(solution)/shard_map/all_gather | solution.py:25
  324.8 204.3 %reduce-scatter.11.cloned.1.call-start = ((), (), s32[]{:S(2)}) async-start(), calls=%async_computation.11 | async-start | bytes 2359296 | tf_op jit(solution)/shard_map/reduce_scatter | solution.py:62
  412.6 1.9 copy-start.7
  417.1 2.6 copy-start.1
  417.1 2.6 copy-start.9
  424.8 2.6 copy-start.1
  424.8 2.6 copy-start.9
  432.5 2.6 copy-start.1
  432.5 2.6 copy-start.9
  440.2 2.6 copy-start.1
  440.2 2.6 copy-start.9
  448.0 2.6 copy-start.1
  448.0 2.6 copy-start.9
  455.7 2.6 copy-start.1
  455.7 2.6 copy-start.9
  463.4 2.6 copy-start.1
  463.4 2.6 copy-start.9
  471.1 2.6 copy-start.1
  471.1 2.6 copy-start.9
  476.2 157.5 %copy-start.14 = (f32[64,1024]{1,0:T(8,128)S(1)}, f32[64,1024]{1,0:T(8,128)}, u32[]{:S(2)}) copy-start(f32[64,1024]{1,0:T(8,128)} %get-tuple-element.423) | copy-start | bytes 786436
  476.2 159.2 %copy-start.12 = (f32[128,512]{1,0:T(8,128)S(1)}, f32[128,512]{1,0:T(8,128)}, u32[]{:S(2)}) copy-start(f32[128,512]{1,0:T(8,128)} %param.11) | copy-start | bytes 786436
  476.2 159.2 %copy-start.13 = (f32[128,512]{1,0:T(8,128)S(1)}, f32[128,512]{1,0:T(8,128)}, u32[]{:S(2)}) copy-start(f32[128,512]{1,0:T(8,128)} %get-tuple-element.422) | copy-start | bytes 786436
  476.2 129.9 %reduce-scatter.9.cloned.1.call-start = ((), (), s32[]{:S(2)}) async-start(), calls=%async_computation.10 | async-start | bytes 2359296 | tf_op jit(solution)/shard_map/reduce_scatter | solution.py:61
  477.5 156.1 %all-reduce.5.cloned.1.call-start = ((), (), s32[]{:S(2)}) async-start(), calls=%async_computation.12 | async-start | bytes 1048576 | tf_op jit(solution)/shard_map/psum | solution.py:63
  (19 other events, 26.5 us)
Sparse Core Ops, SparseCore 0:
  10.9 48.0 all-gather.4
  61.2 36.1 all-gather.6
  162.3 77.5 reduce-scatter.4
  242.1 52.7 reduce-scatter.6
  297.3 24.1 all-reduce.6
  323.6 36.8 all-gather.10
  363.7 48.8 all-gather.8
  476.3 52.7 reduce-scatter.10
  533.3 72.7 reduce-scatter.8
  608.6 25.0 all-reduce.4
where the time goes:
time: 645 us; the launch traced here: 644 us
  waiting for transfers between devices  457 us (71%)
  local copies, waits for them, and re-layouts  60 us (9%)
  matrix products  58.4 us (9%)
  loops' own time  21.6 us (3%)
  blocking collectives  18.8 us (3%)
  between operations  14.9 us (2%)
  other arithmetic  13.2 us (2%)
    reduce_scatter x2, waiting for transfers between devices, per_device(): share_w = lax.psum_scatter(part_w, 'col', scatter_dimension=0, tiled=True)  154 us
    reduce_scatter x2, waiting for transfers between devices, per_device(): share_c = lax.psum_scatter(part_c, 'row', scatter_dimension=0, tiled=True)  107 us
    all_gather x2, waiting for transfers between devices, per_device(): lax.all_gather(col_embed.astype(jnp.bfloat16), 'row', axis=0, tiled=True)  74.1 us
    all_gather x2, waiting for transfers between devices, per_device(): lax.all_gather(row_embed.astype(jnp.bfloat16), 'col', axis=0, tiled=True)  67.3 us
    psum x2, waiting for transfers between devices, per_device(): share_w, share_c = lax.psum((share_w, share_c), 'rep')  53.9 us
    dot_general x16, matrix products, add_block(): dots = jnp.dot(wblock, cblock, preferred_element_type=jnp.float32)  41.8 us
    while x96, local copies, waits for them, and re-layouts  22 us
    another operation x2, loops' own time, per_device(): part_w, part_c = lax.fori_loop(0, slots, add_block, (empty_w, empty_c))  21.6 us
  transfers between devices with their start and end apart: 10, of which 10 were waited for; matrix products, arithmetic and copies ran while one was open for 3% of the time, Pallas kernels for 0%

commit v1 on v0

v1 whole, which is shorter than its diff:
```python
import functools

import jax
import jax.numpy as jnp
from jax import lax
from jax.experimental import pallas as pl
from jax.experimental.pallas import tpu as pltpu
from jax.sharding import PartitionSpec as P

RATE = 0.002
AXES = ("row", "col", "rep")
F32 = jnp.float32
BF16 = jnp.bfloat16
ABN_ROWS = 64
SUB = 16
NT = (((1,), (1,)), ((), ()))
TN = (((0,), (0,)), ((), ()))


def abn_kernel(rows, cols, x, a, b, n):
    for ref in (a, b, n):
        ref[...] = jnp.zeros(ref.shape, ref.dtype)

    def strip(i, carry):
        part = pl.ds(pl.multiple_of(i * SUB, SUB), SUB)
        for slot in range(x.shape[1]):
            xf = x[0, slot, part, :].astype(F32)
            seen = xf > 0
            top = jnp.maximum(xf, 1.0)
            weight = jnp.where(seen, 0.1 + 0.25 * (top * lax.rsqrt(top)), 0.0)
            at = (rows[slot], cols[slot], part, slice(None))
            a[at] += weight
            b[at] += weight * jnp.log(top)
            n[at] = (n[at].astype(F32) + jnp.where(seen, 0.0, 1.0)).astype(BF16)
        return carry

    lax.fori_loop(0, x.shape[2] // SUB, strip, 0)


def abn(counts, rows, cols, step):
    slots, block = counts.shape[1], counts.shape[2]
    out = pl.BlockSpec((2, 2, ABN_ROWS, block), lambda i, *_: (0, 0, i, 0))
    shape = (2, 2, block, block)
    return pl.pallas_call(
        abn_kernel,
        grid_spec=pltpu.PrefetchScalarGridSpec(
            num_scalar_prefetch=2,
            grid=(block // ABN_ROWS,),
            in_specs=[pl.BlockSpec((1, slots, ABN_ROWS, block), lambda i, *_: (step, 0, i, 0))],
            out_specs=[out, out, out],
        ),
        out_shape=[jax.ShapeDtypeStruct(shape, d) for d in (F32, F32, BF16)],
        compiler_params=pltpu.CompilerParams(vmem_limit_bytes=16 * 2**20),
        cost_estimate=pl.CostEstimate(flops=3 * 10**9, bytes_accessed=18 * 2**20, transcendentals=4 * 2**20),
        name="count_factors",
    )(rows, cols, counts)


def step_kernel(first, rep, own, other, a, b, n, lr, lc, *refs):
    if first:
        keep, send, log_total, grads = refs
    else:
        log_total, keep, send, grads = refs
    q = pl.program_id(0)

    def body(w, c, grad_w, grad_c):
        if first:

            @pl.when(q == 0)
            def _():
                pieces = c[:, 128:, :].astype(F32)
                log_total[...] = jnp.broadcast_to(
                    jnp.log(jnp.sum(pieces, axis=(0, 1), keepdims=False)[None, :]), log_total.shape
                )

        wq = w[pl.ds(2 * q, 2), :128, :].reshape(256, 512)
        row_part = lr[...]
        total = jnp.zeros((256, 512), F32)
        for h in range(2):
            ch = c[:, h * 64 : h * 64 + 64, :].reshape(512, 512)
            dots = jnp.dot(wq, ch, preferred_element_type=F32)
            t = dots + row_part + (lc[h] - log_total[0:1, :])
            hinge = 0.5 + 0.5 * jnp.tanh(0.5 * t)
            g = (t * a[0, h] - b[0, h] + n[0, h].astype(F32) * hinge).astype(BF16)
            grads[h, pl.ds(pl.multiple_of(q * 256, 256), 256), :] = g
            total += lax.dot_general(g, ch, NT, preferred_element_type=F32)
        grad_w[pl.ds(2 * q, 2)] = total.reshape(2, 128, 512).astype(grad_w.dtype)

        @pl.when(q == 3)
        def _():
            w_all = w[:, :128, :].reshape(1024, 512)
            for h in range(2):
                gc = lax.dot_general(w_all, grads[h], TN, preferred_element_type=F32)
                grad_c[:, h * 64 : h * 64 + 64, :] = gc.reshape(8, 64, 512).astype(grad_c.dtype)

    @pl.when(rep[0] == 0)
    def _():
        body(own, other, keep, send)

    @pl.when(rep[0] == 1)
    def _():
        body(other, own, send, keep)


def step_grads(rep, own, other, factors, lr, lc, log_total):
    first = log_total is None
    whole = lambda s: pl.BlockSpec(s, lambda q, *_: (0,) * len(s))
    quarter = pl.BlockSpec((1, 2, 256, 512), lambda q, *_: (q // 2, 0, q % 2, 0))
    in_specs = [whole(own.shape)] * 2 + [quarter] * 3 + [pl.BlockSpec((256, 1), lambda q, *_: (q, 0)), whole((2, 1, 512))]
    args = [rep, own, other, *factors, lr, lc]
    shape = (8, 128, 512)
    out_specs = [whole(shape)] * 2
    out_shape = [jax.ShapeDtypeStruct(shape, F32), jax.ShapeDtypeStruct(shape, BF16)]
    if first:
        out_specs.append(whole((8, 512)))
        out_shape.append(jax.ShapeDtypeStruct((8, 512), F32))
    else:
        in_specs.append(whole((8, 512)))
        args.append(log_total)
    return pl.pallas_call(
        functools.partial(step_kernel, first),
        grid_spec=pltpu.PrefetchScalarGridSpec(
            num_scalar_prefetch=1,
            grid=(4,),
            in_specs=in_specs,
            out_specs=out_specs,
            scratch_shapes=[pltpu.VMEM((2, 1024, 512), BF16)],
        ),
        out_shape=out_shape,
        compiler_params=pltpu.CompilerParams(vmem_limit_bytes=40 * 2**20),
        cost_estimate=pl.CostEstimate(flops=3 * 10**9, bytes_accessed=16 * 2**20, transcendentals=2**20),
        name="step_grads",
    )(*args)


def pieces_of(value):
    out = []
    for _ in range(3):
        top = lax.reduce_precision(value, 8, 7)
        out.append(top)
        value = value - top
    return jnp.stack(out + [jnp.zeros_like(value)] * 5).astype(BF16)


def per_device(groups, swap, row_embed, col_embed, counts, block_rows, block_cols, row_marginals, col_marginals):
    core = lax.axis_index("rep")
    is_w = core == 0
    rep = core.astype(jnp.int32).reshape(1)
    steps, slots = counts.shape[:2]

    def spread(x):
        return lax.all_to_all(x, AXES, 0, 0, axis_index_groups=groups, tiled=True)

    def other_core(x):
        return lax.ppermute(x, "rep", swap)

    packed_col = jnp.concatenate([col_embed[:, :512], col_embed[:, 512:]], axis=0)
    embed = jnp.where(is_w, row_embed, packed_col)
    row_f = row_marginals.astype(F32)
    extra = jnp.broadcast_to(pieces_of(jnp.sum(row_f))[:, None], (8, 512))
    lr = jnp.log(row_f)[:, None]
    lc = jnp.log(col_marginals.astype(F32)).reshape(2, 1, 512)
    rows = block_rows[:, :, 0, 0]
    cols = block_cols[:, :, 0, 0]

    log_total = None
    for step in range(steps):
        mine = embed.astype(BF16)
        if step == 0:
            mine = jnp.concatenate([mine, extra], axis=0)
        own = spread(jnp.broadcast_to(mine, (8,) + mine.shape))
        factors = abn(counts, rows[step], cols[step], step)
        other = other_core(own)
        res = step_grads(rep, own, other, factors, lr, lc, log_total)
        if step == 0:
            keep, send, log_total = res
        else:
            keep, send = res
        terms = (keep + other_core(send).astype(F32)).astype(BF16)
        share = spread(terms)
        embed = embed - RATE * jnp.sum(share.astype(F32), axis=0)
    theirs = other_core(embed)
    new_row = jnp.where(is_w, embed, theirs)
    new_col = jnp.where(is_w, theirs, embed)
    return new_row, jnp.concatenate([new_col[:64], new_col[64:]], axis=1)


def solution(mesh):
    n_row, n_col = mesh.shape["row"], mesh.shape["col"]
    index = lambda r, c, p: (r * n_col + c) * 2 + p
    groups = [[index(r, c, 0) for c in range(n_col)] for r in range(n_row)]
    groups += [[index(r, c, 1) for r in range(n_row)] for c in range(n_col)]
    swap = [(0, 1), (1, 0)]
    return jax.shard_map(
        functools.partial(per_device, groups, swap),
        mesh=mesh,
        in_specs=(
            P(("row", "col"), None),
            P("row", "col"),
            P(None, "rep", "row", "col"),
            P(None, "rep", "row", "col"),
            P(None, "rep", "row", "col"),
            P("row"),
            P("col"),
        ),
        out_specs=(P(("row", "col"), None), P("row", "col")),
        check_vma=False,
    )
```

time: 645 us -> 161 us (0.25)
  waiting for transfers between devices: 457 us -> 6.29 us
  matrix products: 58.4 us -> 0 us
  blocking collectives: 18.8 us -> 76.8 us
  local copies, waits for them, and re-layouts: 60 us -> 26.9 us
  Pallas kernels: 0 us -> 29.6 us
  loops' own time: 21.6 us -> 0 us
  between operations: 14.9 us -> 6.33 us
  starting transfers between devices: 0.4 us -> 8.24 us
  other arithmetic: 13.2 us -> 5.77 us
    reduce_scatter x4 -> x0, waiting for transfers between devices: 261 us -> none  [the longest x2 154 us: per_device(): share_w = lax.psum_scatter(part_w, 'col', scatter_dimension=0, tiled=True)]
    all_gather x4 -> x0, waiting for transfers between devices: 141 us -> none  [the longest x2 74.1 us: per_device(): lax.all_gather(col_embed.astype(jnp.bfloat16), 'row', axis=0, tiled=True)]
    all_to_all x0 -> x4, blocking collectives: none -> 76.8 us  [spread(): return lax.all_to_all(x, AXES, 0, 0, axis_index_groups=groups, tiled=True)]
    dot_general x48 -> x0, matrix products: 58.4 us -> none  [the longest x16 41.8 us: add_block(): dots = jnp.dot(wblock, cblock, preferred_element_type=jnp.float32)]
    psum x2 -> x0, waiting for transfers between devices: 53.9 us -> none  [per_device(): share_w, share_c = lax.psum((share_w, share_c), 'rep')]
    pallas_call x0 -> x4, Pallas kernels: none -> 29.6 us  [the longest x2 14.9 us: step_grads(): pl.pallas_call(functools.partial(step_kernel, first), grid_spec=pltpu.Pre...]
    while x96 -> x0, local copies, waits for them, and re-layouts: 22 us -> none
    another operation x2 -> x0, loops' own time: 21.6 us -> none  [per_device(): part_w, part_c = lax.fori_loop(0, slots, add_block, (empty_w, empty_c))]
  transfers between devices with their start and end apart: 10 -> 5, of which waited for: 10 -> 3; matrix products, arithmetic and copies ran while one was open for 3% -> 1% of each run, Pallas kernels for 0% -> 9%
where the time goes in v1:
time: 161 us; the launch traced here: 160 us
  blocking collectives  76.8 us (48%)
  Pallas kernels  29.6 us (18%)
  local copies, waits for them, and re-layouts  26.9 us (17%)
  starting transfers between devices  8.24 us (5%)
  between operations  6.33 us (4%)
  waiting for transfers between devices  6.29 us (4%)
  other arithmetic  5.77 us (4%)
    all_to_all x4, blocking collectives, spread(): return lax.all_to_all(x, AXES, 0, 0, axis_index_groups=groups, tiled=True)  76.8 us
    unnamed x46, local copies, waits for them, and re-layouts  24 us
    pallas_call x2, Pallas kernels, step_grads(): pl.pallas_call(functools.partial(step_kernel, first), grid_spec=pltpu.Pre...  14.9 us
    pallas_call x2, Pallas kernels, abn(): pl.pallas_call(abn_kernel, grid_spec=pltpu.PrefetchScalarGridSpec(num_sca...  14.6 us
    ppermute x5, starting transfers between devices, other_core(): return lax.ppermute(x, 'rep', swap)  8.24 us
    ppermute x5, waiting for transfers between devices, other_core(): return lax.ppermute(x, 'rep', swap)  6.29 us
  transfers between devices with their start and end apart: 5, of which 3 were waited for; matrix products, arithmetic and copies ran while one was open for 1% of the time, Pallas kernels for 9%

profile of v1, /device:TPU:1, one launch (start us, length us, event | category | flops | bytes accessed | tf_op | source)
XLA Modules:
  0.0 159.9 jit_solution(4310556965362311137)
XLA Ops:
  0.6 1.3 convert_log_fusion.1
  7.4 1.0 fusion.3
  8.4 0.7 stack.18
  9.1 0.0 copy-start.17
  9.2 0.0 copy-start.18
  9.2 0.0 copy-start.16
  9.2 0.1 pad_maximum_fusion.1
  9.3 0.1 broadcast_in_dim.16
  9.4 20.8 %all_to_all.20.own = bf16[8,136,512]{2,1,0:T(8,128)(2,1)} all-to-all(bf16[8,136,512]{2,1,0:T(8,128)(2,1)S(1)} %broadcast_in_dim.16), channel_id=1, replica_groups={{0,2,4,6,8,10,12,14},{16,18,20,22,24,26,28,30},{32,34,36,38,40,42,44,46..., dimensions={0} | all-to-all | bytes 2228224 | tf_op jit(solution)/shard_map/all_to_all | solution.py:152
  30.2 4.6 %collective-permute-start = (bf16[8,136,512]{2,1,0:T(8,128)(2,1)}, bf16[8,136,512]{2,1,0:T(8,128)(2,1)}, u32[]{:S(2)}, u32[]{:S(2)}) collective-permute-start(bf16[8,136,512]{2,1,0:T(8,128)(2,1)} %all_to_all.20.own), channel_id=1, source_target_pairs={{0,1},{1,0},{2,3},{3,2},{4,5},{5,4},{6,7},{7,6},{8,9},{9,8},{10,11... | collective-permute-start | bytes 3342344 | tf_op jit(solution)/shard_map/ppermute | solution.py:155
  34.8 1.0 copy.9.lr
  35.9 0.0 copy-start
  35.9 5.8 %copy-done = s32[2,8,512,512]{3,2,1,0:T(8,128)S(1)} copy-done((s32[2,8,512,512]{3,2,1,0:T(8,128)S(1)}, s32[2,8,512,512]{3,2,1,0:T(8,128)}, u32[]{:S(2)}) %copy-start) | copy-done | bytes 16777240
  41.6 7.3 %count_factors.2 = (f32[2,2,512,512]{3,2,1,0:T(8,128)S(1)}, f32[2,2,512,512]{3,2,1,0:T(8,128)S(1)}, bf16[2,2,512,512]{3,2,1,0:T(8,128)(2,1)S(1)}) custom-call(s32[8]{0:T(128)S(1)} %get-tuple-element.38.rows, s32[8]{0:T(128)S(1)} %get-tuple-element.35.cols, s32[2,8,512,512]{3,2,1,0:T(8,128)S(1)} %copy-done), custom_call_target="tpu_custom_call" | custom-call | flops 3000000000 | bytes 18874368 | tf_op jit(solution)/shard_map/count_factors/pallas_call | solution.py:44
  49.0 2.0 %copy-done.3 = f32[2,2,512,512]{3,2,1,0:T(8,128)} copy-done((f32[2,2,512,512]{3,2,1,0:T(8,128)}, f32[2,2,512,512]{3,2,1,0:T(8,128)S(1)}, u32[]{:S(2)}) %copy-start.3) | copy-done | bytes 4194328
  51.0 2.0 %copy-done.5 = f32[2,2,512,512]{3,2,1,0:T(8,128)} copy-done((f32[2,2,512,512]{3,2,1,0:T(8,128)}, f32[2,2,512,512]{3,2,1,0:T(8,128)S(1)}, u32[]{:S(2)}) %copy-start.5) | copy-done | bytes 4194328
  53.0 2.2 %copy-done.4 = f32[2,2,512,512]{3,2,1,0:T(8,128)S(1)} copy-done((f32[2,2,512,512]{3,2,1,0:T(8,128)S(1)}, f32[2,2,512,512]{3,2,1,0:T(8,128)}, u32[]{:S(2)}) %copy-start.4) | copy-done | bytes 4194328
  55.2 7.9 %step_grads.2 = (f32[8,128,512]{2,1,0:T(8,128)S(1)}, bf16[8,128,512]{2,1,0:T(8,128)(2,1)S(1)}, f32[8,512]{1,0:T(8,128)S(1)}) custom-call(s32[1]{0:T(128)} %bitcast.rep, bf16[8,136,512]{2,1,0:T(8,128)(2,1)} %all_to_all.20.own, bf16[8,136,512]{2,1,0:T(8,128)(2,1)} %collective-permute-done.other, f32[2,2,512,512]{3,2,1,0:T(8,128)S(1)} %copy-done.4, ...), custom_call_target="tpu_custom_call" | custom-call | flops 3000000000 | bytes 16777216 | tf_op jit(solution)/shard_map/step_grads/pallas_call | solution.py:120
  63.1 1.3 copy-done.11
  64.4 0.0 collective-permute-start.1
  64.5 2.6 %collective-permute-done.1 = bf16[8,128,512]{2,1,0:T(8,128)(2,1)S(1)} collective-permute-done((bf16[8,128,512]{2,1,0:T(8,128)(2,1)S(1)}, bf16[8,128,512]{2,1,0:T(8,128)(2,1)S(1)}, u32[]{:S(2)}, u32[]{:S(2)}) %collective-permute-start.1) | collective-permute-done | bytes 1048608 | tf_op jit(solution)/shard_map/ppermute | solution.py:155
  67.1 2.1 %add_convert_fusion.1 = bf16[8,128,512]{2,1,0:T(8,128)(2,1)S(1)} fusion(f32[8,128,512]{2,1,0:T(8,128)} %copy-done.11, bf16[8,128,512]{2,1,0:T(8,128)(2,1)S(1)} %collective-permute-done.1), kind=kLoop, calls=%fused_computation.3 | loop fusion | flops 1572864 | bytes 4194304 | tf_op jit(solution)/shard_map/convert_element_type | solution.py:179
  69.2 19.0 %all_to_all.21 = bf16[8,128,512]{2,1,0:T(8,128)(2,1)S(1)} all-to-all(bf16[8,128,512]{2,1,0:T(8,128)(2,1)S(1)} %add_convert_fusion.1), channel_id=1, replica_groups={{0,2,4,6,8,10,12,14},{16,18,20,22,24,26,28,30},{32,34,36,38,40,42,44,46..., dimensions={0} | all-to-all | bytes 2097152 | tf_op jit(solution)/shard_map/all_to_all | solution.py:152
  88.2 0.1 convert_reduce_fusion.1
  88.3 0.0 copy-start.14
  88.4 0.1 broadcast_in_dim.18
  88.5 17.0 %all_to_all.22.own = bf16[8,128,512]{2,1,0:T(8,128)(2,1)S(1)} all-to-all(bf16[8,128,512]{2,1,0:T(8,128)(2,1)S(1)} %broadcast_in_dim.18), channel_id=1, replica_groups={{0,2,4,6,8,10,12,14},{16,18,20,22,24,26,28,30},{32,34,36,38,40,42,44,46..., dimensions={0} | all-to-all | bytes 2097152 | tf_op jit(solution)/shard_map/all_to_all | solution.py:152
  105.5 0.5 collective-permute-start.2
  106.0 7.3 %count_factors.3 = (f32[2,2,512,512]{3,2,1,0:T(8,128)S(1)}, f32[2,2,512,512]{3,2,1,0:T(8,128)S(1)}, bf16[2,2,512,512]{3,2,1,0:T(8,128)(2,1)S(1)}) custom-call(s32[8]{0:T(128)S(1)} %get-tuple-element.39.rows, s32[8]{0:T(128)S(1)} %get-tuple-element.34.cols, s32[2,8,512,512]{3,2,1,0:T(8,128)S(1)} %bitcast.15), custom_call_target="tpu_custom_call" | custom-call | flops 3000000000 | bytes 18874368 | tf_op jit(solution)/shard_map/count_factors/pallas_call | solution.py:44
  113.3 2.0 %copy-done.8 = f32[2,2,512,512]{3,2,1,0:T(8,128)} copy-done((f32[2,2,512,512]{3,2,1,0:T(8,128)}, f32[2,2,512,512]{3,2,1,0:T(8,128)S(1)}, u32[]{:S(2)}) %copy-start.8) | copy-done | bytes 4194328
  115.3 2.0 %copy-done.10 = f32[2,2,512,512]{3,2,1,0:T(8,128)} copy-done((f32[2,2,512,512]{3,2,1,0:T(8,128)}, f32[2,2,512,512]{3,2,1,0:T(8,128)S(1)}, u32[]{:S(2)}) %copy-start.10) | copy-done | bytes 4194328
  117.3 1.0 copy-done.12
  118.3 1.0 copy-done.2
  119.3 1.2 copy-done.7
  120.6 2.2 %copy-done.9 = f32[2,2,512,512]{3,2,1,0:T(8,128)S(1)} copy-done((f32[2,2,512,512]{3,2,1,0:T(8,128)S(1)}, f32[2,2,512,512]{3,2,1,0:T(8,128)}, u32[]{:S(2)}) %copy-start.9) | copy-done | bytes 4194328
  122.8 1.2 copy-done.13
  124.0 7.0 %step_grads.3 = (f32[8,128,512]{2,1,0:T(8,128)S(1)}, bf16[8,128,512]{2,1,0:T(8,128)(2,1)S(1)}) custom-call(s32[1]{0:T(128)} %bitcast.rep, bf16[8,128,512]{2,1,0:T(8,128)(2,1)S(1)} %copy-done.7, bf16[8,128,512]{2,1,0:T(8,128)(2,1)S(1)} %copy-done.13, f32[2,2,512,512]{3,2,1,0:T(8,128)S(1)} %copy-done.9, f32[2,2,512,512]{3,2,1,0:T(8,128)} %copy-done.10, ...), custom_call_target="tpu_custom_call" | custom-call | flops 3000000000 | bytes 16777216 | tf_op jit(solution)/shard_map/step_grads/pallas_call | solution.py:120
  131.0 0.2 collective-permute-start.3
  131.3 2.5 %collective-permute-done.3 = bf16[8,128,512]{2,1,0:T(8,128)(2,1)S(1)} collective-permute-done((bf16[8,128,512]{2,1,0:T(8,128)(2,1)S(1)}, bf16[8,128,512]{2,1,0:T(8,128)(2,1)S(1)}, u32[]{:S(2)}, u32[]{:S(2)}) %collective-permute-start.3) | collective-permute-done | bytes 1048608 | tf_op jit(solution)/shard_map/ppermute | solution.py:155
  133.8 0.4 add_convert_fusion
  134.1 0.0 copy-start.15
  134.2 20.0 %all_to_all.23 = bf16[8,128,512]{2,1,0:T(8,128)(2,1)S(1)} all-to-all(bf16[8,128,512]{2,1,0:T(8,128)(2,1)S(1)} %add_convert_fusion), channel_id=1, replica_groups={{0,2,4,6,8,10,12,14},{16,18,20,22,24,26,28,30},{32,34,36,38,40,42,44,46..., dimensions={0} | all-to-all | bytes 2097152 | tf_op jit(solution)/shard_map/all_to_all | solution.py:152
  154.1 0.1 convert_reduce_fusion
  154.3 0.1 multiply_subtract_fusion
  154.4 2.9 %collective-permute-start.4 = (f32[128,512]{1,0:T(8,128)S(1)}, f32[128,512]{1,0:T(8,128)S(1)}, u32[]{:S(2)}, u32[]{:S(2)}) collective-permute-start(f32[128,512]{1,0:T(8,128)S(1)} %multiply_subtract_fusion), channel_id=1, source_target_pairs={{0,1},{1,0},{2,3},{3,2},{4,5},{5,4},{6,7},{7,6},{8,9},{9,8},{10,11... | collective-permute-start | bytes 786440 | tf_op jit(solution)/shard_map/ppermute | solution.py:155
  157.3 1.2 collective-permute-done.4
  158.4 0.7 broadcast_select_fusion
  159.2 0.7 pad_maximum_fusion
  (38 shorter events, 0.2 us)
Async XLA Ops:
  9.1 26.7 %copy-start.17 = (s32[2,8,1,1]{1,3,2,0:T(1,128)S(1)}, s32[2,8,1,1]{1,3,2,0:T(1,128)}, u32[]{:S(2)}) copy-start(s32[2,8,1,1]{1,3,2,0:T(1,128)} %param.11) | copy-start | bytes 196
  9.2 26.7 %copy-start.18 = (s32[2,8,1,1]{1,3,2,0:T(1,128)S(1)}, s32[2,8,1,1]{1,3,2,0:T(1,128)}, u32[]{:S(2)}) copy-start(s32[2,8,1,1]{1,3,2,0:T(1,128)} %param.10) | copy-start | bytes 196
  9.2 26.7 %copy-start.16 = (s32[1024]{0:T(1024)S(1)}, s32[1024]{0:T(1024)}, u32[]{:S(2)}) copy-start(s32[1024]{0:T(1024)} %param.13) | copy-start | bytes 12292
  30.2 22.8 %collective-permute-start = (bf16[8,136,512]{2,1,0:T(8,128)(2,1)}, bf16[8,136,512]{2,1,0:T(8,128)(2,1)}, u32[]{:S(2)}, u32[]{:S(2)}) collective-permute-start(bf16[8,136,512]{2,1,0:T(8,128)(2,1)} %all_to_all.20.own), channel_id=1, source_target_pairs={{0,1},{1,0},{2,3},{3,2},{4,5},{5,4},{6,7},{7,6},{8,9},{9,8},{10,11... | collective-permute-start | bytes 3342344 | tf_op jit(solution)/shard_map/ppermute | solution.py:155
  35.9 5.8 %copy-start = (s32[2,8,512,512]{3,2,1,0:T(8,128)S(1)}, s32[2,8,512,512]{3,2,1,0:T(8,128)}, u32[]{:S(2)}) copy-start(s32[2,8,512,512]{3,2,1,0:T(8,128)} %x.3) | copy-start | bytes 50331652
  41.6 11.3 %copy-start.1 = (f32[1024,1]{1,0:T(8,128)S(1)}, f32[1024,1]{1,0:T(8,128)}, u32[]{:S(2)}) copy-start(f32[1024,1]{1,0:T(8,128)} %copy.9.lr) | copy-start | bytes 12292
  41.6 64.3 %slice-start = ((s8[16777216]{0:T(1024)(128)(4,1)}), s8[4194304]{0:T(1024)(128)(4,1)S(1)}, s32[]{:S(2)}) async-start(s8[16777216]{0:T(1024)(128)(4,1)} %bitcast.14), calls=%async_computation.4 | async-start | bytes 8388608
  41.6 64.3 %slice-start.1 = ((s8[16777216]{0:T(1024)(128)(4,1)}), s8[4194304]{0:T(1024)(128)(4,1)S(1)}, s32[]{:S(2)}) async-start(s8[16777216]{0:T(1024)(128)(4,1)} %bitcast.14), calls=%async_computation.5 | async-start | bytes 8388608
  49.0 2.0 %copy-start.3 = (f32[2,2,512,512]{3,2,1,0:T(8,128)}, f32[2,2,512,512]{3,2,1,0:T(8,128)S(1)}, u32[]{:S(2)}) copy-start(f32[2,2,512,512]{3,2,1,0:T(8,128)S(1)} %get-tuple-element.13.a) | copy-start | bytes 12582916
  51.0 2.0 %copy-start.5 = (f32[2,2,512,512]{3,2,1,0:T(8,128)}, f32[2,2,512,512]{3,2,1,0:T(8,128)S(1)}, u32[]{:S(2)}) copy-start(f32[2,2,512,512]{3,2,1,0:T(8,128)S(1)} %get-tuple-element.14.b) | copy-start | bytes 12582916
  53.0 2.2 %copy-start.4 = (f32[2,2,512,512]{3,2,1,0:T(8,128)S(1)}, f32[2,2,512,512]{3,2,1,0:T(8,128)}, u32[]{:S(2)}) copy-start(f32[2,2,512,512]{3,2,1,0:T(8,128)} %copy-done.3) | copy-start | bytes 12582916
  55.2 50.8 %slice-start.2 = ((s8[16777216]{0:T(1024)(128)(4,1)}), s8[4194304]{0:T(1024)(128)(4,1)S(1)}, s32[]{:S(2)}) async-start(s8[16777216]{0:T(1024)(128)(4,1)} %bitcast.14), calls=%async_computation.6 | async-start | bytes 8388608
  63.1 1.4 copy-start.11
  64.4 2.7 %collective-permute-start.1 = (bf16[8,128,512]{2,1,0:T(8,128)(2,1)S(1)}, bf16[8,128,512]{2,1,0:T(8,128)(2,1)S(1)}, u32[]{:S(2)}, u32[]{:S(2)}) collective-permute-start(bf16[8,128,512]{2,1,0:T(8,128)(2,1)S(1)} %get-tuple-element.17), channel_id=1, source_target_pairs={{0,1},{1,0},{2,3},{3,2},{4,5},{5,4},{6,7},{7,6},{8,9},{9,8},{10,11... | collective-permute-start | bytes 3145736 | tf_op jit(solution)/shard_map/ppermute | solution.py:155
  67.1 38.9 %slice-start.3 = ((s8[16777216]{0:T(1024)(128)(4,1)}), s8[4194304]{0:T(1024)(128)(4,1)S(1)}, s32[]{:S(2)}) async-start(s8[16777216]{0:T(1024)(128)(4,1)} %bitcast.14), calls=%async_computation.7 | async-start | bytes 8388608
  88.3 17.6 %copy-start.14 = (f32[128,512]{1,0:T(8,128)}, f32[128,512]{1,0:T(8,128)S(1)}, u32[]{:S(2)}) copy-start(f32[128,512]{1,0:T(8,128)S(1)} %convert_reduce_fusion.1) | copy-start | bytes 786436
  105.5 7.8 %copy-start.6 = (bf16[8,128,512]{2,1,0:T(8,128)(2,1)}, bf16[8,128,512]{2,1,0:T(8,128)(2,1)S(1)}, u32[]{:S(2)}) copy-start(bf16[8,128,512]{2,1,0:T(8,128)(2,1)S(1)} %all_to_all.22.own) | copy-start | bytes 3145732
  105.5 11.8 %collective-permute-start.2 = (bf16[8,128,512]{2,1,0:T(8,128)(2,1)S(1)}, bf16[8,128,512]{2,1,0:T(8,128)(2,1)S(1)}, u32[]{:S(2)}, u32[]{:S(2)}) collective-permute-start(bf16[8,128,512]{2,1,0:T(8,128)(2,1)S(1)} %all_to_all.22.own), channel_id=1, source_target_pairs={{0,1},{1,0},{2,3},{3,2},{4,5},{5,4},{6,7},{7,6},{8,9},{9,8},{10,11... | collective-permute-start | bytes 3145736 | tf_op jit(solution)/shard_map/ppermute | solution.py:155
  113.3 2.0 %copy-start.8 = (f32[2,2,512,512]{3,2,1,0:T(8,128)}, f32[2,2,512,512]{3,2,1,0:T(8,128)S(1)}, u32[]{:S(2)}) copy-start(f32[2,2,512,512]{3,2,1,0:T(8,128)S(1)} %get-tuple-element.18.a) | copy-start | bytes 12582916
  115.3 2.0 %copy-start.10 = (f32[2,2,512,512]{3,2,1,0:T(8,128)}, f32[2,2,512,512]{3,2,1,0:T(8,128)S(1)}, u32[]{:S(2)}) copy-start(f32[2,2,512,512]{3,2,1,0:T(8,128)S(1)} %get-tuple-element.19.b) | copy-start | bytes 12582916
  117.3 1.0 copy-start.12
  118.3 1.0 copy-start.2
  119.3 1.2 copy-start.7
  120.6 2.2 %copy-start.9 = (f32[2,2,512,512]{3,2,1,0:T(8,128)S(1)}, f32[2,2,512,512]{3,2,1,0:T(8,128)}, u32[]{:S(2)}) copy-start(f32[2,2,512,512]{3,2,1,0:T(8,128)} %copy-done.8) | copy-start | bytes 12582916
  122.8 1.2 copy-start.13
  131.0 2.7 %collective-permute-start.3 = (bf16[8,128,512]{2,1,0:T(8,128)(2,1)S(1)}, bf16[8,128,512]{2,1,0:T(8,128)(2,1)S(1)}, u32[]{:S(2)}, u32[]{:S(2)}) collective-permute-start(bf16[8,128,512]{2,1,0:T(8,128)(2,1)S(1)} %get-tuple-element.23), channel_id=1, source_target_pairs={{0,1},{1,0},{2,3},{3,2},{4,5},{5,4},{6,7},{7,6},{8,9},{9,8},{10,11... | collective-permute-start | bytes 3145736 | tf_op jit(solution)/shard_map/ppermute | solution.py:155
  134.1 20.2 %copy-start.15 = (f32[128,512]{1,0:T(8,128)S(1)}, f32[128,512]{1,0:T(8,128)}, u32[]{:S(2)}) copy-start(f32[128,512]{1,0:T(8,128)} %copy-done.14) | copy-start | bytes 786436
  154.4 4.0 %collective-permute-start.4 = (f32[128,512]{1,0:T(8,128)S(1)}, f32[128,512]{1,0:T(8,128)S(1)}, u32[]{:S(2)}, u32[]{:S(2)}) collective-permute-start(f32[128,512]{1,0:T(8,128)S(1)} %multiply_subtract_fusion), channel_id=1, source_target_pairs={{0,1},{1,0},{2,3},{3,2},{4,5},{5,4},{6,7},{7,6},{8,9},{9,8},{10,11... | collective-permute-start | bytes 786440 | tf_op jit(solution)/shard_map/ppermute | solution.py:155

commit v2 on v0

v2 whole, which is shorter than its diff:
```python
import functools

import jax
import jax.numpy as jnp
from jax import lax
from jax.experimental import pallas as pl
from jax.experimental.pallas import tpu as pltpu
from jax.sharding import PartitionSpec as P

RATE = 0.002
AXES = ("row", "col", "rep")
F32 = jnp.float32
BF16 = jnp.bfloat16
W_ROLE = 1
PIECE = 64
STRIP = 16
NT = (((1,), (1,)), ((), ()))
TN = (((0,), (0,)), ((), ()))
IN_VMEM = pl.BlockSpec(memory_space=pltpu.VMEM)
IN_HBM = pl.BlockSpec(memory_space=pltpu.HBM)
IN_SMEM = pl.BlockSpec(memory_space=pltpu.SMEM)


def vmem_kernel(kernel, mib, **kwargs):
    call = pl.pallas_call(kernel, compiler_params=pltpu.CompilerParams(vmem_limit_bytes=mib * 2**20), **kwargs)

    def run(*args):
        spaces = {id(IN_VMEM): pltpu.VMEM, id(IN_HBM): pltpu.HBM}
        return call(
            *(
                pltpu.with_memory_space_constraint(x, spaces[id(spec)]) if id(spec) in spaces else x
                for x, spec in zip(args, kwargs["in_specs"])
            )
        )

    return run


def abn_kernel(step, rows, cols, counts, a_out, b_out, n_out, done, held, a, b, n, seen, sem, out_sem):
    slots, block = counts.shape[1], counts.shape[2]

    def piece(i):
        return pltpu.make_async_copy(counts.at[step, :, pl.ds(i * PIECE, PIECE), :], held.at[i], sem.at[i])

    def result(i, k, ref, out):
        part = pl.ds(i * PIECE, PIECE)
        return pltpu.make_async_copy(ref.at[:, :, part, :], out.at[:, :, part, :], out_sem.at[i, k])

    results = [
        [result(i, k, ref, out) for k, (ref, out) in enumerate(((a, a_out), (b, b_out), (n, n_out)))]
        for i in range(block // PIECE)
    ]
    for i in range(block // PIECE):
        piece(i).start()
    for ref in (a, b, done, seen):
        ref[...] = jnp.zeros(ref.shape, F32)
    sampled = {}
    for g in range(2):
        for h in range(2):
            total = jnp.int32(0)
            for slot in range(slots):
                total += ((rows[slot] == g) & (cols[slot] == h)).astype(jnp.int32)
            sampled[g, h] = total.astype(F32)
    for i in range(block // PIECE):
        piece(i).wait()

        def strip(j, carry):
            here = pl.ds(pl.multiple_of(j * STRIP, STRIP), STRIP)
            part = pl.ds(pl.multiple_of(i * PIECE + j * STRIP, STRIP), STRIP)
            for slot in range(slots):
                xf = held[i, slot, here, :].astype(F32)
                top = jnp.maximum(xf, 1.0)
                root = xf * lax.rsqrt(top)
                at = (rows[slot], cols[slot], part, slice(None))
                a[at] += root
                b[at] += (0.1 + 0.25 * root) * jnp.log(top)
                seen[at] += jnp.minimum(xf, 1.0)
            for g in range(2):
                for h in range(2):
                    number = seen[g, h, part, :]
                    a[g, h, part, :] = 0.1 * number + 0.25 * a[g, h, part, :]
                    n[g, h, part, :] = (sampled[g, h] - number).astype(BF16)
            return carry

        lax.fori_loop(0, PIECE // STRIP, strip, 0)
        for copy in results[i]:
            copy.start()
    for copies in results:
        for copy in copies:
            copy.wait()


def abn(counts, rows, cols, step):
    slots, block = counts.shape[1], counts.shape[2]
    shape = (2, 2, block, block)
    return vmem_kernel(
        functools.partial(abn_kernel, step),
        28,
        in_specs=[IN_SMEM, IN_SMEM, IN_HBM],
        out_specs=[IN_HBM] * 3 + [IN_VMEM],
        out_shape=[pltpu.HBM(shape, d) for d in (F32, F32, BF16)] + [pltpu.VMEM((8, 128), F32)],
        scratch_shapes=[
            pltpu.VMEM((block // PIECE, slots, PIECE, block), jnp.int32),
            *(pltpu.VMEM(shape, d) for d in (F32, F32, BF16, F32)),
            pltpu.SemaphoreType.DMA((block // PIECE,)),
            pltpu.SemaphoreType.DMA((block // PIECE, 3)),
        ],
        cost_estimate=pl.CostEstimate(flops=6 * 10**9, bytes_accessed=8 * 2**20, transcendentals=4 * 2**20),
        name="count_factors",
    )(rows, cols, counts)


def step_kernel(first, role, own, other, a, b, n, lr, lc, *refs):
    if first:
        keep, send, log_total, grads = refs
    else:
        log_total, keep, send, grads = refs

    def body(w, c, grad_w, grad_c):
        if first:
            pieces = c[:, 128:, :].astype(F32)
            log_total[...] = jnp.broadcast_to(
                jnp.log(jnp.sum(pieces, axis=(0, 1), keepdims=False)[None, :]), log_total.shape
            )
        for g in range(2):
            wg = w[4 * g : 4 * g + 4, :128, :].reshape(512, 512)
            total = None
            for h in range(2):
                ch = c[:, h * 64 : h * 64 + 64, :].reshape(512, 512)
                dots = jnp.dot(wg, ch, preferred_element_type=F32)
                t = dots + lr[g * 512 : g * 512 + 512, :] + (lc[h] - log_total[0:1, :])
                hinge = 0.5 + 0.5 * jnp.tanh(0.5 * t)
                grad = (t * a[g, h] - b[g, h] + n[g, h].astype(F32) * hinge).astype(BF16)
                grads[h, g * 512 : g * 512 + 512, :] = grad
                term = lax.dot_general(grad, ch, NT, preferred_element_type=F32)
                total = term if total is None else total + term
            grad_w[4 * g : 4 * g + 4] = total.reshape(4, 128, 512).astype(grad_w.dtype)
        w_all = w[:, :128, :].reshape(1024, 512)
        for h in range(2):
            term = lax.dot_general(w_all, grads[h], TN, preferred_element_type=F32)
            grad_c[:, h * 64 : h * 64 + 64, :] = term.reshape(8, 64, 512).astype(grad_c.dtype)

    @pl.when(role[0] == W_ROLE)
    def _():
        body(own, other, keep, send)

    @pl.when(role[0] != W_ROLE)
    def _():
        body(other, own, send, keep)


def step_grads(role, own, other, factors, lr, lc, log_total):
    first = log_total is None
    args = [role, own, other, *factors, lr, lc] + ([] if first else [log_total])
    shape = (8, 128, 512)
    out_shape = [pltpu.VMEM(shape, F32), pltpu.VMEM(shape, BF16)] + ([pltpu.VMEM((8, 512), F32)] if first else [])
    return vmem_kernel(
        functools.partial(step_kernel, first),
        24,
        in_specs=[IN_SMEM] + [IN_VMEM] * (len(args) - 1),
        out_specs=[IN_VMEM] * len(out_shape),
        out_shape=out_shape,
        scratch_shapes=[pltpu.VMEM((2, 1024, 512), BF16)],
        cost_estimate=pl.CostEstimate(flops=3 * 10**9, bytes_accessed=16 * 2**20, transcendentals=2**20),
        name="step_grads",
    )(*args)


def load_kernel(done, *refs):
    *ins_outs, sem = refs
    copies = [
        pltpu.make_async_copy(ins_outs[k].at[g, h], ins_outs[k + 3].at[g, h], sem.at[2 * g + h, k])
        for g in range(2)
        for h in range(2)
        for k in range(3)
    ]
    for copy in copies:
        copy.start()
    for copy in copies:
        copy.wait()


def load(done, factors):
    return vmem_kernel(
        load_kernel,
        2,
        in_specs=[IN_VMEM] + [IN_HBM] * 3,
        out_specs=[IN_VMEM] * 3,
        out_shape=[pltpu.VMEM(x.shape, x.dtype) for x in factors],
        scratch_shapes=[pltpu.SemaphoreType.DMA((4, 3))],
        cost_estimate=pl.CostEstimate(flops=0, bytes_accessed=20 * 2**20, transcendentals=0),
        name="load_factors",
    )(done, *factors)


def update_kernel(share, embed, new, payload=None, chunk=None, sem=None):
    total = share[0].astype(F32)
    for k in range(1, 8):
        total += share[k].astype(F32)
    fresh = embed[...] - RATE * total
    new[...] = fresh
    if payload is not None:
        chunk[...] = fresh.astype(BF16)
        copy_to_all(chunk, payload, sem)


def update(share, embed, last):
    more = not last
    return vmem_kernel(
        update_kernel,
        4,
        in_specs=[IN_VMEM] * 2,
        out_specs=[IN_VMEM] + [IN_HBM] * more,
        out_shape=[pltpu.VMEM(embed.shape, F32)] + [pltpu.HBM(share.shape, BF16)] * more,
        scratch_shapes=[pltpu.VMEM(embed.shape, BF16), pltpu.SemaphoreType.DMA((8,))] * more,
        name="update",
    )(share, embed)


def prep_kernel(role, row_embed, col_embed, marginals, embed, payload, sums, chunk, sem):
    sum_copy = pltpu.make_async_copy(marginals, sums, sem.at[0])
    sum_copy.start()

    @pl.when(role[0] == W_ROLE)
    def _():
        copy = pltpu.make_async_copy(row_embed, embed, sem.at[1])
        copy.start()
        copy.wait()

    @pl.when(role[0] != W_ROLE)
    def _():
        low = pltpu.make_async_copy(col_embed.at[:, pl.ds(0, 512)], embed.at[pl.ds(0, 64)], sem.at[1])
        high = pltpu.make_async_copy(col_embed.at[:, pl.ds(512, 512)], embed.at[pl.ds(64, 64)], sem.at[2])
        low.start()
        high.start()
        low.wait()
        high.wait()

    sum_copy.wait()
    mine = embed[...].astype(BF16)
    rest = jnp.sum(sums[...].astype(F32), axis=(0, 1), keepdims=True)
    line = lax.broadcasted_iota(jnp.int32, (8, 512), 0)
    extra = jnp.zeros((8, 512), F32)
    for k in range(3):
        piece = rest.astype(BF16).astype(F32)
        extra = jnp.where(line == k, piece, extra)
        rest = rest - piece
    chunk[:128, :] = mine
    chunk[128:, :] = extra.astype(BF16)
    copy_to_all(chunk, payload, sem)


def copy_to_all(chunk, payload, sem):
    copies = [pltpu.make_async_copy(chunk, payload.at[k], sem.at[k]) for k in range(8)]
    for copy in copies:
        copy.start()
    for copy in copies:
        copy.wait()


def prep(role, row_embed, col_embed, marginals):
    return vmem_kernel(
        prep_kernel,
        4,
        in_specs=[IN_SMEM, IN_HBM, IN_HBM, IN_HBM],
        out_specs=[IN_VMEM, IN_HBM],
        out_shape=[pltpu.VMEM((128, 512), F32), pltpu.HBM((8, 136, 512), BF16)],
        scratch_shapes=[
            pltpu.VMEM((8, 128), jnp.int32),
            pltpu.VMEM((136, 512), BF16),
            pltpu.SemaphoreType.DMA((8,)),
        ],
        name="first_payload",
    )(role, row_embed, col_embed, marginals.reshape(8, 128))


def finish_kernel(role, embed, theirs, new_row, new_col, sem):
    def write(row, col):
        copies = [
            pltpu.make_async_copy(row, new_row, sem.at[0]),
            pltpu.make_async_copy(col.at[pl.ds(0, 64)], new_col.at[:, pl.ds(0, 512)], sem.at[1]),
            pltpu.make_async_copy(col.at[pl.ds(64, 64)], new_col.at[:, pl.ds(512, 512)], sem.at[2]),
        ]
        for copy in copies:
            copy.start()
        for copy in copies:
            copy.wait()

    @pl.when(role[0] == W_ROLE)
    def _():
        write(embed, theirs)

    @pl.when(role[0] != W_ROLE)
    def _():
        write(theirs, embed)


def finish(role, embed, theirs):
    return vmem_kernel(
        finish_kernel,
        4,
        in_specs=[IN_SMEM, IN_VMEM, IN_VMEM],
        out_specs=[IN_HBM] * 2,
        out_shape=[pltpu.HBM((128, 512), F32), pltpu.HBM((64, 1024), F32)],
        scratch_shapes=[pltpu.SemaphoreType.DMA((3,))],
        name="results",
    )(role, embed, theirs)


def per_device(groups, swap, row_embed, col_embed, counts, block_rows, block_cols, row_marginals, col_marginals):
    role = lax.axis_index("rep").astype(jnp.int32).reshape(1)
    steps = counts.shape[0]

    def spread(x):
        return lax.all_to_all(x, AXES, 0, 0, axis_index_groups=groups, tiled=True)

    def other_core(x):
        return lax.ppermute(x, "rep", swap)

    embed, payload = prep(role, row_embed, col_embed, row_marginals)
    payload, block_rows, block_cols, row_marginals, col_marginals = lax.optimization_barrier(
        (payload, block_rows, block_cols, row_marginals, col_marginals)
    )
    lr = jnp.log(row_marginals.astype(F32))[:, None]
    lc = jnp.log(col_marginals.astype(F32)).reshape(2, 1, 512)
    rows = block_rows[:, :, 0, 0]
    cols = block_cols[:, :, 0, 0]

    log_total = None
    for step in range(steps):
        last = step + 1 == steps
        payload, rows, cols = lax.optimization_barrier((payload, rows, cols))
        own = spread(payload)
        *factors, done = abn(counts, rows[step], cols[step], step)
        own, done = lax.optimization_barrier((own, done))
        other = other_core(own)
        factors = load(done, factors)
        res = step_grads(role, own, other, factors, lr, lc, log_total)
        if step == 0:
            keep, send, log_total = res
        else:
            keep, send = res
        terms = (keep + other_core(send).astype(F32)).astype(BF16)
        res = update(spread(terms), embed, last)
        if last:
            (embed,) = res
        else:
            embed, payload = res
    return tuple(finish(role, embed, other_core(embed)))


def solution(mesh):
    n_row, n_col = mesh.shape["row"], mesh.shape["col"]
    index = lambda r, c, p: (r * n_col + c) * 2 + p
    groups = [[index(r, c, W_ROLE) for c in range(n_col)] for r in range(n_row)]
    groups += [[index(r, c, 1 - W_ROLE) for r in range(n_row)] for c in range(n_col)]
    swap = [(0, 1), (1, 0)]
    return jax.shard_map(
        functools.partial(per_device, groups, swap),
        mesh=mesh,
        in_specs=(
            P(("row", "col"), None),
            P("row", "col"),
            P(None, "rep", "row", "col"),
            P(None, "rep", "row", "col"),
            P(None, "rep", "row", "col"),
            P("row"),
            P("col"),
        ),
        out_specs=(P(("row", "col"), None), P("row", "col")),
        check_vma=False,
    )
```

time: 645 us -> 115 us (0.18)
  waiting for transfers between devices: 457 us -> 24 us
  local copies, waits for them, and re-layouts: 60 us -> 0.26 us
  matrix products: 58.4 us -> 0 us
  Pallas kernels: 0 us -> 36.3 us
  loops' own time: 21.6 us -> 0 us
  blocking collectives: 18.8 us -> 39.1 us
  between operations: 14.9 us -> 0.99 us
  starting transfers between devices: 0.4 us -> 13.3 us
  other arithmetic: 13.2 us -> 0.7 us
    reduce_scatter x4 -> x0, waiting for transfers between devices: 261 us -> none  [the longest x2 154 us: per_device(): share_w = lax.psum_scatter(part_w, 'col', scatter_dimension=0, tiled=True)]
    all_gather x4 -> x0, waiting for transfers between devices: 141 us -> none  [the longest x2 74.1 us: per_device(): lax.all_gather(col_embed.astype(jnp.bfloat16), 'row', axis=0, tiled=True)]
    dot_general x48 -> x0, matrix products: 58.4 us -> none  [the longest x16 41.8 us: add_block(): dots = jnp.dot(wblock, cblock, preferred_element_type=jnp.float32)]
    psum x2 -> x0, waiting for transfers between devices: 53.9 us -> none  [per_device(): share_w, share_c = lax.psum((share_w, share_c), 'rep')]
    all_to_all x0 -> x2, blocking collectives: none -> 39.1 us  [spread(): return lax.all_to_all(x, AXES, 0, 0, axis_index_groups=groups, tiled=True)]
    pallas_call x0 -> x10, Pallas kernels: none -> 36.3 us  [run(): call(*(pltpu.with_memory_space_constraint(x, spaces[id(spec)]) if id(spec...]
    while x96 -> x0, local copies, waits for them, and re-layouts: 22 us -> none
    another operation x2 -> x0, loops' own time: 21.6 us -> none  [per_device(): part_w, part_c = lax.fori_loop(0, slots, add_block, (empty_w, empty_c))]
  transfers between devices with their start and end apart: 10 -> 7, of which waited for: 10 -> 5; matrix products, arithmetic and copies ran while one was open for 3% -> 0% of each run, Pallas kernels for 0% -> 21%
where the time goes in v2:
time: 115 us
  blocking collectives  39.1 us (34%)
  Pallas kernels  36.3 us (32%)
  waiting for transfers between devices  24 us (21%)
  starting transfers between devices  13.3 us (12%)
    all_to_all x2, blocking collectives, spread(): return lax.all_to_all(x, AXES, 0, 0, axis_index_groups=groups, tiled=True)  39.1 us
    pallas_call x10, Pallas kernels, run(): call(*(pltpu.with_memory_space_constraint(x, spaces[id(spec)]) if id(spec...  36.3 us
    all_to_all x2, waiting for transfers between devices, spread(): return lax.all_to_all(x, AXES, 0, 0, axis_index_groups=groups, tiled=True)  17.9 us
    all_to_all x2, starting transfers between devices, spread(): return lax.all_to_all(x, AXES, 0, 0, axis_index_groups=groups, tiled=True)  11.9 us
    ppermute x5, waiting for transfers between devices, other_core(): return lax.ppermute(x, 'rep', swap)  6.1 us
  transfers between devices with their start and end apart: 7, of which 5 were waited for; matrix products, arithmetic and copies ran while one was open for 0% of the time, Pallas kernels for 21%

profile of v2, /device:TPU:1, one launch (start us, length us, event | category | flops | bytes accessed | tf_op | source)
XLA Modules:
  0.0 114.6 jit_solution(1278882211359106239)
XLA Ops:
  0.6 0.0 copy-start.3
  0.6 0.0 copy-start.2
  0.7 2.2 %first_payload.1 = (f32[128,512]{1,0:T(8,128)S(1)}, bf16[8,136,512]{2,1,0:T(8,128)(2,1)}) custom-call(s32[1]{0:T(128)} %bitcast.role, f32[128,512]{1,0:T(8,128)} %row_embed.1, f32[64,1024]{1,0:T(8,128)} %col_embed.1, s32[8,128]{1,0:T(8,128)} %bitcast.16), custom_call_target="tpu_custom_call" | custom-call | tf_op jit(solution)/shard_map/first_payload/pallas_call | solution.py:29
  2.8 7.5 %all-to-all-start = ((bf16[8,136,512]{2,1,0:T(8,128)(2,1)}), bf16[8,136,512]{2,1,0:T(8,128)(2,1)S(1)}, u32[]{:S(2)}, u32[]{:S(2)}) async-start(bf16[8,136,512]{2,1,0:T(8,128)(2,1)} %get-tuple-element.44), calls=%async_computation | async-start | bytes 2228224 | tf_op jit(solution)/shard_map/all_to_all | solution.py:315
  10.3 0.0 copy-done.3
  10.3 0.0 copy-done.2
  10.4 0.0 copy-start
  10.4 0.0 copy-start.1
  10.4 8.1 %count_factors.2 = (f32[2,2,512,512]{3,2,1,0:T(8,128)}, f32[2,2,512,512]{3,2,1,0:T(8,128)}, bf16[2,2,512,512]{3,2,1,0:T(8,128)(2,1)}, f32[8,128]{1,0:T(8,128)S(1)}) custom-call(s32[8]{0:T(128)S(1)} %get-tuple-element.79.rows, s32[8]{0:T(128)S(1)} %get-tuple-element.78.cols, s32[2,8,512,512]{3,2,1,0:T(8,128)} %counts.3), custom_call_target="tpu_custom_call" | custom-call | flops 6000000000 | bytes 8388608 | tf_op jit(solution)/shard_map/count_factors/pallas_call | solution.py:29
  18.5 9.7 %all-to-all-done.own = bf16[8,136,512]{2,1,0:T(8,128)(2,1)S(1)} async-done(((bf16[8,136,512]{2,1,0:T(8,128)(2,1)}), bf16[8,136,512]{2,1,0:T(8,128)(2,1)S(1)}, u32[]{:S(2)}, u32[]{:S(2)}) %all-to-all-start) | async-done | bytes 1114144 | tf_op jit(solution)/shard_map/all_to_all | solution.py:315
  28.2 0.0 collective-permute-start
  28.2 0.0 copy-done
  28.2 0.2 copy.9.lr
  28.5 0.0 copy-done.1
  28.5 4.1 %load_factors.2 = (f32[2,2,512,512]{3,2,1,0:T(8,128)S(1)}, f32[2,2,512,512]{3,2,1,0:T(8,128)S(1)}, bf16[2,2,512,512]{3,2,1,0:T(8,128)(2,1)S(1)}) custom-call(f32[8,128]{1,0:T(8,128)S(1)} %get-tuple-element.49.done, f32[2,2,512,512]{3,2,1,0:T(8,128)} %get-tuple-element.50.refs_0_, f32[2,2,512,512]{3,2,1,0:T(8,128)} %get-tuple-element.51.refs_1_, ...), custom_call_target="tpu_custom_call" | custom-call | bytes 20971520 | tf_op jit(solution)/shard_map/load_factors/pallas_call | solution.py:29
  32.6 0.0 collective-permute-done.other
  32.6 4.1 %step_grads.2 = (f32[8,128,512]{2,1,0:T(8,128)S(1)}, bf16[8,128,512]{2,1,0:T(8,128)(2,1)S(1)}, f32[8,512]{1,0:T(8,128)S(1)}) custom-call(s32[1]{0:T(128)} %bitcast.role, bf16[8,136,512]{2,1,0:T(8,128)(2,1)S(1)} %all-to-all-done.own, bf16[8,136,512]{2,1,0:T(8,128)(2,1)S(1)} %collective-permute-done.other, f32[2,2,512,512]{3,2,1,0:T(8,128)S(1)} %get-tuple-element.53.a, ...), custom_call_target="tpu_custom_call" | custom-call | flops 3000000000 | bytes 16777216 | tf_op jit(solution)/shard_map/step_grads/pallas_call | solution.py:29
  36.7 0.6 collective-permute-start.1
  37.3 2.3 %collective-permute-done.1 = bf16[8,128,512]{2,1,0:T(8,128)(2,1)S(1)} collective-permute-done((bf16[8,128,512]{2,1,0:T(8,128)(2,1)S(1)}, bf16[8,128,512]{2,1,0:T(8,128)(2,1)S(1)}, u32[]{:S(2)}, u32[]{:S(2)}) %collective-permute-start.1) | collective-permute-done | bytes 1048608 | tf_op jit(solution)/shard_map/ppermute | solution.py:318
  39.6 0.3 add_convert_fusion.1
  39.9 19.9 %all_to_all.20.share = bf16[8,128,512]{2,1,0:T(8,128)(2,1)S(1)} all-to-all(bf16[8,128,512]{2,1,0:T(8,128)(2,1)S(1)} %add_convert_fusion.1), channel_id=1, replica_groups={{1,3,5,7,9,11,13,15},{17,19,21,23,25,27,29,31},{33,35,37,39,41,43,45,47..., dimensions={0} | all-to-all | bytes 2097152 | tf_op jit(solution)/shard_map/all_to_all | solution.py:315
  59.8 1.2 %update.2 = (f32[128,512]{1,0:T(8,128)S(1)}, bf16[8,128,512]{2,1,0:T(8,128)(2,1)}) custom-call(bf16[8,128,512]{2,1,0:T(8,128)(2,1)S(1)} %all_to_all.20.share, f32[128,512]{1,0:T(8,128)S(1)} %get-tuple-element.60.embed), custom_call_target="tpu_custom_call" | custom-call | tf_op jit(solution)/shard_map/update/pallas_call | solution.py:29
  61.0 4.4 %all-to-all-start.2 = ((bf16[8,128,512]{2,1,0:T(8,128)(2,1)}), bf16[8,128,512]{2,1,0:T(8,128)(2,1)S(1)}, u32[]{:S(2)}, u32[]{:S(2)}) async-start(bf16[8,128,512]{2,1,0:T(8,128)(2,1)} %get-tuple-element.62), calls=%async_computation.2 | async-start | bytes 2097152 | tf_op jit(solution)/shard_map/all_to_all | solution.py:315
  65.5 7.7 %count_factors.3 = (f32[2,2,512,512]{3,2,1,0:T(8,128)}, f32[2,2,512,512]{3,2,1,0:T(8,128)}, bf16[2,2,512,512]{3,2,1,0:T(8,128)(2,1)}, f32[8,128]{1,0:T(8,128)S(1)}) custom-call(s32[8]{0:T(128)S(1)} %slice_bitcast_fusion.1.rows, s32[8]{0:T(128)S(1)} %slice_bitcast_fusion.cols, s32[2,8,512,512]{3,2,1,0:T(8,128)} %counts.3), custom_call_target="tpu_custom_call" | custom-call | flops 6000000000 | bytes 8388608 | tf_op jit(solution)/shard_map/count_factors/pallas_call | solution.py:29
  73.1 8.1 %all-to-all-done.2.own = bf16[8,128,512]{2,1,0:T(8,128)(2,1)S(1)} async-done(((bf16[8,128,512]{2,1,0:T(8,128)(2,1)}), bf16[8,128,512]{2,1,0:T(8,128)(2,1)S(1)}, u32[]{:S(2)}, u32[]{:S(2)}) %all-to-all-start.2) | async-done | bytes 1048608 | tf_op jit(solution)/shard_map/all_to_all | solution.py:315
  81.3 0.0 collective-permute-start.2
  81.3 4.1 %load_factors.3 = (f32[2,2,512,512]{3,2,1,0:T(8,128)S(1)}, f32[2,2,512,512]{3,2,1,0:T(8,128)S(1)}, bf16[2,2,512,512]{3,2,1,0:T(8,128)(2,1)S(1)}) custom-call(f32[8,128]{1,0:T(8,128)S(1)} %get-tuple-element.67.done, f32[2,2,512,512]{3,2,1,0:T(8,128)} %get-tuple-element.68.refs_0_, f32[2,2,512,512]{3,2,1,0:T(8,128)} %get-tuple-element.69.refs_1_, ...), custom_call_target="tpu_custom_call" | custom-call | bytes 20971520 | tf_op jit(solution)/shard_map/load_factors/pallas_call | solution.py:29
  85.3 0.0 collective-permute-done.2.other
  85.4 3.9 %step_grads.3 = (f32[8,128,512]{2,1,0:T(8,128)S(1)}, bf16[8,128,512]{2,1,0:T(8,128)(2,1)S(1)}) custom-call(s32[1]{0:T(128)} %bitcast.role, bf16[8,128,512]{2,1,0:T(8,128)(2,1)S(1)} %all-to-all-done.2.own, bf16[8,128,512]{2,1,0:T(8,128)(2,1)S(1)} %collective-permute-done.2.other, f32[2,2,512,512]{3,2,1,0:T(8,128)S(1)} %get-tuple-element.71.a, ...), custom_call_target="tpu_custom_call" | custom-call | flops 3000000000 | bytes 16777216 | tf_op jit(solution)/shard_map/step_grads/pallas_call | solution.py:29
  89.3 0.7 collective-permute-start.3
  90.0 2.3 %collective-permute-done.3 = bf16[8,128,512]{2,1,0:T(8,128)(2,1)S(1)} collective-permute-done((bf16[8,128,512]{2,1,0:T(8,128)(2,1)S(1)}, bf16[8,128,512]{2,1,0:T(8,128)(2,1)S(1)}, u32[]{:S(2)}, u32[]{:S(2)}) %collective-permute-start.3) | collective-permute-done | bytes 1048608 | tf_op jit(solution)/shard_map/ppermute | solution.py:318
  92.3 0.3 add_convert_fusion
  92.7 19.2 %all_to_all.21.share = bf16[8,128,512]{2,1,0:T(8,128)(2,1)S(1)} all-to-all(bf16[8,128,512]{2,1,0:T(8,128)(2,1)S(1)} %add_convert_fusion), channel_id=1, replica_groups={{1,3,5,7,9,11,13,15},{17,19,21,23,25,27,29,31},{33,35,37,39,41,43,45,47..., dimensions={0} | all-to-all | bytes 2097152 | tf_op jit(solution)/shard_map/all_to_all | solution.py:315
  111.8 0.2 update.3.embed
  112.0 0.1 collective-permute-start.4
  112.1 1.5 %collective-permute-done.4.theirs = f32[128,512]{1,0:T(8,128)S(1)} collective-permute-done((f32[128,512]{1,0:T(8,128)S(1)}, f32[128,512]{1,0:T(8,128)S(1)}, u32[]{:S(2)}, u32[]{:S(2)}) %collective-permute-start.4) | collective-permute-done | bytes 262176 | tf_op jit(solution)/shard_map/ppermute | solution.py:318
  113.6 0.8 results.1
  (5 shorter events, 0.0 us)
Async XLA Ops:
  0.6 9.7 %copy-start.3 = (s32[2,8,1,1]{1,3,2,0:T(1,128)S(1)}, s32[2,8,1,1]{1,3,2,0:T(1,128)}, u32[]{:S(2)}) copy-start(s32[2,8,1,1]{1,3,2,0:T(1,128)} %param.10) | copy-start | bytes 196
  0.6 9.7 %copy-start.2 = (s32[2,8,1,1]{1,3,2,0:T(1,128)S(1)}, s32[2,8,1,1]{1,3,2,0:T(1,128)}, u32[]{:S(2)}) copy-start(s32[2,8,1,1]{1,3,2,0:T(1,128)} %param.11) | copy-start | bytes 196
  2.8 25.4 %all-to-all-start = ((bf16[8,136,512]{2,1,0:T(8,128)(2,1)}), bf16[8,136,512]{2,1,0:T(8,128)(2,1)S(1)}, u32[]{:S(2)}, u32[]{:S(2)}) async-start(bf16[8,136,512]{2,1,0:T(8,128)(2,1)} %get-tuple-element.44), calls=%async_computation | async-start | bytes 2228224 | tf_op jit(solution)/shard_map/all_to_all | solution.py:315
  10.4 17.9 %copy-start = (s32[1024]{0:T(1024)S(1)}, s32[1024]{0:T(1024)}, u32[]{:S(2)}) copy-start(s32[1024]{0:T(1024)} %param.12) | copy-start | bytes 12292
  10.4 18.1 %copy-start.1 = (s32[1024]{0:T(1024)S(1)}, s32[1024]{0:T(1024)}, u32[]{:S(2)}) copy-start(s32[1024]{0:T(1024)} %param.13) | copy-start | bytes 12292
  28.2 4.4 %collective-permute-start = (bf16[8,136,512]{2,1,0:T(8,128)(2,1)S(1)}, bf16[8,136,512]{2,1,0:T(8,128)(2,1)S(1)}, u32[]{:S(2)}, u32[]{:S(2)}) collective-permute-start(bf16[8,136,512]{2,1,0:T(8,128)(2,1)S(1)} %all-to-all-done.own), channel_id=1, source_target_pairs={{0,1},{1,0},{2,3},{3,2},{4,5},{5,4},{6,7},{7,6},{8,9},{9,8},{10,11... | collective-permute-start | bytes 3342344 | tf_op jit(solution)/shard_map/ppermute | solution.py:318
  36.7 2.9 %collective-permute-start.1 = (bf16[8,128,512]{2,1,0:T(8,128)(2,1)S(1)}, bf16[8,128,512]{2,1,0:T(8,128)(2,1)S(1)}, u32[]{:S(2)}, u32[]{:S(2)}) collective-permute-start(bf16[8,128,512]{2,1,0:T(8,128)(2,1)S(1)} %get-tuple-element.59), channel_id=1, source_target_pairs={{0,1},{1,0},{2,3},{3,2},{4,5},{5,4},{6,7},{7,6},{8,9},{9,8},{10,11... | collective-permute-start | bytes 3145736 | tf_op jit(solution)/shard_map/ppermute | solution.py:318
  61.0 20.3 %all-to-all-start.2 = ((bf16[8,128,512]{2,1,0:T(8,128)(2,1)}), bf16[8,128,512]{2,1,0:T(8,128)(2,1)S(1)}, u32[]{:S(2)}, u32[]{:S(2)}) async-start(bf16[8,128,512]{2,1,0:T(8,128)(2,1)} %get-tuple-element.62), calls=%async_computation.2 | async-start | bytes 2097152 | tf_op jit(solution)/shard_map/all_to_all | solution.py:315
  81.3 4.1 %collective-permute-start.2 = (bf16[8,128,512]{2,1,0:T(8,128)(2,1)S(1)}, bf16[8,128,512]{2,1,0:T(8,128)(2,1)S(1)}, u32[]{:S(2)}, u32[]{:S(2)}) collective-permute-start(bf16[8,128,512]{2,1,0:T(8,128)(2,1)S(1)} %all-to-all-done.2.own), channel_id=1, source_target_pairs={{0,1},{1,0},{2,3},{3,2},{4,5},{5,4},{6,7},{7,6},{8,9},{9,8},{10,11... | collective-permute-start | bytes 3145736 | tf_op jit(solution)/shard_map/ppermute | solution.py:318
  89.3 3.0 %collective-permute-start.3 = (bf16[8,128,512]{2,1,0:T(8,128)(2,1)S(1)}, bf16[8,128,512]{2,1,0:T(8,128)(2,1)S(1)}, u32[]{:S(2)}, u32[]{:S(2)}) collective-permute-start(bf16[8,128,512]{2,1,0:T(8,128)(2,1)S(1)} %get-tuple-element.76), channel_id=1, source_target_pairs={{0,1},{1,0},{2,3},{3,2},{4,5},{5,4},{6,7},{7,6},{8,9},{9,8},{10,11... | collective-permute-start | bytes 3145736 | tf_op jit(solution)/shard_map/ppermute | solution.py:318
  112.0 1.6 %collective-permute-start.4 = (f32[128,512]{1,0:T(8,128)S(1)}, f32[128,512]{1,0:T(8,128)S(1)}, u32[]{:S(2)}, u32[]{:S(2)}) collective-permute-start(f32[128,512]{1,0:T(8,128)S(1)} %update.3.embed), channel_id=1, source_target_pairs={{0,1},{1,0},{2,3},{3,2},{4,5},{5,4},{6,7},{7,6},{8,9},{9,8},{10,11... | collective-permute-start | bytes 786440 | tf_op jit(solution)/shard_map/ppermute | solution.py:318

commit v3 on v2

v3 whole, which is shorter than its diff:
```python
import functools

import jax
import jax.numpy as jnp
from jax import lax
from jax.experimental import pallas as pl
from jax.experimental.pallas import tpu as pltpu
from jax.sharding import PartitionSpec as P

RATE = 0.002
AXES = ("row", "col", "rep")
F32 = jnp.float32
BF16 = jnp.bfloat16
W_ROLE = 1
PIECE = 64
STRIP = 16
NT = (((1,), (1,)), ((), ()))
TN = (((0,), (0,)), ((), ()))
IN_VMEM = pl.BlockSpec(memory_space=pltpu.VMEM)
IN_HBM = pl.BlockSpec(memory_space=pltpu.HBM)
IN_SMEM = pl.BlockSpec(memory_space=pltpu.SMEM)


def vmem_kernel(kernel, mib, **kwargs):
    call = pl.pallas_call(kernel, compiler_params=pltpu.CompilerParams(vmem_limit_bytes=mib * 2**20), **kwargs)

    def run(*args):
        spaces = {id(IN_VMEM): pltpu.VMEM, id(IN_HBM): pltpu.HBM}
        return call(
            *(
                pltpu.with_memory_space_constraint(x, spaces[id(spec)]) if id(spec) in spaces else x
                for x, spec in zip(args, kwargs["in_specs"])
            )
        )

    return run


def place(here):
    i = here[0]
    col, row = (i >> 1) & 7, i >> 4
    return i & 1, (col >> 1, col & 1), (row >> 1, row & 1)


def own_place(here):
    role, of_w, of_c = place(here)
    return [jnp.where(role == W_ROLE, p, q) for p, q in zip(of_w, of_c)]


def abn_kernel(step, half, rows, cols, counts, a, b, n, done, held, seen, sem):
    slots, extent = counts.shape[1], counts.shape[2] // 2

    def piece(i):
        part = pl.ds(half * extent + i * PIECE, PIECE)
        return pltpu.make_async_copy(counts.at[step, :, part, :], held.at[i], sem.at[i])

    for i in range(extent // PIECE):
        piece(i).start()
    for ref in (a, b, done, seen):
        ref[...] = jnp.zeros(ref.shape, F32)
    sampled = {}
    for g in range(2):
        for h in range(2):
            total = jnp.int32(0)
            for slot in range(slots):
                total += ((rows[step, slot] == g) & (cols[step, slot] == h)).astype(jnp.int32)
            sampled[g, h] = total.astype(F32)
    for i in range(extent // PIECE):
        piece(i).wait()

        def strip(j, carry):
            here = pl.ds(pl.multiple_of(j * STRIP, STRIP), STRIP)
            part = pl.ds(pl.multiple_of(i * PIECE + j * STRIP, STRIP), STRIP)
            for slot in range(slots):
                xf = held[i, slot, here, :].astype(F32)
                top = jnp.maximum(xf, 1.0)
                root = xf * lax.rsqrt(top)
                at = (rows[step, slot], cols[step, slot], part, slice(None))
                a[at] += root
                b[at] += (0.1 + 0.25 * root) * jnp.log(top)
                seen[at] += jnp.minimum(xf, 1.0)
            for g in range(2):
                for h in range(2):
                    number = seen[g, h, part, :]
                    a[g, h, part, :] = 0.1 * number + 0.25 * a[g, h, part, :]
                    n[g, h, part, :] = (sampled[g, h] - number).astype(BF16)
            return carry

        lax.fori_loop(0, PIECE // STRIP, strip, 0)


def abn(counts, rows, cols, step, half):
    slots, block = counts.shape[1], counts.shape[2]
    shape = (2, 2, block // 2, block)
    pieces = block // 2 // PIECE
    *factors, done = vmem_kernel(
        functools.partial(abn_kernel, step, half),
        8,
        in_specs=[IN_SMEM, IN_SMEM, IN_HBM],
        out_specs=[IN_VMEM] * 4,
        out_shape=[pltpu.VMEM(shape, d) for d in (F32, F32, BF16)] + [pltpu.VMEM((8, 128), F32)],
        scratch_shapes=[
            pltpu.VMEM((pieces, slots, PIECE, block), jnp.int32),
            pltpu.VMEM(shape, F32),
            pltpu.SemaphoreType.DMA((pieces,)),
        ],
        cost_estimate=pl.CostEstimate(flops=3 * 10**9, bytes_accessed=4 * 2**20, transcendentals=2 * 2**20),
        name="count_factors",
    )(rows, cols, counts)
    return factors, done


def front_kernel(first, here, own_a, own_b, other_a, other_b, *refs):
    a, b, n = refs[0:6:3], refs[1:6:3], refs[2:6:3]
    lr, lc, *refs = refs[6:]
    if first:
        w, c, grads, send, log_total = refs
    else:
        log_total, w, c, grads, send = refs
    role, (_, ws), (_, cs) = place(here)

    def assemble(w_a, w_b, c_a, c_b):
        for k in range(4):
            w[2 * k + ws] = w_a[k, :128, :]
            w[2 * k + 1 - ws] = w_b[k, :128, :]
            c[2 * k + cs] = c_a[k, :128, :]
            c[2 * k + 1 - cs] = c_b[k, :128, :]
        if first:
            pieces = c_a[:, 128:, :].astype(F32) + c_b[:, 128:, :].astype(F32)
            log_total[...] = jnp.broadcast_to(
                jnp.log(jnp.sum(pieces, axis=(0, 1), keepdims=False)[None, :]), log_total.shape
            )

    @pl.when(role == W_ROLE)
    def _():
        assemble(own_a, own_b, other_a, other_b)

    @pl.when(role != W_ROLE)
    def _():
        assemble(other_a, other_b, own_a, own_b)

    for g in range(2):
        wg = w[4 * g : 4 * g + 4].reshape(512, 512)
        for h in range(2):
            ch = c[:, h * 64 : h * 64 + 64, :].reshape(512, 512)
            dots = jnp.dot(wg, ch, preferred_element_type=F32)
            t = dots + jnp.tile(lr[g * 512 : g * 512 + 512, :], (1, 4)) + (lc[h] - log_total[0:1, :])
            hinge = 0.5 + 0.5 * jnp.tanh(0.5 * t)
            for e in range(2):
                part = slice(e * 256, e * 256 + 256)
                grad = t[part] * a[e][g, h] - b[e][g, h] + n[e][g, h].astype(F32) * hinge[part]
                grads[h, g * 512 + e * 256 : g * 512 + e * 256 + 256, :] = grad.astype(BF16)

    @pl.when(role == W_ROLE)
    def _():
        col_grad(w, c, grads, send)

    @pl.when(role != W_ROLE)
    def _():
        row_grad(w, c, grads, send)


def row_grad(w, c, grads, out):
    for g in range(2):
        total = jnp.zeros((512, 512), F32)
        for h in range(2):
            ch = c[:, h * 64 : h * 64 + 64, :].reshape(512, 512)
            total += lax.dot_general(grads[h, g * 512 : g * 512 + 512, :], ch, NT, preferred_element_type=F32)
        out[4 * g : 4 * g + 4] = total.reshape(4, 128, 512).astype(out.dtype)


def col_grad(w, c, grads, out):
    w_all = w[...].reshape(1024, 512)
    for h in range(2):
        total = lax.dot_general(w_all, grads[h], TN, preferred_element_type=F32)
        out[:, h * 64 : h * 64 + 64, :] = total.reshape(8, 64, 512).astype(out.dtype)


def front(here, gathered, factors, lr, lc, log_total):
    first = log_total is None
    args = [here, *gathered, *factors, lr, lc] + ([] if first else [log_total])
    shape = (8, 128, 512)
    out_shape = [pltpu.VMEM(s, BF16) for s in (shape, shape, (2, 1024, 512), shape)]
    if first:
        out_shape.append(pltpu.VMEM((8, 512), F32))
    return vmem_kernel(
        functools.partial(front_kernel, first),
        16,
        in_specs=[IN_SMEM] + [IN_VMEM] * (len(args) - 1),
        out_specs=[IN_VMEM] * len(out_shape),
        out_shape=out_shape,
        cost_estimate=pl.CostEstimate(flops=3 * 10**9, bytes_accessed=16 * 2**20, transcendentals=2**20),
        name="cell_grads",
    )(*args)


def back_kernel(here, w, c, grads, keep):
    role, _, _ = place(here)

    @pl.when(role == W_ROLE)
    def _():
        row_grad(w, c, grads, keep)

    @pl.when(role != W_ROLE)
    def _():
        col_grad(w, c, grads, keep)


def back(here, w, c, grads):
    return vmem_kernel(
        back_kernel,
        12,
        in_specs=[IN_SMEM] + [IN_VMEM] * 3,
        out_specs=IN_VMEM,
        out_shape=pltpu.VMEM(w.shape, F32),
        cost_estimate=pl.CostEstimate(flops=10**9, bytes_accessed=8 * 2**20, transcendentals=0),
        name="own_products",
    )(here, w, c, grads)


def merge_kernel(here, keep, extra, *outs):
    at, _ = own_place(here)
    for k, out in enumerate(outs):
        block = pl.ds(2 * ((at + k) & 3), 2)
        out[...] = (keep[block] + extra[block].astype(F32)).astype(BF16)


def merge(here, keep, extra):
    return vmem_kernel(
        merge_kernel,
        8,
        in_specs=[IN_SMEM] + [IN_VMEM] * 2,
        out_specs=[IN_VMEM] * 4,
        out_shape=[pltpu.VMEM((2, 128, 512), BF16)] * 4,
        name="core_sum",
    )(here, keep, extra)


def ring_sum_kernel(here, *refs):
    *terms, mine, theirs = refs
    _, side = own_place(here)

    def total(s):
        out = terms[0][s].astype(F32)
        for term in terms[1:4]:
            out += term[s].astype(F32)
        return out

    mine[...] = total(side)
    theirs[...] = total(1 - side).astype(BF16)


def ring_sum(here, terms, *after):
    return vmem_kernel(
        ring_sum_kernel,
        8,
        in_specs=[IN_SMEM] + [IN_VMEM] * (4 + len(after)),
        out_specs=[IN_VMEM] * 2,
        out_shape=[pltpu.VMEM((128, 512), F32), pltpu.VMEM((128, 512), BF16)],
        name="ring_sum",
    )(here, *terms, *after)


def pack_kernel(here, *refs):
    at, _ = own_place(here)
    for k in range(4):
        refs[-1][(at - k) & 3] = refs[k][...]


def pack(here, shards, *after):
    return vmem_kernel(
        pack_kernel,
        4,
        in_specs=[IN_SMEM] + [IN_VMEM] * (4 + len(after)),
        out_specs=IN_VMEM,
        out_shape=pltpu.VMEM((4, *shards[0].shape), BF16),
        name="in_ring_order",
    )(here, *shards, *after)


def update_kernel(mine, theirs, embed, new, payload=None):
    fresh = embed[...] - RATE * (mine[...] + theirs[...].astype(F32))
    new[...] = fresh
    if payload is not None:
        payload[...] = fresh.astype(BF16)


def update(mine, theirs, embed, last):
    more = not last
    return vmem_kernel(
        update_kernel,
        4,
        in_specs=[IN_VMEM] * 3,
        out_specs=[IN_VMEM] * (1 + more),
        out_shape=[pltpu.VMEM(embed.shape, F32)] + [pltpu.VMEM(embed.shape, BF16)] * more,
        name="update",
    )(mine, theirs, embed)


def logs_kernel(row_marginals, col_marginals, lr, lc, rows, cols, sem):
    copies = [
        pltpu.make_async_copy(row_marginals, rows, sem.at[0]),
        pltpu.make_async_copy(col_marginals, cols, sem.at[1]),
    ]
    for copy in copies:
        copy.start()
    for copy in copies:
        copy.wait()
    log_rows = jnp.log(rows[...].astype(F32))
    log_cols = jnp.log(cols[...].astype(F32))
    for k in range(8):
        lr[k * 128 : k * 128 + 128, :] = jnp.broadcast_to(log_rows[k : k + 1, :], (128, 128)).T
    for h in range(2):
        lc[h] = jnp.concatenate([log_cols[4 * h + k : 4 * h + k + 1, :] for k in range(4)], axis=1)


def logs(row_marginals, col_marginals):
    return vmem_kernel(
        logs_kernel,
        4,
        in_specs=[IN_HBM] * 2,
        out_specs=[IN_VMEM] * 2,
        out_shape=[pltpu.VMEM((1024, 128), F32), pltpu.VMEM((2, 1, 512), F32)],
        scratch_shapes=[pltpu.VMEM((8, 128), jnp.int32)] * 2 + [pltpu.SemaphoreType.DMA((2,))],
        name="log_marginals",
    )(row_marginals.reshape(8, 128), col_marginals.reshape(8, 128))


def prep_kernel(here, row_embed, col_embed, marginals, embed, payload, sums, sem):
    sum_copy = pltpu.make_async_copy(marginals, sums, sem.at[0])
    sum_copy.start()

    @pl.when(place(here)[0] == W_ROLE)
    def _():
        copy = pltpu.make_async_copy(row_embed, embed, sem.at[1])
        copy.start()
        copy.wait()

    @pl.when(place(here)[0] != W_ROLE)
    def _():
        low = pltpu.make_async_copy(col_embed.at[:, pl.ds(0, 512)], embed.at[pl.ds(0, 64)], sem.at[1])
        high = pltpu.make_async_copy(col_embed.at[:, pl.ds(512, 512)], embed.at[pl.ds(64, 64)], sem.at[2])
        low.start()
        high.start()
        low.wait()
        high.wait()

    sum_copy.wait()
    mine = embed[...].astype(BF16)
    rest = jnp.sum(sums[...].astype(F32), axis=(0, 1), keepdims=True)
    line = lax.broadcasted_iota(jnp.int32, (8, 512), 0)
    extra = jnp.zeros((8, 512), F32)
    for k in range(3):
        piece = rest.astype(BF16).astype(F32)
        extra = jnp.where(line == k, piece, extra)
        rest = rest - piece
    payload[:128, :] = mine
    payload[128:, :] = extra.astype(BF16)


def prep(here, row_embed, col_embed, marginals):
    return vmem_kernel(
        prep_kernel,
        4,
        in_specs=[IN_SMEM, IN_HBM, IN_HBM, IN_HBM],
        out_specs=[IN_VMEM] * 2,
        out_shape=[pltpu.VMEM((128, 512), F32), pltpu.VMEM((136, 512), BF16)],
        scratch_shapes=[pltpu.VMEM((8, 128), jnp.int32), pltpu.SemaphoreType.DMA((3,))],
        name="first_payload",
    )(here, row_embed, col_embed, marginals.reshape(8, 128))


def finish_kernel(here, embed, theirs, new_row, new_col, sem):
    def write(row, col):
        copies = [
            pltpu.make_async_copy(row, new_row, sem.at[0]),
            pltpu.make_async_copy(col.at[pl.ds(0, 64)], new_col.at[:, pl.ds(0, 512)], sem.at[1]),
            pltpu.make_async_copy(col.at[pl.ds(64, 64)], new_col.at[:, pl.ds(512, 512)], sem.at[2]),
        ]
        for copy in copies:
            copy.start()
        for copy in copies:
            copy.wait()

    @pl.when(place(here)[0] == W_ROLE)
    def _():
        write(embed, theirs)

    @pl.when(place(here)[0] != W_ROLE)
    def _():
        write(theirs, embed)


def finish(here, embed, theirs):
    return vmem_kernel(
        finish_kernel,
        4,
        in_specs=[IN_SMEM, IN_VMEM, IN_VMEM],
        out_specs=[IN_HBM] * 2,
        out_shape=[pltpu.HBM((128, 512), F32), pltpu.HBM((64, 1024), F32)],
        scratch_shapes=[pltpu.SemaphoreType.DMA((3,))],
        name="results",
    )(here, embed, theirs)


def per_device(swap, across, along, row_embed, col_embed, counts, block_rows, block_cols, row_marginals, col_marginals):
    here = lax.axis_index(AXES).astype(jnp.int32).reshape(1)
    steps = counts.shape[0]

    def other_core(x):
        return lax.ppermute(x, "rep", swap)

    def other_side(x):
        return lax.ppermute(x, AXES, across)

    def ring(x, k):
        return lax.ppermute(x, AXES, along[k])

    embed, payload = prep(here, row_embed, col_embed, row_marginals)
    payload, block_rows, block_cols, row_marginals, col_marginals = lax.optimization_barrier(
        (payload, block_rows, block_cols, row_marginals, col_marginals)
    )
    lr, lc = logs(row_marginals, col_marginals)
    rows = block_rows.reshape(block_rows.shape[:2])
    cols = block_cols.reshape(block_cols.shape[:2])

    low, done_low = abn(counts, rows, cols, 0, 0)
    log_total = None
    for step in range(steps):
        last = step + 1 == steps
        payload, rows, cols = lax.optimization_barrier((payload, rows, cols))
        far = other_side(payload)
        near = [payload] + [ring(payload, k) for k in (1, 3, 2)]
        far = [far] + [ring(far, k) for k in (1, 3, 2)]
        high, done_high = abn(counts, rows, cols, step, 1)
        in_order = lambda x: [x[0], x[1], x[3], x[2]]
        near = pack(here, in_order(near), done_low)
        near_other = other_core(near)
        far = pack(here, in_order(far), done_high)
        far_other = other_core(far)
        res = front(here, (near, far, near_other, far_other), low + high, lr, lc, log_total)
        if step == 0:
            *res, log_total = res
        w, c, grads, send = res
        extra = other_core(send)
        keep = back(here, w, c, grads)
        terms = merge(here, keep, extra)
        after = []
        if not last:
            *terms, rows, cols = lax.optimization_barrier((*terms, rows, cols))
            low, done_low = abn(counts, rows, cols, step + 1, 0)
            after = [done_low]
        got = {k: ring(terms[k], k) for k in (2, 1, 3)}
        mine, theirs = ring_sum(here, [terms[0], got[1], got[2], got[3]], *after)
        res = update(mine, other_side(theirs), embed, last)
        if last:
            (embed,) = res
        else:
            embed, payload = res
    return tuple(finish(here, embed, other_core(embed)))


def solution(mesh):
    n_row, n_col = mesh.shape["row"], mesh.shape["col"]
    across, along = [], {1: [], 2: [], 3: []}
    for r in range(n_row):
        for c in range(n_col):
            for p in range(2):
                i = (r * n_col + c) * 2 + p
                if p == W_ROLE:
                    across.append((i, (r * n_col + (c ^ 1)) * 2 + p))
                    for k in along:
                        along[k].append((i, (r * n_col + (c + 2 * k) % n_col) * 2 + p))
                else:
                    across.append((i, ((r ^ 1) * n_col + c) * 2 + p))
                    for k in along:
                        along[k].append((i, ((r + 2 * k) % n_row * n_col + c) * 2 + p))
    swap = [(0, 1), (1, 0)]
    return jax.shard_map(
        functools.partial(per_device, swap, across, along),
        mesh=mesh,
        in_specs=(
            P(("row", "col"), None),
            P("row", "col"),
            P(None, "rep", "row", "col"),
            P(None, "rep", "row", "col"),
            P(None, "rep", "row", "col"),
            P("row"),
            P("col"),
        ),
        out_specs=(P(("row", "col"), None), P("row", "col")),
        check_vma=False,
    )
```

time: 115 us -> 96.1 us (0.84)
  blocking collectives: 39.1 us -> 0 us
  starting transfers between devices: 13.3 us -> 43.6 us
  Pallas kernels: 36.3 us -> 30.9 us
  waiting for transfers between devices: 24 us -> 19 us
    all_to_all x2 -> x0, blocking collectives: 39.1 us -> none  [spread(): return lax.all_to_all(x, AXES, 0, 0, axis_index_groups=groups, tiled=True)]
    ppermute x0 -> x22, starting transfers between devices: none -> 35.8 us  [the longest x18 24.2 us: ring(): return lax.ppermute(x, AXES, along[k])]
    all_to_all x2 -> x0, waiting for transfers between devices: 17.9 us -> none  [spread(): return lax.all_to_all(x, AXES, 0, 0, axis_index_groups=groups, tiled=True)]
    ppermute x0 -> x22, waiting for transfers between devices: none -> 13.6 us  [the longest x18 7.61 us: ring(): return lax.ppermute(x, AXES, along[k])]
    all_to_all x2 -> x0, starting transfers between devices: 11.9 us -> none  [spread(): return lax.all_to_all(x, AXES, 0, 0, axis_index_groups=groups, tiled=True)]
    ppermute x5 -> x7, starting transfers between devices: 1.39 us -> 7.81 us  [other_core(): return lax.ppermute(x, 'rep', swap)]
    pallas_call x10 -> x21, Pallas kernels: 36.3 us -> 30.9 us  [run(): call(*(pltpu.with_memory_space_constraint(x, spaces[id(spec)]) if id(spec...]
    unnamed x8, local copies, waits for them, and re-layouts: 0.02 us -> 1.37 us
  transfers between devices with their start and end apart: 7 -> 29, of which waited for: 5 -> 11; matrix products, arithmetic and copies ran while one was open for 0% -> 0% of each run, Pallas kernels for 21% -> 22%
where the time goes in v3:
time: 96.1 us; the launch traced here: 95.9 us
  starting transfers between devices  43.6 us (45%)
  Pallas kernels  30.9 us (32%)
  waiting for transfers between devices  19 us (20%)
  local copies, waits for them, and re-layouts  1.37 us (1%)
  between operations  1.03 us (1%)
    pallas_call x21, Pallas kernels, run(): call(*(pltpu.with_memory_space_constraint(x, spaces[id(spec)]) if id(spec...  30.9 us
    ppermute x18, starting transfers between devices, ring(): return lax.ppermute(x, AXES, along[k])  24.2 us
    ppermute x4, starting transfers between devices, other_side(): return lax.ppermute(x, AXES, across)  11.6 us
    ppermute x7, starting transfers between devices, other_core(): return lax.ppermute(x, 'rep', swap)  7.81 us
    ppermute x18, waiting for transfers between devices, ring(): return lax.ppermute(x, AXES, along[k])  7.61 us
    ppermute x4, waiting for transfers between devices, other_side(): return lax.ppermute(x, AXES, across)  6.02 us
    ppermute x7, waiting for transfers between devices, other_core(): return lax.ppermute(x, 'rep', swap)  5.33 us
  transfers between devices with their start and end apart: 29, of which 11 were waited for; matrix products, arithmetic and copies ran while one was open for 0% of the time, Pallas kernels for 22%

profile of v3, /device:TPU:1, one launch (start us, length us, event | category | flops | bytes accessed | tf_op | source)
XLA Modules:
  0.0 95.9 jit_solution(7972952932544704962)
XLA Ops:
  0.6 1.1 %first_payload.1 = (f32[128,512]{1,0:T(8,128)S(1)}, bf16[136,512]{1,0:T(8,128)(2,1)S(1)}) custom-call(s32[1]{0:T(128)} %bitcast.here, f32[128,512]{1,0:T(8,128)} %row_embed.1, f32[64,1024]{1,0:T(8,128)} %col_embed.1, s32[8,128]{1,0:T(8,128)} %bitcast.14), custom_call_target="tpu_custom_call" | custom-call | tf_op jit(solution)/shard_map/first_payload/pallas_call | solution.py:29
  1.8 3.7 %collective-permute-start.3 = (bf16[136,512]{1,0:T(8,128)(2,1)S(1)}, bf16[136,512]{1,0:T(8,128)(2,1)S(1)}, u32[]{:S(2)}, u32[]{:S(2)}) collective-permute-start(bf16[136,512]{1,0:T(8,128)(2,1)S(1)} %get-tuple-element.66.refs_0_), channel_id=1, source_target_pairs={{0,16},{1,3},{2,18},{3,1},{4,20},{5,7},{6,22},{7,5},{8,24},{9,11},... | collective-permute-start | bytes 417800 | tf_op jit(solution)/shard_map/ppermute | solution.py:414
  5.4 2.7 %collective-permute-start.2 = (bf16[136,512]{1,0:T(8,128)(2,1)S(1)}, bf16[136,512]{1,0:T(8,128)(2,1)S(1)}, u32[]{:S(2)}, u32[]{:S(2)}) collective-permute-start(bf16[136,512]{1,0:T(8,128)(2,1)S(1)} %get-tuple-element.66.refs_0_), channel_id=1, source_target_pairs={{0,96},{1,13},{2,98},{3,15},{4,100},{5,1},{6,102},{7,3},{8,104},{9... | collective-permute-start | bytes 417800 | tf_op jit(solution)/shard_map/ppermute | solution.py:417
  8.5 0.7 collective-permute-start
  9.2 0.7 copy-done
  9.9 0.7 copy-done.2
  10.6 4.3 %count_factors.4 = (f32[2,2,256,512]{3,2,1,0:T(8,128)S(1)}, f32[2,2,256,512]{3,2,1,0:T(8,128)S(1)}, bf16[2,2,256,512]{3,2,1,0:T(8,128)(2,1)S(1)}, f32[8,128]{1,0:T(8,128)S(1)}) custom-call(s32[2,8]{1,0:T(2,128)S(1)} %bitcast.6, s32[2,8]{1,0:T(2,128)S(1)} %bitcast.10, s32[2,8,512,512]{3,2,1,0:T(8,128)} %counts.7), custom_call_target="tpu_custom_call" | custom-call | flops 3000000000 | bytes 4194304 | tf_op jit(solution)/shard_map/count_factors/pallas_call | solution.py:29
  14.9 2.1 %collective-permute-start.6 = (bf16[136,512]{1,0:T(8,128)(2,1)S(1)}, bf16[136,512]{1,0:T(8,128)(2,1)S(1)}, u32[]{:S(2)}, u32[]{:S(2)}) collective-permute-start(bf16[136,512]{1,0:T(8,128)(2,1)S(1)} %collective-permute-done.3.refs_0_), channel_id=1, source_target_pairs={{0,96},{1,13},{2,98},{3,15},{4,100},{5,1},{6,102},{7,3},{8,104},{9... | collective-permute-start | bytes 417800 | tf_op jit(solution)/shard_map/ppermute | solution.py:417
  16.9 1.4 %collective-permute-start.5 = (bf16[136,512]{1,0:T(8,128)(2,1)S(1)}, bf16[136,512]{1,0:T(8,128)(2,1)S(1)}, u32[]{:S(2)}, u32[]{:S(2)}) collective-permute-start(bf16[136,512]{1,0:T(8,128)(2,1)S(1)} %collective-permute-done.3.refs_0_), channel_id=1, source_target_pairs={{0,64},{1,9},{2,66},{3,11},{4,68},{5,13},{6,70},{7,15},{8,72},{9,1... | collective-permute-start | bytes 417800 | tf_op jit(solution)/shard_map/ppermute | solution.py:417
  18.3 4.3 %count_factors.5 = (f32[2,2,256,512]{3,2,1,0:T(8,128)S(1)}, f32[2,2,256,512]{3,2,1,0:T(8,128)S(1)}, bf16[2,2,256,512]{3,2,1,0:T(8,128)(2,1)S(1)}, f32[8,128]{1,0:T(8,128)S(1)}) custom-call(s32[2,8]{1,0:T(2,128)S(1)} %bitcast.7, s32[2,8]{1,0:T(2,128)S(1)} %bitcast.11, s32[2,8,512,512]{3,2,1,0:T(8,128)} %counts.7), custom_call_target="tpu_custom_call" | custom-call | flops 3000000000 | bytes 4194304 | tf_op jit(solution)/shard_map/count_factors/pallas_call | solution.py:29
  22.7 1.9 %collective-permute-start.7 = (bf16[4,136,512]{2,1,0:T(8,128)(2,1)S(1)}, bf16[4,136,512]{2,1,0:T(8,128)(2,1)S(1)}, u32[]{:S(2)}, u32[]{:S(2)}) collective-permute-start(bf16[4,136,512]{2,1,0:T(8,128)(2,1)S(1)} %in_ring_order.4.own_a), channel_id=1, source_target_pairs={{0,1},{1,0},{2,3},{3,2},{4,5},{5,4},{6,7},{7,6},{8,9},{9,8},{10,11... | collective-permute-start | bytes 1671176 | tf_op jit(solution)/shard_map/ppermute | solution.py:411
  24.7 1.9 %collective-permute-start.8 = (bf16[4,136,512]{2,1,0:T(8,128)(2,1)S(1)}, bf16[4,136,512]{2,1,0:T(8,128)(2,1)S(1)}, u32[]{:S(2)}, u32[]{:S(2)}) collective-permute-start(bf16[4,136,512]{2,1,0:T(8,128)(2,1)S(1)} %in_ring_order.5.own_b), channel_id=1, source_target_pairs={{0,1},{1,0},{2,3},{3,2},{4,5},{5,4},{6,7},{7,6},{8,9},{9,8},{10,11... | collective-permute-start | bytes 1671176 | tf_op jit(solution)/shard_map/ppermute | solution.py:411
  26.6 0.9 log_marginals.1
  27.5 0.6 collective-permute-done.8.other_b
  28.2 3.7 %cell_grads.2 = (bf16[8,128,512]{2,1,0:T(8,128)(2,1)S(1)}, bf16[8,128,512]{2,1,0:T(8,128)(2,1)S(1)}, bf16[2,1024,512]{2,1,0:T(8,128)(2,1)S(1)}, bf16[8,128,512]{2,1,0:T(8,128)(2,1)S(1)}, f32[8,512]{1,0:T(8,128)S(1)}) custom-call(s32[1]{0:T(128)} %bitcast.here, bf16[4,136,512]{2,1,0:T(8,128)(2,1)S(1)} %in_ring_order.4.own_a, ...), custom_call_target="tpu_custom_call" | custom-call | flops 3000000000 | bytes 16777216 | tf_op jit(solution)/shard_map/cell_grads/pallas_call | solution.py:29
  32.4 1.3 %own_products.2.keep = f32[8,128,512]{2,1,0:T(8,128)S(1)} custom-call(s32[1]{0:T(128)} %bitcast.here, bf16[8,128,512]{2,1,0:T(8,128)(2,1)S(1)} %get-tuple-element.81.w, bf16[8,128,512]{2,1,0:T(8,128)(2,1)S(1)} %get-tuple-element.82.c, bf16[2,1024,512]{2,1,0:T(8,128)(2,1)S(1)} %get-tuple-element.83.grads), custom_call_target="tpu_custom_call" | custom-call | flops 1000000000 | bytes 8388608 | tf_op jit(solution)/shard_map/own_products/pallas_call | solution.py:29
  33.7 1.0 %collective-permute-done.9.extra = bf16[8,128,512]{2,1,0:T(8,128)(2,1)S(1)} collective-permute-done((bf16[8,128,512]{2,1,0:T(8,128)(2,1)S(1)}, bf16[8,128,512]{2,1,0:T(8,128)(2,1)S(1)}, u32[]{:S(2)}, u32[]{:S(2)}) %collective-permute-start.9) | collective-permute-done | bytes 1048608 | tf_op jit(solution)/shard_map/ppermute | solution.py:411
  34.9 1.4 %collective-permute-start.10 = (bf16[2,128,512]{2,1,0:T(8,128)(2,1)S(1)}, bf16[2,128,512]{2,1,0:T(8,128)(2,1)S(1)}, u32[]{:S(2)}, u32[]{:S(2)}) collective-permute-start(bf16[2,128,512]{2,1,0:T(8,128)(2,1)S(1)} %get-tuple-element.90), channel_id=1, source_target_pairs={{0,32},{1,5},{2,34},{3,7},{4,36},{5,9},{6,38},{7,11},{8,40},{9,13}... | collective-permute-start | bytes 786440 | tf_op jit(solution)/shard_map/ppermute | solution.py:417
  36.3 2.6 %collective-permute-start.11 = (bf16[2,128,512]{2,1,0:T(8,128)(2,1)S(1)}, bf16[2,128,512]{2,1,0:T(8,128)(2,1)S(1)}, u32[]{:S(2)}, u32[]{:S(2)}) collective-permute-start(bf16[2,128,512]{2,1,0:T(8,128)(2,1)S(1)} %get-tuple-element.91), channel_id=1, source_target_pairs={{0,64},{1,9},{2,66},{3,11},{4,68},{5,13},{6,70},{7,15},{8,72},{9,1... | collective-permute-start | bytes 786440 | tf_op jit(solution)/shard_map/ppermute | solution.py:417
  38.9 1.1 %collective-permute-start.12 = (bf16[2,128,512]{2,1,0:T(8,128)(2,1)S(1)}, bf16[2,128,512]{2,1,0:T(8,128)(2,1)S(1)}, u32[]{:S(2)}, u32[]{:S(2)}) collective-permute-start(bf16[2,128,512]{2,1,0:T(8,128)(2,1)S(1)} %get-tuple-element.92), channel_id=1, source_target_pairs={{0,96},{1,13},{2,98},{3,15},{4,100},{5,1},{6,102},{7,3},{8,104},{9... | collective-permute-start | bytes 786440 | tf_op jit(solution)/shard_map/ppermute | solution.py:417
  40.0 4.3 %count_factors.6 = (f32[2,2,256,512]{3,2,1,0:T(8,128)S(1)}, f32[2,2,256,512]{3,2,1,0:T(8,128)S(1)}, bf16[2,2,256,512]{3,2,1,0:T(8,128)(2,1)S(1)}, f32[8,128]{1,0:T(8,128)S(1)}) custom-call(s32[2,8]{1,0:T(2,128)S(1)} %bitcast.8, s32[2,8]{1,0:T(2,128)S(1)} %bitcast.12, s32[2,8,512,512]{3,2,1,0:T(8,128)} %counts.7), custom_call_target="tpu_custom_call" | custom-call | flops 3000000000 | bytes 4194304 | tf_op jit(solution)/shard_map/count_factors/pallas_call | solution.py:29
  44.3 1.4 %collective-permute-done.11.refs_2_ = bf16[2,128,512]{2,1,0:T(8,128)(2,1)S(1)} collective-permute-done((bf16[2,128,512]{2,1,0:T(8,128)(2,1)S(1)}, bf16[2,128,512]{2,1,0:T(8,128)(2,1)S(1)}, u32[]{:S(2)}, u32[]{:S(2)}) %collective-permute-start.11) | collective-permute-done | bytes 262176 | tf_op jit(solution)/shard_map/ppermute | solution.py:417
  45.8 2.5 %collective-permute-start.13 = (bf16[128,512]{1,0:T(8,128)(2,1)S(1)}, bf16[128,512]{1,0:T(8,128)(2,1)S(1)}, u32[]{:S(2)}, u32[]{:S(2)}) collective-permute-start(bf16[128,512]{1,0:T(8,128)(2,1)S(1)} %get-tuple-element.97), channel_id=1, source_target_pairs={{0,16},{1,3},{2,18},{3,1},{4,20},{5,7},{6,22},{7,5},{8,24},{9,11},... | collective-permute-start | bytes 393224 | tf_op jit(solution)/shard_map/ppermute | solution.py:414
  48.3 2.9 %collective-permute-done.13.theirs = bf16[128,512]{1,0:T(8,128)(2,1)S(1)} collective-permute-done((bf16[128,512]{1,0:T(8,128)(2,1)S(1)}, bf16[128,512]{1,0:T(8,128)(2,1)S(1)}, u32[]{:S(2)}, u32[]{:S(2)}) %collective-permute-start.13) | collective-permute-done | bytes 131104 | tf_op jit(solution)/shard_map/ppermute | solution.py:414
  51.3 3.2 %collective-permute-start.17 = (bf16[128,512]{1,0:T(8,128)(2,1)S(1)}, bf16[128,512]{1,0:T(8,128)(2,1)S(1)}, u32[]{:S(2)}, u32[]{:S(2)}) collective-permute-start(bf16[128,512]{1,0:T(8,128)(2,1)S(1)} %get-tuple-element.100.refs_0_), channel_id=1, source_target_pairs={{0,16},{1,3},{2,18},{3,1},{4,20},{5,7},{6,22},{7,5},{8,24},{9,11},... | collective-permute-start | bytes 393224 | tf_op jit(solution)/shard_map/ppermute | solution.py:414
  54.5 2.7 %collective-permute-start.16 = (bf16[128,512]{1,0:T(8,128)(2,1)S(1)}, bf16[128,512]{1,0:T(8,128)(2,1)S(1)}, u32[]{:S(2)}, u32[]{:S(2)}) collective-permute-start(bf16[128,512]{1,0:T(8,128)(2,1)S(1)} %get-tuple-element.100.refs_0_), channel_id=1, source_target_pairs={{0,96},{1,13},{2,98},{3,15},{4,100},{5,1},{6,102},{7,3},{8,104},{9... | collective-permute-start | bytes 393224 | tf_op jit(solution)/shard_map/ppermute | solution.py:417
  57.6 0.7 collective-permute-start.14
  58.3 2.0 %collective-permute-start.20 = (bf16[128,512]{1,0:T(8,128)(2,1)S(1)}, bf16[128,512]{1,0:T(8,128)(2,1)S(1)}, u32[]{:S(2)}, u32[]{:S(2)}) collective-permute-start(bf16[128,512]{1,0:T(8,128)(2,1)S(1)} %collective-permute-done.17.refs_0_), channel_id=1, source_target_pairs={{0,96},{1,13},{2,98},{3,15},{4,100},{5,1},{6,102},{7,3},{8,104},{9... | collective-permute-start | bytes 393224 | tf_op jit(solution)/shard_map/ppermute | solution.py:417
  60.2 1.4 %collective-permute-start.19 = (bf16[128,512]{1,0:T(8,128)(2,1)S(1)}, bf16[128,512]{1,0:T(8,128)(2,1)S(1)}, u32[]{:S(2)}, u32[]{:S(2)}) collective-permute-start(bf16[128,512]{1,0:T(8,128)(2,1)S(1)} %collective-permute-done.17.refs_0_), channel_id=1, source_target_pairs={{0,64},{1,9},{2,66},{3,11},{4,68},{5,13},{6,70},{7,15},{8,72},{9,1... | collective-permute-start | bytes 393224 | tf_op jit(solution)/shard_map/ppermute | solution.py:417
  61.6 4.3 %count_factors.7 = (f32[2,2,256,512]{3,2,1,0:T(8,128)S(1)}, f32[2,2,256,512]{3,2,1,0:T(8,128)S(1)}, bf16[2,2,256,512]{3,2,1,0:T(8,128)(2,1)S(1)}, f32[8,128]{1,0:T(8,128)S(1)}) custom-call(s32[2,8]{1,0:T(2,128)S(1)} %bitcast.9, s32[2,8]{1,0:T(2,128)S(1)} %bitcast.13, s32[2,8,512,512]{3,2,1,0:T(8,128)} %counts.7), custom_call_target="tpu_custom_call" | custom-call | flops 3000000000 | bytes 4194304 | tf_op jit(solution)/shard_map/count_factors/pallas_call | solution.py:29
  66.0 0.6 collective-permute-start.21
  66.6 0.7 collective-permute-done.18.refs_1_
  67.3 1.1 %collective-permute-start.22 = (bf16[4,128,512]{2,1,0:T(8,128)(2,1)S(1)}, bf16[4,128,512]{2,1,0:T(8,128)(2,1)S(1)}, u32[]{:S(2)}, u32[]{:S(2)}) collective-permute-start(bf16[4,128,512]{2,1,0:T(8,128)(2,1)S(1)} %in_ring_order.7.own_b), channel_id=1, source_target_pairs={{0,1},{1,0},{2,3},{3,2},{4,5},{5,4},{6,7},{7,6},{8,9},{9,8},{10,11... | collective-permute-start | bytes 1572872 | tf_op jit(solution)/shard_map/ppermute | solution.py:411
  68.4 1.5 %collective-permute-done.22.other_b = bf16[4,128,512]{2,1,0:T(8,128)(2,1)S(1)} collective-permute-done((bf16[4,128,512]{2,1,0:T(8,128)(2,1)S(1)}, bf16[4,128,512]{2,1,0:T(8,128)(2,1)S(1)}, u32[]{:S(2)}, u32[]{:S(2)}) %collective-permute-start.22) | collective-permute-done | bytes 524320 | tf_op jit(solution)/shard_map/ppermute | solution.py:411
  70.0 3.6 %cell_grads.3 = (bf16[8,128,512]{2,1,0:T(8,128)(2,1)S(1)}, bf16[8,128,512]{2,1,0:T(8,128)(2,1)S(1)}, bf16[2,1024,512]{2,1,0:T(8,128)(2,1)S(1)}, bf16[8,128,512]{2,1,0:T(8,128)(2,1)S(1)}) custom-call(s32[1]{0:T(128)} %bitcast.here, bf16[4,128,512]{2,1,0:T(8,128)(2,1)S(1)} %in_ring_order.6.own_a, bf16[4,128,512]{2,1,0:T(8,128)(2,1)S(1)} %in_ring_order.7.own_b, ...), custom_call_target="tpu_custom_call" | custom-call | flops 3000000000 | bytes 16777216 | tf_op jit(solution)/shard_map/cell_grads/pallas_call | solution.py:29
  73.6 0.5 collective-permute-start.23
  74.0 1.3 %own_products.3.keep = f32[8,128,512]{2,1,0:T(8,128)S(1)} custom-call(s32[1]{0:T(128)} %bitcast.here, bf16[8,128,512]{2,1,0:T(8,128)(2,1)S(1)} %get-tuple-element.111.w, bf16[8,128,512]{2,1,0:T(8,128)(2,1)S(1)} %get-tuple-element.112.c, bf16[2,1024,512]{2,1,0:T(8,128)(2,1)S(1)} %get-tuple-element.113.grads), custom_call_target="tpu_custom_call" | custom-call | flops 1000000000 | bytes 8388608 | tf_op jit(solution)/shard_map/own_products/pallas_call | solution.py:29
  75.3 1.0 %collective-permute-done.23.extra = bf16[8,128,512]{2,1,0:T(8,128)(2,1)S(1)} collective-permute-done((bf16[8,128,512]{2,1,0:T(8,128)(2,1)S(1)}, bf16[8,128,512]{2,1,0:T(8,128)(2,1)S(1)}, u32[]{:S(2)}, u32[]{:S(2)}) %collective-permute-start.23) | collective-permute-done | bytes 1048608 | tf_op jit(solution)/shard_map/ppermute | solution.py:411
  76.5 1.3 %collective-permute-start.24 = (bf16[2,128,512]{2,1,0:T(8,128)(2,1)S(1)}, bf16[2,128,512]{2,1,0:T(8,128)(2,1)S(1)}, u32[]{:S(2)}, u32[]{:S(2)}) collective-permute-start(bf16[2,128,512]{2,1,0:T(8,128)(2,1)S(1)} %get-tuple-element.116), channel_id=1, source_target_pairs={{0,32},{1,5},{2,34},{3,7},{4,36},{5,9},{6,38},{7,11},{8,40},{9,13}... | collective-permute-start | bytes 786440 | tf_op jit(solution)/shard_map/ppermute | solution.py:417
  77.8 2.1 %collective-permute-start.25 = (bf16[2,128,512]{2,1,0:T(8,128)(2,1)S(1)}, bf16[2,128,512]{2,1,0:T(8,128)(2,1)S(1)}, u32[]{:S(2)}, u32[]{:S(2)}) collective-permute-start(bf16[2,128,512]{2,1,0:T(8,128)(2,1)S(1)} %get-tuple-element.117), channel_id=1, source_target_pairs={{0,64},{1,9},{2,66},{3,11},{4,68},{5,13},{6,70},{7,15},{8,72},{9,1... | collective-permute-start | bytes 786440 | tf_op jit(solution)/shard_map/ppermute | solution.py:417
  79.9 1.3 %collective-permute-start.26 = (bf16[2,128,512]{2,1,0:T(8,128)(2,1)S(1)}, bf16[2,128,512]{2,1,0:T(8,128)(2,1)S(1)}, u32[]{:S(2)}, u32[]{:S(2)}) collective-permute-start(bf16[2,128,512]{2,1,0:T(8,128)(2,1)S(1)} %get-tuple-element.118), channel_id=1, source_target_pairs={{0,96},{1,13},{2,98},{3,15},{4,100},{5,1},{6,102},{7,3},{8,104},{9... | collective-permute-start | bytes 786440 | tf_op jit(solution)/shard_map/ppermute | solution.py:417
  81.2 2.1 %collective-permute-done.24.refs_1_ = bf16[2,128,512]{2,1,0:T(8,128)(2,1)S(1)} collective-permute-done((bf16[2,128,512]{2,1,0:T(8,128)(2,1)S(1)}, bf16[2,128,512]{2,1,0:T(8,128)(2,1)S(1)}, u32[]{:S(2)}, u32[]{:S(2)}) %collective-permute-start.24) | collective-permute-done | bytes 262176 | tf_op jit(solution)/shard_map/ppermute | solution.py:417
  83.3 3.5 %collective-permute-done.25.refs_2_ = bf16[2,128,512]{2,1,0:T(8,128)(2,1)S(1)} collective-permute-done((bf16[2,128,512]{2,1,0:T(8,128)(2,1)S(1)}, bf16[2,128,512]{2,1,0:T(8,128)(2,1)S(1)}, u32[]{:S(2)}, u32[]{:S(2)}) %collective-permute-start.25) | collective-permute-done | bytes 262176 | tf_op jit(solution)/shard_map/ppermute | solution.py:417
  86.9 2.3 %collective-permute-start.27 = (bf16[128,512]{1,0:T(8,128)(2,1)S(1)}, bf16[128,512]{1,0:T(8,128)(2,1)S(1)}, u32[]{:S(2)}, u32[]{:S(2)}) collective-permute-start(bf16[128,512]{1,0:T(8,128)(2,1)S(1)} %get-tuple-element.120), channel_id=1, source_target_pairs={{0,16},{1,3},{2,18},{3,1},{4,20},{5,7},{6,22},{7,5},{8,24},{9,11},... | collective-permute-start | bytes 393224 | tf_op jit(solution)/shard_map/ppermute | solution.py:414
  89.2 3.1 %collective-permute-done.27.theirs = bf16[128,512]{1,0:T(8,128)(2,1)S(1)} collective-permute-done((bf16[128,512]{1,0:T(8,128)(2,1)S(1)}, bf16[128,512]{1,0:T(8,128)(2,1)S(1)}, u32[]{:S(2)}, u32[]{:S(2)}) %collective-permute-start.27) | collective-permute-done | bytes 131104 | tf_op jit(solution)/shard_map/ppermute | solution.py:414
  92.3 1.4 %collective-permute-start.28 = (f32[128,512]{1,0:T(8,128)S(1)}, f32[128,512]{1,0:T(8,128)S(1)}, u32[]{:S(2)}, u32[]{:S(2)}) collective-permute-start(f32[128,512]{1,0:T(8,128)S(1)} %update.3.embed), channel_id=1, source_target_pairs={{0,1},{1,0},{2,3},{3,2},{4,5},{5,4},{6,7},{7,6},{8,9},{9,8},{10,11... | collective-permute-start | bytes 786440 | tf_op jit(solution)/shard_map/ppermute | solution.py:411
  93.7 1.2 %collective-permute-done.28.theirs = f32[128,512]{1,0:T(8,128)S(1)} collective-permute-done((f32[128,512]{1,0:T(8,128)S(1)}, f32[128,512]{1,0:T(8,128)S(1)}, u32[]{:S(2)}, u32[]{:S(2)}) %collective-permute-start.28) | collective-permute-done | bytes 262176 | tf_op jit(solution)/shard_map/ppermute | solution.py:411
  94.9 0.8 results.1
  (39 shorter events, 2.2 us)
Async XLA Ops:
  1.8 16.6 %copy-start.3 = (s32[2,8,1,1]{1,3,2,0:T(1,128)S(1)}, s32[2,8,1,1]{1,3,2,0:T(1,128)}, u32[]{:S(2)}) copy-start(s32[2,8,1,1]{1,3,2,0:T(1,128)} %param.11) | copy-start | bytes 196
  1.8 13.1 %collective-permute-start.3 = (bf16[136,512]{1,0:T(8,128)(2,1)S(1)}, bf16[136,512]{1,0:T(8,128)(2,1)S(1)}, u32[]{:S(2)}, u32[]{:S(2)}) collective-permute-start(bf16[136,512]{1,0:T(8,128)(2,1)S(1)} %get-tuple-element.66.refs_0_), channel_id=1, source_target_pairs={{0,16},{1,3},{2,18},{3,1},{4,20},{5,7},{6,22},{7,5},{8,24},{9,11},... | collective-permute-start | bytes 417800 | tf_op jit(solution)/shard_map/ppermute | solution.py:414
  5.4 12.9 %collective-permute-start.2 = (bf16[136,512]{1,0:T(8,128)(2,1)S(1)}, bf16[136,512]{1,0:T(8,128)(2,1)S(1)}, u32[]{:S(2)}, u32[]{:S(2)}) collective-permute-start(bf16[136,512]{1,0:T(8,128)(2,1)S(1)} %get-tuple-element.66.refs_0_), channel_id=1, source_target_pairs={{0,96},{1,13},{2,98},{3,15},{4,100},{5,1},{6,102},{7,3},{8,104},{9... | collective-permute-start | bytes 417800 | tf_op jit(solution)/shard_map/ppermute | solution.py:417
  8.2 14.4 %collective-permute-start.1 = (bf16[136,512]{1,0:T(8,128)(2,1)S(1)}, bf16[136,512]{1,0:T(8,128)(2,1)S(1)}, u32[]{:S(2)}, u32[]{:S(2)}) collective-permute-start(bf16[136,512]{1,0:T(8,128)(2,1)S(1)} %get-tuple-element.66.refs_0_), channel_id=1, source_target_pairs={{0,64},{1,9},{2,66},{3,11},{4,68},{5,13},{6,70},{7,15},{8,72},{9,1... | collective-permute-start | bytes 417800 | tf_op jit(solution)/shard_map/ppermute | solution.py:417
  8.5 14.1 %collective-permute-start = (bf16[136,512]{1,0:T(8,128)(2,1)S(1)}, bf16[136,512]{1,0:T(8,128)(2,1)S(1)}, u32[]{:S(2)}, u32[]{:S(2)}) collective-permute-start(bf16[136,512]{1,0:T(8,128)(2,1)S(1)} %get-tuple-element.66.refs_0_), channel_id=1, source_target_pairs={{0,32},{1,5},{2,34},{3,7},{4,36},{5,9},{6,38},{7,11},{8,40},{9,13}... | collective-permute-start | bytes 417800 | tf_op jit(solution)/shard_map/ppermute | solution.py:417
  9.2 0.7 copy-start
  9.9 0.7 copy-start.2
  14.9 9.8 %collective-permute-start.6 = (bf16[136,512]{1,0:T(8,128)(2,1)S(1)}, bf16[136,512]{1,0:T(8,128)(2,1)S(1)}, u32[]{:S(2)}, u32[]{:S(2)}) collective-permute-start(bf16[136,512]{1,0:T(8,128)(2,1)S(1)} %collective-permute-done.3.refs_0_), channel_id=1, source_target_pairs={{0,96},{1,13},{2,98},{3,15},{4,100},{5,1},{6,102},{7,3},{8,104},{9... | collective-permute-start | bytes 417800 | tf_op jit(solution)/shard_map/ppermute | solution.py:417
  16.9 7.7 %collective-permute-start.5 = (bf16[136,512]{1,0:T(8,128)(2,1)S(1)}, bf16[136,512]{1,0:T(8,128)(2,1)S(1)}, u32[]{:S(2)}, u32[]{:S(2)}) collective-permute-start(bf16[136,512]{1,0:T(8,128)(2,1)S(1)} %collective-permute-done.3.refs_0_), channel_id=1, source_target_pairs={{0,64},{1,9},{2,66},{3,11},{4,68},{5,13},{6,70},{7,15},{8,72},{9,1... | collective-permute-start | bytes 417800 | tf_op jit(solution)/shard_map/ppermute | solution.py:417
  18.3 6.3 %collective-permute-start.4 = (bf16[136,512]{1,0:T(8,128)(2,1)S(1)}, bf16[136,512]{1,0:T(8,128)(2,1)S(1)}, u32[]{:S(2)}, u32[]{:S(2)}) collective-permute-start(bf16[136,512]{1,0:T(8,128)(2,1)S(1)} %collective-permute-done.3.refs_0_), channel_id=1, source_target_pairs={{0,32},{1,5},{2,34},{3,7},{4,36},{5,9},{6,38},{7,11},{8,40},{9,13}... | collective-permute-start | bytes 417800 | tf_op jit(solution)/shard_map/ppermute | solution.py:417
  22.7 4.8 %collective-permute-start.7 = (bf16[4,136,512]{2,1,0:T(8,128)(2,1)S(1)}, bf16[4,136,512]{2,1,0:T(8,128)(2,1)S(1)}, u32[]{:S(2)}, u32[]{:S(2)}) collective-permute-start(bf16[4,136,512]{2,1,0:T(8,128)(2,1)S(1)} %in_ring_order.4.own_a), channel_id=1, source_target_pairs={{0,1},{1,0},{2,3},{3,2},{4,5},{5,4},{6,7},{7,6},{8,9},{9,8},{10,11... | collective-permute-start | bytes 1671176 | tf_op jit(solution)/shard_map/ppermute | solution.py:411
  24.7 3.5 %collective-permute-start.8 = (bf16[4,136,512]{2,1,0:T(8,128)(2,1)S(1)}, bf16[4,136,512]{2,1,0:T(8,128)(2,1)S(1)}, u32[]{:S(2)}, u32[]{:S(2)}) collective-permute-start(bf16[4,136,512]{2,1,0:T(8,128)(2,1)S(1)} %in_ring_order.5.own_b), channel_id=1, source_target_pairs={{0,1},{1,0},{2,3},{3,2},{4,5},{5,4},{6,7},{7,6},{8,9},{9,8},{10,11... | collective-permute-start | bytes 1671176 | tf_op jit(solution)/shard_map/ppermute | solution.py:411
  31.9 2.7 %collective-permute-start.9 = (bf16[8,128,512]{2,1,0:T(8,128)(2,1)S(1)}, bf16[8,128,512]{2,1,0:T(8,128)(2,1)S(1)}, u32[]{:S(2)}, u32[]{:S(2)}) collective-permute-start(bf16[8,128,512]{2,1,0:T(8,128)(2,1)S(1)} %get-tuple-element.84), channel_id=1, source_target_pairs={{0,1},{1,0},{2,3},{3,2},{4,5},{5,4},{6,7},{7,6},{8,9},{9,8},{10,11... | collective-permute-start | bytes 3145736 | tf_op jit(solution)/shard_map/ppermute | solution.py:411
  33.6 6.4 %copy-start.1 = (s32[2,8,1,1]{1,3,2,0:T(1,128)S(1)}, s32[2,8,1,1]{1,3,2,0:T(1,128)}, u32[]{:S(2)}) copy-start(s32[2,8,1,1]{1,3,2,0:T(1,128)} %param.10) | copy-start | bytes 196
  34.9 9.4 %collective-permute-start.10 = (bf16[2,128,512]{2,1,0:T(8,128)(2,1)S(1)}, bf16[2,128,512]{2,1,0:T(8,128)(2,1)S(1)}, u32[]{:S(2)}, u32[]{:S(2)}) collective-permute-start(bf16[2,128,512]{2,1,0:T(8,128)(2,1)S(1)} %get-tuple-element.90), channel_id=1, source_target_pairs={{0,32},{1,5},{2,34},{3,7},{4,36},{5,9},{6,38},{7,11},{8,40},{9,13}... | collective-permute-start | bytes 786440 | tf_op jit(solution)/shard_map/ppermute | solution.py:417
  36.3 9.4 %collective-permute-start.11 = (bf16[2,128,512]{2,1,0:T(8,128)(2,1)S(1)}, bf16[2,128,512]{2,1,0:T(8,128)(2,1)S(1)}, u32[]{:S(2)}, u32[]{:S(2)}) collective-permute-start(bf16[2,128,512]{2,1,0:T(8,128)(2,1)S(1)} %get-tuple-element.91), channel_id=1, source_target_pairs={{0,64},{1,9},{2,66},{3,11},{4,68},{5,13},{6,70},{7,15},{8,72},{9,1... | collective-permute-start | bytes 786440 | tf_op jit(solution)/shard_map/ppermute | solution.py:417
  38.9 6.8 %collective-permute-start.12 = (bf16[2,128,512]{2,1,0:T(8,128)(2,1)S(1)}, bf16[2,128,512]{2,1,0:T(8,128)(2,1)S(1)}, u32[]{:S(2)}, u32[]{:S(2)}) collective-permute-start(bf16[2,128,512]{2,1,0:T(8,128)(2,1)S(1)} %get-tuple-element.92), channel_id=1, source_target_pairs={{0,96},{1,13},{2,98},{3,15},{4,100},{5,1},{6,102},{7,3},{8,104},{9... | collective-permute-start | bytes 786440 | tf_op jit(solution)/shard_map/ppermute | solution.py:417
  45.8 5.4 %collective-permute-start.13 = (bf16[128,512]{1,0:T(8,128)(2,1)S(1)}, bf16[128,512]{1,0:T(8,128)(2,1)S(1)}, u32[]{:S(2)}, u32[]{:S(2)}) collective-permute-start(bf16[128,512]{1,0:T(8,128)(2,1)S(1)} %get-tuple-element.97), channel_id=1, source_target_pairs={{0,16},{1,3},{2,18},{3,1},{4,20},{5,7},{6,22},{7,5},{8,24},{9,11},... | collective-permute-start | bytes 393224 | tf_op jit(solution)/shard_map/ppermute | solution.py:414
  51.3 7.0 %collective-permute-start.17 = (bf16[128,512]{1,0:T(8,128)(2,1)S(1)}, bf16[128,512]{1,0:T(8,128)(2,1)S(1)}, u32[]{:S(2)}, u32[]{:S(2)}) collective-permute-start(bf16[128,512]{1,0:T(8,128)(2,1)S(1)} %get-tuple-element.100.refs_0_), channel_id=1, source_target_pairs={{0,16},{1,3},{2,18},{3,1},{4,20},{5,7},{6,22},{7,5},{8,24},{9,11},... | collective-permute-start | bytes 393224 | tf_op jit(solution)/shard_map/ppermute | solution.py:414
  54.5 7.2 %collective-permute-start.16 = (bf16[128,512]{1,0:T(8,128)(2,1)S(1)}, bf16[128,512]{1,0:T(8,128)(2,1)S(1)}, u32[]{:S(2)}, u32[]{:S(2)}) collective-permute-start(bf16[128,512]{1,0:T(8,128)(2,1)S(1)} %get-tuple-element.100.refs_0_), channel_id=1, source_target_pairs={{0,96},{1,13},{2,98},{3,15},{4,100},{5,1},{6,102},{7,3},{8,104},{9... | collective-permute-start | bytes 393224 | tf_op jit(solution)/shard_map/ppermute | solution.py:417
  57.2 8.8 %collective-permute-start.15 = (bf16[128,512]{1,0:T(8,128)(2,1)S(1)}, bf16[128,512]{1,0:T(8,128)(2,1)S(1)}, u32[]{:S(2)}, u32[]{:S(2)}) collective-permute-start(bf16[128,512]{1,0:T(8,128)(2,1)S(1)} %get-tuple-element.100.refs_0_), channel_id=1, source_target_pairs={{0,64},{1,9},{2,66},{3,11},{4,68},{5,13},{6,70},{7,15},{8,72},{9,1... | collective-permute-start | bytes 393224 | tf_op jit(solution)/shard_map/ppermute | solution.py:417
  57.6 8.4 %collective-permute-start.14 = (bf16[128,512]{1,0:T(8,128)(2,1)S(1)}, bf16[128,512]{1,0:T(8,128)(2,1)S(1)}, u32[]{:S(2)}, u32[]{:S(2)}) collective-permute-start(bf16[128,512]{1,0:T(8,128)(2,1)S(1)} %get-tuple-element.100.refs_0_), channel_id=1, source_target_pairs={{0,32},{1,5},{2,34},{3,7},{4,36},{5,9},{6,38},{7,11},{8,40},{9,13}... | collective-permute-start | bytes 393224 | tf_op jit(solution)/shard_map/ppermute | solution.py:417
  58.3 8.3 %collective-permute-start.20 = (bf16[128,512]{1,0:T(8,128)(2,1)S(1)}, bf16[128,512]{1,0:T(8,128)(2,1)S(1)}, u32[]{:S(2)}, u32[]{:S(2)}) collective-permute-start(bf16[128,512]{1,0:T(8,128)(2,1)S(1)} %collective-permute-done.17.refs_0_), channel_id=1, source_target_pairs={{0,96},{1,13},{2,98},{3,15},{4,100},{5,1},{6,102},{7,3},{8,104},{9... | collective-permute-start | bytes 393224 | tf_op jit(solution)/shard_map/ppermute | solution.py:417
  60.2 6.4 %collective-permute-start.19 = (bf16[128,512]{1,0:T(8,128)(2,1)S(1)}, bf16[128,512]{1,0:T(8,128)(2,1)S(1)}, u32[]{:S(2)}, u32[]{:S(2)}) collective-permute-start(bf16[128,512]{1,0:T(8,128)(2,1)S(1)} %collective-permute-done.17.refs_0_), channel_id=1, source_target_pairs={{0,64},{1,9},{2,66},{3,11},{4,68},{5,13},{6,70},{7,15},{8,72},{9,1... | collective-permute-start | bytes 393224 | tf_op jit(solution)/shard_map/ppermute | solution.py:417
  61.6 5.6 %collective-permute-start.18 = (bf16[128,512]{1,0:T(8,128)(2,1)S(1)}, bf16[128,512]{1,0:T(8,128)(2,1)S(1)}, u32[]{:S(2)}, u32[]{:S(2)}) collective-permute-start(bf16[128,512]{1,0:T(8,128)(2,1)S(1)} %collective-permute-done.17.refs_0_), channel_id=1, source_target_pairs={{0,32},{1,5},{2,34},{3,7},{4,36},{5,9},{6,38},{7,11},{8,40},{9,13}... | collective-permute-start | bytes 393224 | tf_op jit(solution)/shard_map/ppermute | solution.py:417
  66.0 2.4 %collective-permute-start.21 = (bf16[4,128,512]{2,1,0:T(8,128)(2,1)S(1)}, bf16[4,128,512]{2,1,0:T(8,128)(2,1)S(1)}, u32[]{:S(2)}, u32[]{:S(2)}) collective-permute-start(bf16[4,128,512]{2,1,0:T(8,128)(2,1)S(1)} %in_ring_order.6.own_a), channel_id=1, source_target_pairs={{0,1},{1,0},{2,3},{3,2},{4,5},{5,4},{6,7},{7,6},{8,9},{9,8},{10,11... | collective-permute-start | bytes 1572872 | tf_op jit(solution)/shard_map/ppermute | solution.py:411
  67.3 2.7 %collective-permute-start.22 = (bf16[4,128,512]{2,1,0:T(8,128)(2,1)S(1)}, bf16[4,128,512]{2,1,0:T(8,128)(2,1)S(1)}, u32[]{:S(2)}, u32[]{:S(2)}) collective-permute-start(bf16[4,128,512]{2,1,0:T(8,128)(2,1)S(1)} %in_ring_order.7.own_b), channel_id=1, source_target_pairs={{0,1},{1,0},{2,3},{3,2},{4,5},{5,4},{6,7},{7,6},{8,9},{9,8},{10,11... | collective-permute-start | bytes 1572872 | tf_op jit(solution)/shard_map/ppermute | solution.py:411
  73.6 2.7 %collective-permute-start.23 = (bf16[8,128,512]{2,1,0:T(8,128)(2,1)S(1)}, bf16[8,128,512]{2,1,0:T(8,128)(2,1)S(1)}, u32[]{:S(2)}, u32[]{:S(2)}) collective-permute-start(bf16[8,128,512]{2,1,0:T(8,128)(2,1)S(1)} %get-tuple-element.114), channel_id=1, source_target_pairs={{0,1},{1,0},{2,3},{3,2},{4,5},{5,4},{6,7},{7,6},{8,9},{9,8},{10,11... | collective-permute-start | bytes 3145736 | tf_op jit(solution)/shard_map/ppermute | solution.py:411
  76.5 6.8 %collective-permute-start.24 = (bf16[2,128,512]{2,1,0:T(8,128)(2,1)S(1)}, bf16[2,128,512]{2,1,0:T(8,128)(2,1)S(1)}, u32[]{:S(2)}, u32[]{:S(2)}) collective-permute-start(bf16[2,128,512]{2,1,0:T(8,128)(2,1)S(1)} %get-tuple-element.116), channel_id=1, source_target_pairs={{0,32},{1,5},{2,34},{3,7},{4,36},{5,9},{6,38},{7,11},{8,40},{9,13}... | collective-permute-start | bytes 786440 | tf_op jit(solution)/shard_map/ppermute | solution.py:417
  77.8 9.0 %collective-permute-start.25 = (bf16[2,128,512]{2,1,0:T(8,128)(2,1)S(1)}, bf16[2,128,512]{2,1,0:T(8,128)(2,1)S(1)}, u32[]{:S(2)}, u32[]{:S(2)}) collective-permute-start(bf16[2,128,512]{2,1,0:T(8,128)(2,1)S(1)} %get-tuple-element.117), channel_id=1, source_target_pairs={{0,64},{1,9},{2,66},{3,11},{4,68},{5,13},{6,70},{7,15},{8,72},{9,1... | collective-permute-start | bytes 786440 | tf_op jit(solution)/shard_map/ppermute | solution.py:417
  79.9 6.9 %collective-permute-start.26 = (bf16[2,128,512]{2,1,0:T(8,128)(2,1)S(1)}, bf16[2,128,512]{2,1,0:T(8,128)(2,1)S(1)}, u32[]{:S(2)}, u32[]{:S(2)}) collective-permute-start(bf16[2,128,512]{2,1,0:T(8,128)(2,1)S(1)} %get-tuple-element.118), channel_id=1, source_target_pairs={{0,96},{1,13},{2,98},{3,15},{4,100},{5,1},{6,102},{7,3},{8,104},{9... | collective-permute-start | bytes 786440 | tf_op jit(solution)/shard_map/ppermute | solution.py:417
  86.9 5.4 %collective-permute-start.27 = (bf16[128,512]{1,0:T(8,128)(2,1)S(1)}, bf16[128,512]{1,0:T(8,128)(2,1)S(1)}, u32[]{:S(2)}, u32[]{:S(2)}) collective-permute-start(bf16[128,512]{1,0:T(8,128)(2,1)S(1)} %get-tuple-element.120), channel_id=1, source_target_pairs={{0,16},{1,3},{2,18},{3,1},{4,20},{5,7},{6,22},{7,5},{8,24},{9,11},... | collective-permute-start | bytes 393224 | tf_op jit(solution)/shard_map/ppermute | solution.py:414
  92.3 2.6 %collective-permute-start.28 = (f32[128,512]{1,0:T(8,128)S(1)}, f32[128,512]{1,0:T(8,128)S(1)}, u32[]{:S(2)}, u32[]{:S(2)}) collective-permute-start(f32[128,512]{1,0:T(8,128)S(1)} %update.3.embed), channel_id=1, source_target_pairs={{0,1},{1,0},{2,3},{3,2},{4,5},{5,4},{6,7},{7,6},{8,9},{9,8},{10,11... | collective-permute-start | bytes 786440 | tf_op jit(solution)/shard_map/ppermute | solution.py:411

commit v4 on v3

--- a/solution.py
+++ b/solution.py
@@ -12,7 +12,7 @@
 F32 = jnp.float32
 BF16 = jnp.bfloat16
 W_ROLE = 1
-PIECE = 64
+PIECE = 32
 STRIP = 16
 NT = (((1,), (1,)), ((), ()))
 TN = (((0,), (0,)), ((), ()))
@@ -47,23 +47,32 @@
     return [jnp.where(role == W_ROLE, p, q) for p, q in zip(of_w, of_c)]
 
 
-def abn_kernel(step, half, rows, cols, counts, a, b, n, done, held, seen, sem):
+def abn_kernel(step, half, rows_in, cols_in, counts, after, a, b, n, done, rows, cols, held, seen, sem):
     slots, extent = counts.shape[1], counts.shape[2] // 2
 
     def piece(i):
         part = pl.ds(half * extent + i * PIECE, PIECE)
         return pltpu.make_async_copy(counts.at[step, :, part, :], held.at[i], sem.at[i])
 
-    for i in range(extent // PIECE):
+    pieces = extent // PIECE
+    indices = [
+        pltpu.make_async_copy(rows_in.at[step], rows, sem.at[pieces]),
+        pltpu.make_async_copy(cols_in.at[step], cols, sem.at[pieces + 1]),
+    ]
+    for copy in indices:
+        copy.start()
+    for i in range(pieces):
         piece(i).start()
     for ref in (a, b, done, seen):
         ref[...] = jnp.zeros(ref.shape, F32)
+    for copy in indices:
+        copy.wait()
     sampled = {}
     for g in range(2):
         for h in range(2):
             total = jnp.int32(0)
             for slot in range(slots):
-                total += ((rows[step, slot] == g) & (cols[step, slot] == h)).astype(jnp.int32)
+                total += ((rows[0, slot] == g) & (cols[0, slot] == h)).astype(jnp.int32)
             sampled[g, h] = total.astype(F32)
     for i in range(extent // PIECE):
         piece(i).wait()
@@ -75,7 +84,7 @@
                 xf = held[i, slot, here, :].astype(F32)
                 top = jnp.maximum(xf, 1.0)
                 root = xf * lax.rsqrt(top)
-                at = (rows[step, slot], cols[step, slot], part, slice(None))
+                at = (rows[0, slot], cols[0, slot], part, slice(None))
                 a[at] += root
                 b[at] += (0.1 + 0.25 * root) * jnp.log(top)
                 seen[at] += jnp.minimum(xf, 1.0)
@@ -89,55 +98,56 @@
         lax.fori_loop(0, PIECE // STRIP, strip, 0)
 
 
-def abn(counts, rows, cols, step, half):
+def abn(counts, rows, cols, step, half, after):
     slots, block = counts.shape[1], counts.shape[2]
     shape = (2, 2, block // 2, block)
     pieces = block // 2 // PIECE
     *factors, done = vmem_kernel(
         functools.partial(abn_kernel, step, half),
         8,
-        in_specs=[IN_SMEM, IN_SMEM, IN_HBM],
+        in_specs=[IN_HBM, IN_HBM, IN_HBM, IN_VMEM],
         out_specs=[IN_VMEM] * 4,
         out_shape=[pltpu.VMEM(shape, d) for d in (F32, F32, BF16)] + [pltpu.VMEM((8, 128), F32)],
         scratch_shapes=[
+            pltpu.SMEM((1, slots), jnp.int32),
+            pltpu.SMEM((1, slots), jnp.int32),
             pltpu.VMEM((pieces, slots, PIECE, block), jnp.int32),
             pltpu.VMEM(shape, F32),
-            pltpu.SemaphoreType.DMA((pieces,)),
+            pltpu.SemaphoreType.DMA((pieces + 2,)),
         ],
         cost_estimate=pl.CostEstimate(flops=3 * 10**9, bytes_accessed=4 * 2**20, transcendentals=2 * 2**20),
         name="count_factors",
-    )(rows, cols, counts)
+    )(rows, cols, counts, after)
     return factors, done
 
 
-def front_kernel(first, here, own_a, own_b, other_a, other_b, *refs):
+def front_kernel(first, here, done, *refs):
+    own, other, refs = refs[:4], refs[4:8], refs[8:]
     a, b, n = refs[0:6:3], refs[1:6:3], refs[2:6:3]
     lr, lc, *refs = refs[6:]
     if first:
         w, c, grads, send, log_total = refs
     else:
         log_total, w, c, grads, send = refs
-    role, (_, ws), (_, cs) = place(here)
-
-    def assemble(w_a, w_b, c_a, c_b):
+    role, (w_at, _), (c_at, _) = place(here)
+
+    def assemble(of_w, of_c):
         for k in range(4):
-            w[2 * k + ws] = w_a[k, :128, :]
-            w[2 * k + 1 - ws] = w_b[k, :128, :]
-            c[2 * k + cs] = c_a[k, :128, :]
-            c[2 * k + 1 - cs] = c_b[k, :128, :]
+            w[pl.ds(2 * ((w_at - k) & 3), 2)] = of_w[k][:, :128, :]
+            c[pl.ds(2 * ((c_at - k) & 3), 2)] = of_c[k][:, :128, :]
         if first:
-            pieces = c_a[:, 128:, :].astype(F32) + c_b[:, 128:, :].astype(F32)
-            log_total[...] = jnp.broadcast_to(
-                jnp.log(jnp.sum(pieces, axis=(0, 1), keepdims=False)[None, :]), log_total.shape
-            )
+            pieces = jnp.zeros((8, 512), F32)
+            for k in range(4):
+                pieces += jnp.sum(of_c[k][:, 128:, :].astype(F32), axis=0)
+            log_total[...] = jnp.broadcast_to(jnp.log(jnp.sum(pieces, axis=0, keepdims=True)), log_total.shape)
 
     @pl.when(role == W_ROLE)
     def _():
-        assemble(own_a, own_b, other_a, other_b)
+        assemble(own, other)
 
     @pl.when(role != W_ROLE)
     def _():
-        assemble(other_a, other_b, own_a, own_b)
+        assemble(other, own)
 
     for g in range(2):
         wg = w[4 * g : 4 * g + 4].reshape(512, 512)
@@ -176,9 +186,9 @@
         out[:, h * 64 : h * 64 + 64, :] = total.reshape(8, 64, 512).astype(out.dtype)
 
 
-def front(here, gathered, factors, lr, lc, log_total):
+def front(here, done, gathered, factors, lr, lc, log_total):
     first = log_total is None
-    args = [here, *gathered, *factors, lr, lc] + ([] if first else [log_total])
+    args = [here, done, *gathered, *factors, lr, lc] + ([] if first else [log_total])
     shape = (8, 128, 512)
     out_shape = [pltpu.VMEM(s, BF16) for s in (shape, shape, (2, 1024, 512), shape)]
     if first:
@@ -236,8 +246,8 @@
     )(here, keep, extra)
 
 
-def ring_sum_kernel(here, *refs):
-    *terms, mine, theirs = refs
+def ring_sum_kernel(last, here, *refs):
+    terms, outs = refs[:4], refs[-2:]
     _, side = own_place(here)
 
     def total(s):
@@ -246,89 +256,87 @@
             out += term[s].astype(F32)
         return out
 
-    mine[...] = total(side)
-    theirs[...] = total(1 - side).astype(BF16)
-
-
-def ring_sum(here, terms, *after):
-    return vmem_kernel(
-        ring_sum_kernel,
+    mine, theirs = outs
+    if last:
+        mine[...] = total(side)
+        theirs[...] = total(1 - side).astype(BF16)
+    else:
+        for s in range(2):
+            mine[s] = total(s)
+            theirs[s] = mine[s].astype(BF16)
+
+
+def ring_sum(here, terms, last, *after):
+    shape = (128, 512) if last else (2, 128, 512)
+    return vmem_kernel(
+        functools.partial(ring_sum_kernel, last),
         8,
         in_specs=[IN_SMEM] + [IN_VMEM] * (4 + len(after)),
         out_specs=[IN_VMEM] * 2,
-        out_shape=[pltpu.VMEM((128, 512), F32), pltpu.VMEM((128, 512), BF16)],
+        out_shape=[pltpu.VMEM(shape, F32), pltpu.VMEM(shape, BF16)],
         name="ring_sum",
     )(here, *terms, *after)
 
 
-def pack_kernel(here, *refs):
-    at, _ = own_place(here)
-    for k in range(4):
-        refs[-1][(at - k) & 3] = refs[k][...]
-
-
-def pack(here, shards, *after):
-    return vmem_kernel(
-        pack_kernel,
+def pair_kernel(here, mine, far, done, out):
+    _, side = own_place(here)
+    out[side] = mine[...]
+    out[1 - side] = far[...]
+
+
+def pair(here, mine, far, done):
+    return vmem_kernel(
+        pair_kernel,
         4,
-        in_specs=[IN_SMEM] + [IN_VMEM] * (4 + len(after)),
+        in_specs=[IN_SMEM] + [IN_VMEM] * 3,
         out_specs=IN_VMEM,
-        out_shape=pltpu.VMEM((4, *shards[0].shape), BF16),
-        name="in_ring_order",
-    )(here, *shards, *after)
-
-
-def update_kernel(mine, theirs, embed, new, payload=None):
-    fresh = embed[...] - RATE * (mine[...] + theirs[...].astype(F32))
-    new[...] = fresh
-    if payload is not None:
-        payload[...] = fresh.astype(BF16)
-
-
-def update(mine, theirs, embed, last):
-    more = not last
+        out_shape=pltpu.VMEM((2, *mine.shape), BF16),
+        name="both_sides",
+    )(here, mine, far, done)
+
+
+def update_kernel(mine, theirs, embed, new):
+    new[...] = embed[...] - RATE * (mine[...] + theirs[...].astype(F32))
+
+
+def update(mine, theirs, embed):
     return vmem_kernel(
         update_kernel,
         4,
         in_specs=[IN_VMEM] * 3,
-        out_specs=[IN_VMEM] * (1 + more),
-        out_shape=[pltpu.VMEM(embed.shape, F32)] + [pltpu.VMEM(embed.shape, BF16)] * more,
+        out_specs=IN_VMEM,
+        out_shape=pltpu.VMEM(embed.shape, F32),
         name="update",
     )(mine, theirs, embed)
 
 
-def logs_kernel(row_marginals, col_marginals, lr, lc, rows, cols, sem):
-    copies = [
-        pltpu.make_async_copy(row_marginals, rows, sem.at[0]),
-        pltpu.make_async_copy(col_marginals, cols, sem.at[1]),
-    ]
-    for copy in copies:
-        copy.start()
-    for copy in copies:
-        copy.wait()
-    log_rows = jnp.log(rows[...].astype(F32))
-    log_cols = jnp.log(cols[...].astype(F32))
-    for k in range(8):
-        lr[k * 128 : k * 128 + 128, :] = jnp.broadcast_to(log_rows[k : k + 1, :], (128, 128)).T
-    for h in range(2):
-        lc[h] = jnp.concatenate([log_cols[4 * h + k : 4 * h + k + 1, :] for k in range(4)], axis=1)
-
-
-def logs(row_marginals, col_marginals):
-    return vmem_kernel(
-        logs_kernel,
-        4,
-        in_specs=[IN_HBM] * 2,
+def update_both_kernel(here, mine, theirs, embed, far, done, new, payload):
+    _, side = own_place(here)
+
+    def fresh(s, old):
+        return old[...] - RATE * (mine[s] + theirs[s].astype(F32))
+
+    new[...] = fresh(side, embed)
+    payload[side] = new[...].astype(BF16)
+    payload[1 - side] = fresh(1 - side, far).astype(BF16)
+
+
+def update_both(here, mine, theirs, embed, far, done):
+    return vmem_kernel(
+        update_both_kernel,
+        8,
+        in_specs=[IN_SMEM] + [IN_VMEM] * 5,
         out_specs=[IN_VMEM] * 2,
-        out_shape=[pltpu.VMEM((1024, 128), F32), pltpu.VMEM((2, 1, 512), F32)],
-        scratch_shapes=[pltpu.VMEM((8, 128), jnp.int32)] * 2 + [pltpu.SemaphoreType.DMA((2,))],
-        name="log_marginals",
-    )(row_marginals.reshape(8, 128), col_marginals.reshape(8, 128))
-
-
-def prep_kernel(here, row_embed, col_embed, marginals, embed, payload, sums, sem):
-    sum_copy = pltpu.make_async_copy(marginals, sums, sem.at[0])
-    sum_copy.start()
+        out_shape=[pltpu.VMEM(embed.shape, F32), pltpu.VMEM(mine.shape, BF16)],
+        name="update",
+    )(here, mine, theirs, embed, far, done)
+
+
+def prep_kernel(here, row_embed, col_embed, row_marginals, col_marginals, embed, payload, lr, lc, rows, cols, sem):
+    row_copy = pltpu.make_async_copy(row_marginals, rows, sem.at[0])
+    col_copy = pltpu.make_async_copy(col_marginals, cols, sem.at[3])
+    row_copy.start()
+    col_copy.start()
 
     @pl.when(place(here)[0] == W_ROLE)
     def _():
@@ -345,9 +353,11 @@
         low.wait()
         high.wait()
 
-    sum_copy.wait()
+    row_copy.wait()
+    col_copy.wait()
     mine = embed[...].astype(BF16)
-    rest = jnp.sum(sums[...].astype(F32), axis=(0, 1), keepdims=True)
+    row_values = rows[...].astype(F32)
+    rest = jnp.sum(row_values, axis=(0, 1), keepdims=True)
     line = lax.broadcasted_iota(jnp.int32, (8, 512), 0)
     extra = jnp.zeros((8, 512), F32)
     for k in range(3):
@@ -356,18 +366,29 @@
         rest = rest - piece
     payload[:128, :] = mine
     payload[128:, :] = extra.astype(BF16)
-
-
-def prep(here, row_embed, col_embed, marginals):
+    log_rows = jnp.log(row_values)
+    log_cols = jnp.log(cols[...].astype(F32))
+    for k in range(8):
+        lr[k * 128 : k * 128 + 128, :] = jnp.broadcast_to(log_rows[k : k + 1, :], (128, 128)).T
+    for h in range(2):
+        lc[h] = jnp.concatenate([log_cols[4 * h + k : 4 * h + k + 1, :] for k in range(4)], axis=1)
+
+
+def prep(here, row_embed, col_embed, row_marginals, col_marginals):
     return vmem_kernel(
         prep_kernel,
         4,
-        in_specs=[IN_SMEM, IN_HBM, IN_HBM, IN_HBM],
-        out_specs=[IN_VMEM] * 2,
-        out_shape=[pltpu.VMEM((128, 512), F32), pltpu.VMEM((136, 512), BF16)],
-        scratch_shapes=[pltpu.VMEM((8, 128), jnp.int32), pltpu.SemaphoreType.DMA((3,))],
+        in_specs=[IN_SMEM] + [IN_HBM] * 4,
+        out_specs=[IN_VMEM] * 4,
+        out_shape=[
+            pltpu.VMEM((128, 512), F32),
+            pltpu.VMEM((136, 512), BF16),
+            pltpu.VMEM((1024, 128), F32),
+            pltpu.VMEM((2, 1, 512), F32),
+        ],
+        scratch_shapes=[pltpu.VMEM((8, 128), jnp.int32)] * 2 + [pltpu.SemaphoreType.DMA((4,))],
         name="first_payload",
-    )(here, row_embed, col_embed, marginals.reshape(8, 128))
+    )(here, row_embed, col_embed, row_marginals.reshape(8, 128), col_marginals.reshape(8, 128))
 
 
 def finish_kernel(here, embed, theirs, new_row, new_col, sem):
@@ -416,47 +437,41 @@
     def ring(x, k):
         return lax.ppermute(x, AXES, along[k])
 
-    embed, payload = prep(here, row_embed, col_embed, row_marginals)
-    payload, block_rows, block_cols, row_marginals, col_marginals = lax.optimization_barrier(
-        (payload, block_rows, block_cols, row_marginals, col_marginals)
-    )
-    lr, lc = logs(row_marginals, col_marginals)
-    rows = block_rows.reshape(block_rows.shape[:2])
-    cols = block_cols.reshape(block_cols.shape[:2])
-
-    low, done_low = abn(counts, rows, cols, 0, 0)
+    embed, payload, lr, lc = prep(here, row_embed, col_embed, row_marginals, col_marginals)
+    rows = block_rows.reshape(steps, 1, -1)
+    cols = block_cols.reshape(steps, 1, -1)
+
+    low, done = abn(counts, rows, cols, 0, 0, payload)
+    payload = pair(here, payload, other_side(payload), done)
     log_total = None
     for step in range(steps):
         last = step + 1 == steps
-        payload, rows, cols = lax.optimization_barrier((payload, rows, cols))
-        far = other_side(payload)
-        near = [payload] + [ring(payload, k) for k in (1, 3, 2)]
-        far = [far] + [ring(far, k) for k in (1, 3, 2)]
-        high, done_high = abn(counts, rows, cols, step, 1)
-        in_order = lambda x: [x[0], x[1], x[3], x[2]]
-        near = pack(here, in_order(near), done_low)
-        near_other = other_core(near)
-        far = pack(here, in_order(far), done_high)
-        far_other = other_core(far)
-        res = front(here, (near, far, near_other, far_other), low + high, lr, lc, log_total)
+        got = {k: ring(payload, k) for k in (2, 1, 3)}
+        if step == 0:
+            high, done = abn(counts, rows, cols, 0, 1, payload)
+            got[3], done = lax.optimization_barrier((got[3], done))
+        own = [payload, got[1], got[2], got[3]]
+        other = [other_core(x) for x in own]
+        res = front(here, done, own + other, low + high, lr, lc, log_total)
         if step == 0:
             *res, log_total = res
         w, c, grads, send = res
         extra = other_core(send)
         keep = back(here, w, c, grads)
         terms = merge(here, keep, extra)
-        after = []
         if not last:
-            *terms, rows, cols = lax.optimization_barrier((*terms, rows, cols))
-            low, done_low = abn(counts, rows, cols, step + 1, 0)
-            after = [done_low]
+            embed, *terms = lax.optimization_barrier((embed, *terms))
         got = {k: ring(terms[k], k) for k in (2, 1, 3)}
-        mine, theirs = ring_sum(here, [terms[0], got[1], got[2], got[3]], *after)
-        res = update(mine, other_side(theirs), embed, last)
+        terms = [terms[0], got[1], got[2], got[3]]
         if last:
-            (embed,) = res
+            mine, theirs = ring_sum(here, terms, last)
+            embed = update(mine, other_side(theirs), embed)
         else:
-            embed, payload = res
+            far = other_side(embed)
+            low, done = abn(counts, rows, cols, step + 1, 0, terms[0])
+            mine, theirs = ring_sum(here, terms, last, done)
+            high, done = abn(counts, rows, cols, step + 1, 1, theirs)
+            embed, payload = update_both(here, mine, other_side(theirs), embed, far, done)
     return tuple(finish(here, embed, other_core(embed)))
 
 

time: 96.1 us -> 92.6 us (0.964)
  Pallas kernels: 30.9 us -> 27.1 us
  starting transfers between devices: 43.6 us -> 45 us
  local copies, waits for them, and re-layouts: 1.37 us -> 0 us
    ppermute x7 -> x11, starting transfers between devices: 7.81 us -> 15.8 us  [other_core(): return lax.ppermute(x, 'rep', swap)]
    ppermute x18 -> x12, starting transfers between devices: 24.2 us -> 18.6 us  [ring(): return lax.ppermute(x, AXES, along[k])]
    pallas_call x21 -> x17, Pallas kernels: 30.9 us -> 27.1 us  [run(): call(*(pltpu.with_memory_space_constraint(x, spaces[id(spec)]) if id(spec...]
    unnamed x8 -> x0, local copies, waits for them, and re-layouts: 1.37 us -> none
    ppermute x7 -> x11, waiting for transfers between devices: 5.33 us -> 5.61 us  [other_core(): return lax.ppermute(x, 'rep', swap)]
    ppermute x18 -> x12, waiting for transfers between devices: 7.61 us -> 7.58 us  [ring(): return lax.ppermute(x, AXES, along[k])]
  transfers between devices with their start and end apart: 29 -> 27, of which waited for: 11 -> 14; matrix products, arithmetic and copies ran while one was open for 0% -> 0% of each run, Pallas kernels for 22% -> 18%
where the time goes in v4:
time: 92.6 us; the launch traced here: 92.4 us
  starting transfers between devices  45 us (49%)
  Pallas kernels  27.1 us (29%)
  waiting for transfers between devices  19.4 us (21%)
  between operations  0.98 us (1%)
    pallas_call x17, Pallas kernels, run(): call(*(pltpu.with_memory_space_constraint(x, spaces[id(spec)]) if id(spec...  27.1 us
    ppermute x12, starting transfers between devices, ring(): return lax.ppermute(x, AXES, along[k])  18.6 us
    ppermute x11, starting transfers between devices, other_core(): return lax.ppermute(x, 'rep', swap)  15.8 us
    ppermute x4, starting transfers between devices, other_side(): return lax.ppermute(x, AXES, across)  10.7 us
    ppermute x12, waiting for transfers between devices, ring(): return lax.ppermute(x, AXES, along[k])  7.58 us
    ppermute x4, waiting for transfers between devices, other_side(): return lax.ppermute(x, AXES, across)  6.18 us
    ppermute x11, waiting for transfers between devices, other_core(): return lax.ppermute(x, 'rep', swap)  5.61 us
  transfers between devices with their start and end apart: 27, of which 14 were waited for; matrix products, arithmetic and copies ran while one was open for 0% of the time, Pallas kernels for 18%

profile of v4, /device:TPU:1, one launch (start us, length us, event | category | flops | bytes accessed | tf_op | source)
XLA Modules:
  0.0 92.4 jit_solution(4602700712503524827)
XLA Ops:
  0.6 1.3 %first_payload.1 = (f32[128,512]{1,0:T(8,128)S(1)}, bf16[136,512]{1,0:T(8,128)(2,1)S(1)}, f32[1024,128]{1,0:T(8,128)S(1)}, f32[2,1,512]{2,1,0:T(1,128)S(1)}) custom-call(s32[1]{0:T(128)} %bitcast.here, f32[128,512]{1,0:T(8,128)} %row_embed.1, f32[64,1024]{1,0:T(8,128)} %col_embed.1, s32[8,128]{1,0:T(8,128)} %bitcast.17, s32[8,128]{1,0:T(8,128)} %bitcast.18), custom_call_target="tpu_custom_call" | custom-call | tf_op jit(solution)/shard_map/first_payload/pallas_call | solution.py:29
  1.9 3.7 %collective-permute-start = (bf16[136,512]{1,0:T(8,128)(2,1)S(1)}, bf16[136,512]{1,0:T(8,128)(2,1)S(1)}, u32[]{:S(2)}, u32[]{:S(2)}) collective-permute-start(bf16[136,512]{1,0:T(8,128)(2,1)S(1)} %get-tuple-element.53.after.mine), channel_id=1, source_target_pairs={{0,16},{1,3},{2,18},{3,1},{4,20},{5,7},{6,22},{7,5},{8,24},{9,11},... | collective-permute-start | bytes 417800 | tf_op jit(solution)/shard_map/ppermute | solution.py:435
  5.6 3.5 %count_factors.4 = (f32[2,2,256,512]{3,2,1,0:T(8,128)S(1)}, f32[2,2,256,512]{3,2,1,0:T(8,128)S(1)}, bf16[2,2,256,512]{3,2,1,0:T(8,128)(2,1)S(1)}, f32[8,128]{1,0:T(8,128)S(1)}) custom-call(s32[2,1,8]{2,1,0:T(1,128)} %bitcast.9, s32[2,1,8]{2,1,0:T(1,128)} %bitcast.13, s32[2,8,512,512]{3,2,1,0:T(8,128)} %counts.7, ...), custom_call_target="tpu_custom_call" | custom-call | flops 3000000000 | bytes 4194304 | tf_op jit(solution)/shard_map/count_factors/pallas_call | solution.py:29
  9.1 0.5 collective-permute-start.4
  9.6 3.1 %collective-permute-start.3 = (bf16[2,136,512]{2,1,0:T(8,128)(2,1)S(1)}, bf16[2,136,512]{2,1,0:T(8,128)(2,1)S(1)}, u32[]{:S(2)}, u32[]{:S(2)}) collective-permute-start(bf16[2,136,512]{2,1,0:T(8,128)(2,1)S(1)} %both_sides.1.after.refs_0_), channel_id=1, source_target_pairs={{0,64},{1,9},{2,66},{3,11},{4,68},{5,13},{6,70},{7,15},{8,72},{9,1... | collective-permute-start | bytes 835592 | tf_op jit(solution)/shard_map/ppermute | solution.py:438
  12.7 0.4 collective-permute-start.2
  13.1 2.3 %collective-permute-start.1 = (bf16[2,136,512]{2,1,0:T(8,128)(2,1)S(1)}, bf16[2,136,512]{2,1,0:T(8,128)(2,1)S(1)}, u32[]{:S(2)}, u32[]{:S(2)}) collective-permute-start(bf16[2,136,512]{2,1,0:T(8,128)(2,1)S(1)} %both_sides.1.after.refs_0_), channel_id=1, source_target_pairs={{0,96},{1,13},{2,98},{3,15},{4,100},{5,1},{6,102},{7,3},{8,104},{9... | collective-permute-start | bytes 835592 | tf_op jit(solution)/shard_map/ppermute | solution.py:438
  15.4 3.5 %count_factors.5 = (f32[2,2,256,512]{3,2,1,0:T(8,128)S(1)}, f32[2,2,256,512]{3,2,1,0:T(8,128)S(1)}, bf16[2,2,256,512]{3,2,1,0:T(8,128)(2,1)S(1)}, f32[8,128]{1,0:T(8,128)S(1)}) custom-call(s32[2,1,8]{2,1,0:T(1,128)} %bitcast.10, s32[2,1,8]{2,1,0:T(1,128)} %bitcast.14, s32[2,8,512,512]{3,2,1,0:T(8,128)} %counts.7, ...), custom_call_target="tpu_custom_call" | custom-call | flops 3000000000 | bytes 4194304 | tf_op jit(solution)/shard_map/count_factors/pallas_call | solution.py:29
  18.9 1.5 %collective-permute-done.1.refs_3_ = bf16[2,136,512]{2,1,0:T(8,128)(2,1)S(1)} collective-permute-done((bf16[2,136,512]{2,1,0:T(8,128)(2,1)S(1)}, bf16[2,136,512]{2,1,0:T(8,128)(2,1)S(1)}, u32[]{:S(2)}, u32[]{:S(2)}) %collective-permute-start.1) | collective-permute-done | bytes 278560 | tf_op jit(solution)/shard_map/ppermute | solution.py:438
  20.3 2.0 %collective-permute-start.6 = (bf16[2,136,512]{2,1,0:T(8,128)(2,1)S(1)}, bf16[2,136,512]{2,1,0:T(8,128)(2,1)S(1)}, u32[]{:S(2)}, u32[]{:S(2)}) collective-permute-start(bf16[2,136,512]{2,1,0:T(8,128)(2,1)S(1)} %collective-permute-done.3.refs_2_), channel_id=1, source_target_pairs={{0,1},{1,0},{2,3},{3,2},{4,5},{5,4},{6,7},{7,6},{8,9},{9,8},{10,11... | collective-permute-start | bytes 835592 | tf_op jit(solution)/shard_map/ppermute | solution.py:432
  22.4 0.4 collective-permute-start.7
  22.8 0.7 collective-permute-done.6.refs_6_
  23.5 0.4 collective-permute-done.5.refs_5_
  23.9 0.4 collective-permute-done.7.refs_7_
  24.3 3.7 %cell_grads.2 = (bf16[8,128,512]{2,1,0:T(8,128)(2,1)S(1)}, bf16[8,128,512]{2,1,0:T(8,128)(2,1)S(1)}, bf16[2,1024,512]{2,1,0:T(8,128)(2,1)S(1)}, bf16[8,128,512]{2,1,0:T(8,128)(2,1)S(1)}, f32[8,512]{1,0:T(8,128)S(1)}) custom-call(s32[1]{0:T(128)} %bitcast.here, f32[8,128]{1,0:T(8,128)S(1)} %get-tuple-element.56.done, ...), custom_call_target="tpu_custom_call" | custom-call | flops 3000000000 | bytes 16777216 | tf_op jit(solution)/shard_map/cell_grads/pallas_call | solution.py:29
  28.1 0.5 collective-permute-start.8
  28.5 1.5 %own_products.2.keep = f32[8,128,512]{2,1,0:T(8,128)S(1)} custom-call(s32[1]{0:T(128)} %bitcast.here, bf16[8,128,512]{2,1,0:T(8,128)(2,1)S(1)} %get-tuple-element.66.w, bf16[8,128,512]{2,1,0:T(8,128)(2,1)S(1)} %get-tuple-element.67.c, bf16[2,1024,512]{2,1,0:T(8,128)(2,1)S(1)} %get-tuple-element.68.grads), custom_call_target="tpu_custom_call" | custom-call | flops 1000000000 | bytes 8388608 | tf_op jit(solution)/shard_map/own_products/pallas_call | solution.py:29
  30.0 0.8 collective-permute-done.8.extra
  31.0 1.4 %collective-permute-start.9 = (bf16[2,128,512]{2,1,0:T(8,128)(2,1)S(1)}, bf16[2,128,512]{2,1,0:T(8,128)(2,1)S(1)}, u32[]{:S(2)}, u32[]{:S(2)}) collective-permute-start(bf16[2,128,512]{2,1,0:T(8,128)(2,1)S(1)} %get-tuple-element.75), channel_id=1, source_target_pairs={{0,32},{1,5},{2,34},{3,7},{4,36},{5,9},{6,38},{7,11},{8,40},{9,13}... | collective-permute-start | bytes 786440 | tf_op jit(solution)/shard_map/ppermute | solution.py:438
  32.4 2.6 %collective-permute-start.10 = (bf16[2,128,512]{2,1,0:T(8,128)(2,1)S(1)}, bf16[2,128,512]{2,1,0:T(8,128)(2,1)S(1)}, u32[]{:S(2)}, u32[]{:S(2)}) collective-permute-start(bf16[2,128,512]{2,1,0:T(8,128)(2,1)S(1)} %get-tuple-element.76), channel_id=1, source_target_pairs={{0,64},{1,9},{2,66},{3,11},{4,68},{5,13},{6,70},{7,15},{8,72},{9,1... | collective-permute-start | bytes 786440 | tf_op jit(solution)/shard_map/ppermute | solution.py:438
  35.0 1.1 %collective-permute-start.11 = (bf16[2,128,512]{2,1,0:T(8,128)(2,1)S(1)}, bf16[2,128,512]{2,1,0:T(8,128)(2,1)S(1)}, u32[]{:S(2)}, u32[]{:S(2)}) collective-permute-start(bf16[2,128,512]{2,1,0:T(8,128)(2,1)S(1)} %get-tuple-element.77), channel_id=1, source_target_pairs={{0,96},{1,13},{2,98},{3,15},{4,100},{5,1},{6,102},{7,3},{8,104},{9... | collective-permute-start | bytes 786440 | tf_op jit(solution)/shard_map/ppermute | solution.py:438
  36.1 2.8 %collective-permute-start.13 = (f32[128,512]{1,0:T(8,128)S(1)}, f32[128,512]{1,0:T(8,128)S(1)}, u32[]{:S(2)}, u32[]{:S(2)}) collective-permute-start(f32[128,512]{1,0:T(8,128)S(1)} %get-tuple-element.82.embed), channel_id=1, source_target_pairs={{0,16},{1,3},{2,18},{3,1},{4,20},{5,7},{6,22},{7,5},{8,24},{9,11},... | collective-permute-start | bytes 786440 | tf_op jit(solution)/shard_map/ppermute | solution.py:435
  38.9 3.5 %count_factors.6 = (f32[2,2,256,512]{3,2,1,0:T(8,128)S(1)}, f32[2,2,256,512]{3,2,1,0:T(8,128)S(1)}, bf16[2,2,256,512]{3,2,1,0:T(8,128)(2,1)S(1)}, f32[8,128]{1,0:T(8,128)S(1)}) custom-call(s32[2,1,8]{2,1,0:T(1,128)} %bitcast.11, s32[2,1,8]{2,1,0:T(1,128)} %bitcast.15, s32[2,8,512,512]{3,2,1,0:T(8,128)} %counts.7, ...), custom_call_target="tpu_custom_call" | custom-call | flops 3000000000 | bytes 4194304 | tf_op jit(solution)/shard_map/count_factors/pallas_call | solution.py:29
  42.6 2.4 %collective-permute-start.12 = (bf16[2,128,512]{2,1,0:T(8,128)(2,1)S(1)}, bf16[2,128,512]{2,1,0:T(8,128)(2,1)S(1)}, u32[]{:S(2)}, u32[]{:S(2)}) collective-permute-start(bf16[2,128,512]{2,1,0:T(8,128)(2,1)S(1)} %get-tuple-element.79.after), channel_id=1, source_target_pairs={{0,16},{1,3},{2,18},{3,1},{4,20},{5,7},{6,22},{7,5},{8,24},{9,11},... | collective-permute-start | bytes 786440 | tf_op jit(solution)/shard_map/ppermute | solution.py:435
  44.9 3.5 %count_factors.7 = (f32[2,2,256,512]{3,2,1,0:T(8,128)S(1)}, f32[2,2,256,512]{3,2,1,0:T(8,128)S(1)}, bf16[2,2,256,512]{3,2,1,0:T(8,128)(2,1)S(1)}, f32[8,128]{1,0:T(8,128)S(1)}) custom-call(s32[2,1,8]{2,1,0:T(1,128)} %bitcast.12, s32[2,1,8]{2,1,0:T(1,128)} %bitcast.16, s32[2,8,512,512]{3,2,1,0:T(8,128)} %counts.7, ...), custom_call_target="tpu_custom_call" | custom-call | flops 3000000000 | bytes 4194304 | tf_op jit(solution)/shard_map/count_factors/pallas_call | solution.py:29
  48.4 2.5 %collective-permute-done.12.theirs = bf16[2,128,512]{2,1,0:T(8,128)(2,1)S(1)} collective-permute-done((bf16[2,128,512]{2,1,0:T(8,128)(2,1)S(1)}, bf16[2,128,512]{2,1,0:T(8,128)(2,1)S(1)}, u32[]{:S(2)}, u32[]{:S(2)}) %collective-permute-start.12) | collective-permute-done | bytes 262176 | tf_op jit(solution)/shard_map/ppermute | solution.py:435
  51.0 1.5 %collective-permute-start.16 = (bf16[2,128,512]{2,1,0:T(8,128)(2,1)S(1)}, bf16[2,128,512]{2,1,0:T(8,128)(2,1)S(1)}, u32[]{:S(2)}, u32[]{:S(2)}) collective-permute-start(bf16[2,128,512]{2,1,0:T(8,128)(2,1)S(1)} %get-tuple-element.83.refs_0_), channel_id=1, source_target_pairs={{0,96},{1,13},{2,98},{3,15},{4,100},{5,1},{6,102},{7,3},{8,104},{9... | collective-permute-start | bytes 786440 | tf_op jit(solution)/shard_map/ppermute | solution.py:438
  52.5 1.3 %collective-permute-start.15 = (bf16[2,128,512]{2,1,0:T(8,128)(2,1)S(1)}, bf16[2,128,512]{2,1,0:T(8,128)(2,1)S(1)}, u32[]{:S(2)}, u32[]{:S(2)}) collective-permute-start(bf16[2,128,512]{2,1,0:T(8,128)(2,1)S(1)} %get-tuple-element.83.refs_0_), channel_id=1, source_target_pairs={{0,64},{1,9},{2,66},{3,11},{4,68},{5,13},{6,70},{7,15},{8,72},{9,1... | collective-permute-start | bytes 786440 | tf_op jit(solution)/shard_map/ppermute | solution.py:438
  54.0 1.9 %collective-permute-start.17 = (bf16[2,128,512]{2,1,0:T(8,128)(2,1)S(1)}, bf16[2,128,512]{2,1,0:T(8,128)(2,1)S(1)}, u32[]{:S(2)}, u32[]{:S(2)}) collective-permute-start(bf16[2,128,512]{2,1,0:T(8,128)(2,1)S(1)} %get-tuple-element.83.refs_0_), channel_id=1, source_target_pairs={{0,1},{1,0},{2,3},{3,2},{4,5},{5,4},{6,7},{7,6},{8,9},{9,8},{10,11... | collective-permute-start | bytes 786440 | tf_op jit(solution)/shard_map/ppermute | solution.py:432
  56.0 0.7 collective-permute-done.16.refs_3_
  56.6 5.1 %collective-permute-start.20 = (bf16[2,128,512]{2,1,0:T(8,128)(2,1)S(1)}, bf16[2,128,512]{2,1,0:T(8,128)(2,1)S(1)}, u32[]{:S(2)}, u32[]{:S(2)}) collective-permute-start(bf16[2,128,512]{2,1,0:T(8,128)(2,1)S(1)} %collective-permute-done.16.refs_3_), channel_id=1, source_target_pairs={{0,1},{1,0},{2,3},{3,2},{4,5},{5,4},{6,7},{7,6},{8,9},{9,8},{10,11... | collective-permute-start | bytes 786440 | tf_op jit(solution)/shard_map/ppermute | solution.py:432
  61.7 1.3 %collective-permute-start.19 = (bf16[2,128,512]{2,1,0:T(8,128)(2,1)S(1)}, bf16[2,128,512]{2,1,0:T(8,128)(2,1)S(1)}, u32[]{:S(2)}, u32[]{:S(2)}) collective-permute-start(bf16[2,128,512]{2,1,0:T(8,128)(2,1)S(1)} %collective-permute-done.15.refs_2_), channel_id=1, source_target_pairs={{0,1},{1,0},{2,3},{3,2},{4,5},{5,4},{6,7},{7,6},{8,9},{9,8},{10,11... | collective-permute-start | bytes 786440 | tf_op jit(solution)/shard_map/ppermute | solution.py:432
  63.0 2.5 %collective-permute-start.18 = (bf16[2,128,512]{2,1,0:T(8,128)(2,1)S(1)}, bf16[2,128,512]{2,1,0:T(8,128)(2,1)S(1)}, u32[]{:S(2)}, u32[]{:S(2)}) collective-permute-start(bf16[2,128,512]{2,1,0:T(8,128)(2,1)S(1)} %collective-permute-done.14.refs_1_), channel_id=1, source_target_pairs={{0,1},{1,0},{2,3},{3,2},{4,5},{5,4},{6,7},{7,6},{8,9},{9,8},{10,11... | collective-permute-start | bytes 786440 | tf_op jit(solution)/shard_map/ppermute | solution.py:432
  65.5 1.1 %collective-permute-done.18.refs_5_ = bf16[2,128,512]{2,1,0:T(8,128)(2,1)S(1)} collective-permute-done((bf16[2,128,512]{2,1,0:T(8,128)(2,1)S(1)}, bf16[2,128,512]{2,1,0:T(8,128)(2,1)S(1)}, u32[]{:S(2)}, u32[]{:S(2)}) %collective-permute-start.18) | collective-permute-done | bytes 262176 | tf_op jit(solution)/shard_map/ppermute | solution.py:432
  66.6 3.7 %cell_grads.3 = (bf16[8,128,512]{2,1,0:T(8,128)(2,1)S(1)}, bf16[8,128,512]{2,1,0:T(8,128)(2,1)S(1)}, bf16[2,1024,512]{2,1,0:T(8,128)(2,1)S(1)}, bf16[8,128,512]{2,1,0:T(8,128)(2,1)S(1)}) custom-call(s32[1]{0:T(128)} %bitcast.here, f32[8,128]{1,0:T(8,128)S(1)} %get-tuple-element.80.done, bf16[2,128,512]{2,1,0:T(8,128)(2,1)S(1)} %get-tuple-element.83.refs_0_, ...), custom_call_target="tpu_custom_call" | custom-call | flops 3000000000 | bytes 16777216 | tf_op jit(solution)/shard_map/cell_grads/pallas_call | solution.py:29
  70.3 0.4 collective-permute-start.21
  70.8 1.3 %own_products.3.keep = f32[8,128,512]{2,1,0:T(8,128)S(1)} custom-call(s32[1]{0:T(128)} %bitcast.here, bf16[8,128,512]{2,1,0:T(8,128)(2,1)S(1)} %get-tuple-element.91.w, bf16[8,128,512]{2,1,0:T(8,128)(2,1)S(1)} %get-tuple-element.92.c, bf16[2,1024,512]{2,1,0:T(8,128)(2,1)S(1)} %get-tuple-element.93.grads), custom_call_target="tpu_custom_call" | custom-call | flops 1000000000 | bytes 8388608 | tf_op jit(solution)/shard_map/own_products/pallas_call | solution.py:29
  72.1 1.0 %collective-permute-done.21.extra = bf16[8,128,512]{2,1,0:T(8,128)(2,1)S(1)} collective-permute-done((bf16[8,128,512]{2,1,0:T(8,128)(2,1)S(1)}, bf16[8,128,512]{2,1,0:T(8,128)(2,1)S(1)}, u32[]{:S(2)}, u32[]{:S(2)}) %collective-permute-start.21) | collective-permute-done | bytes 1048608 | tf_op jit(solution)/shard_map/ppermute | solution.py:432
  73.3 1.3 %collective-permute-start.22 = (bf16[2,128,512]{2,1,0:T(8,128)(2,1)S(1)}, bf16[2,128,512]{2,1,0:T(8,128)(2,1)S(1)}, u32[]{:S(2)}, u32[]{:S(2)}) collective-permute-start(bf16[2,128,512]{2,1,0:T(8,128)(2,1)S(1)} %get-tuple-element.96), channel_id=1, source_target_pairs={{0,32},{1,5},{2,34},{3,7},{4,36},{5,9},{6,38},{7,11},{8,40},{9,13}... | collective-permute-start | bytes 786440 | tf_op jit(solution)/shard_map/ppermute | solution.py:438
  74.6 2.1 %collective-permute-start.23 = (bf16[2,128,512]{2,1,0:T(8,128)(2,1)S(1)}, bf16[2,128,512]{2,1,0:T(8,128)(2,1)S(1)}, u32[]{:S(2)}, u32[]{:S(2)}) collective-permute-start(bf16[2,128,512]{2,1,0:T(8,128)(2,1)S(1)} %get-tuple-element.97), channel_id=1, source_target_pairs={{0,64},{1,9},{2,66},{3,11},{4,68},{5,13},{6,70},{7,15},{8,72},{9,1... | collective-permute-start | bytes 786440 | tf_op jit(solution)/shard_map/ppermute | solution.py:438
  76.6 1.3 %collective-permute-start.24 = (bf16[2,128,512]{2,1,0:T(8,128)(2,1)S(1)}, bf16[2,128,512]{2,1,0:T(8,128)(2,1)S(1)}, u32[]{:S(2)}, u32[]{:S(2)}) collective-permute-start(bf16[2,128,512]{2,1,0:T(8,128)(2,1)S(1)} %get-tuple-element.98), channel_id=1, source_target_pairs={{0,96},{1,13},{2,98},{3,15},{4,100},{5,1},{6,102},{7,3},{8,104},{9... | collective-permute-start | bytes 786440 | tf_op jit(solution)/shard_map/ppermute | solution.py:438
  78.0 2.1 %collective-permute-done.22.refs_1_ = bf16[2,128,512]{2,1,0:T(8,128)(2,1)S(1)} collective-permute-done((bf16[2,128,512]{2,1,0:T(8,128)(2,1)S(1)}, bf16[2,128,512]{2,1,0:T(8,128)(2,1)S(1)}, u32[]{:S(2)}, u32[]{:S(2)}) %collective-permute-start.22) | collective-permute-done | bytes 262176 | tf_op jit(solution)/shard_map/ppermute | solution.py:438
  80.1 3.1 %collective-permute-done.23.refs_2_ = bf16[2,128,512]{2,1,0:T(8,128)(2,1)S(1)} collective-permute-done((bf16[2,128,512]{2,1,0:T(8,128)(2,1)S(1)}, bf16[2,128,512]{2,1,0:T(8,128)(2,1)S(1)}, u32[]{:S(2)}, u32[]{:S(2)}) %collective-permute-start.23) | collective-permute-done | bytes 262176 | tf_op jit(solution)/shard_map/ppermute | solution.py:438
  83.6 1.9 %collective-permute-start.25 = (bf16[128,512]{1,0:T(8,128)(2,1)S(1)}, bf16[128,512]{1,0:T(8,128)(2,1)S(1)}, u32[]{:S(2)}, u32[]{:S(2)}) collective-permute-start(bf16[128,512]{1,0:T(8,128)(2,1)S(1)} %get-tuple-element.100), channel_id=1, source_target_pairs={{0,16},{1,3},{2,18},{3,1},{4,20},{5,7},{6,22},{7,5},{8,24},{9,11},... | collective-permute-start | bytes 393224 | tf_op jit(solution)/shard_map/ppermute | solution.py:435
  85.4 3.7 %collective-permute-done.25.theirs = bf16[128,512]{1,0:T(8,128)(2,1)S(1)} collective-permute-done((bf16[128,512]{1,0:T(8,128)(2,1)S(1)}, bf16[128,512]{1,0:T(8,128)(2,1)S(1)}, u32[]{:S(2)}, u32[]{:S(2)}) %collective-permute-start.25) | collective-permute-done | bytes 131104 | tf_op jit(solution)/shard_map/ppermute | solution.py:435
  89.2 1.1 %collective-permute-start.26 = (f32[128,512]{1,0:T(8,128)S(1)}, f32[128,512]{1,0:T(8,128)S(1)}, u32[]{:S(2)}, u32[]{:S(2)}) collective-permute-start(f32[128,512]{1,0:T(8,128)S(1)} %update.3.embed), channel_id=1, source_target_pairs={{0,1},{1,0},{2,3},{3,2},{4,5},{5,4},{6,7},{7,6},{8,9},{9,8},{10,11... | collective-permute-start | bytes 786440 | tf_op jit(solution)/shard_map/ppermute | solution.py:432
  90.3 1.2 %collective-permute-done.26.theirs = f32[128,512]{1,0:T(8,128)S(1)} collective-permute-done((f32[128,512]{1,0:T(8,128)S(1)}, f32[128,512]{1,0:T(8,128)S(1)}, u32[]{:S(2)}, u32[]{:S(2)}) %collective-permute-start.26) | collective-permute-done | bytes 262176 | tf_op jit(solution)/shard_map/ppermute | solution.py:432
  91.5 0.8 results.1
  (23 shorter events, 1.5 us)
Async XLA Ops:
  1.9 7.1 %collective-permute-start = (bf16[136,512]{1,0:T(8,128)(2,1)S(1)}, bf16[136,512]{1,0:T(8,128)(2,1)S(1)}, u32[]{:S(2)}, u32[]{:S(2)}) collective-permute-start(bf16[136,512]{1,0:T(8,128)(2,1)S(1)} %get-tuple-element.53.after.mine), channel_id=1, source_target_pairs={{0,16},{1,3},{2,18},{3,1},{4,20},{5,7},{6,22},{7,5},{8,24},{9,11},... | collective-permute-start | bytes 417800 | tf_op jit(solution)/shard_map/ppermute | solution.py:435
  9.1 13.7 %collective-permute-start.4 = (bf16[2,136,512]{2,1,0:T(8,128)(2,1)S(1)}, bf16[2,136,512]{2,1,0:T(8,128)(2,1)S(1)}, u32[]{:S(2)}, u32[]{:S(2)}) collective-permute-start(bf16[2,136,512]{2,1,0:T(8,128)(2,1)S(1)} %both_sides.1.after.refs_0_), channel_id=1, source_target_pairs={{0,1},{1,0},{2,3},{3,2},{4,5},{5,4},{6,7},{7,6},{8,9},{9,8},{10,11... | collective-permute-start | bytes 835592 | tf_op jit(solution)/shard_map/ppermute | solution.py:432
  9.6 10.7 %collective-permute-start.3 = (bf16[2,136,512]{2,1,0:T(8,128)(2,1)S(1)}, bf16[2,136,512]{2,1,0:T(8,128)(2,1)S(1)}, u32[]{:S(2)}, u32[]{:S(2)}) collective-permute-start(bf16[2,136,512]{2,1,0:T(8,128)(2,1)S(1)} %both_sides.1.after.refs_0_), channel_id=1, source_target_pairs={{0,64},{1,9},{2,66},{3,11},{4,68},{5,13},{6,70},{7,15},{8,72},{9,1... | collective-permute-start | bytes 835592 | tf_op jit(solution)/shard_map/ppermute | solution.py:438
  12.7 9.6 %collective-permute-start.2 = (bf16[2,136,512]{2,1,0:T(8,128)(2,1)S(1)}, bf16[2,136,512]{2,1,0:T(8,128)(2,1)S(1)}, u32[]{:S(2)}, u32[]{:S(2)}) collective-permute-start(bf16[2,136,512]{2,1,0:T(8,128)(2,1)S(1)} %both_sides.1.after.refs_0_), channel_id=1, source_target_pairs={{0,32},{1,5},{2,34},{3,7},{4,36},{5,9},{6,38},{7,11},{8,40},{9,13}... | collective-permute-start | bytes 835592 | tf_op jit(solution)/shard_map/ppermute | solution.py:438
  13.1 7.2 %collective-permute-start.1 = (bf16[2,136,512]{2,1,0:T(8,128)(2,1)S(1)}, bf16[2,136,512]{2,1,0:T(8,128)(2,1)S(1)}, u32[]{:S(2)}, u32[]{:S(2)}) collective-permute-start(bf16[2,136,512]{2,1,0:T(8,128)(2,1)S(1)} %both_sides.1.after.refs_0_), channel_id=1, source_target_pairs={{0,96},{1,13},{2,98},{3,15},{4,100},{5,1},{6,102},{7,3},{8,104},{9... | collective-permute-start | bytes 835592 | tf_op jit(solution)/shard_map/ppermute | solution.py:438
  20.3 3.2 %collective-permute-start.6 = (bf16[2,136,512]{2,1,0:T(8,128)(2,1)S(1)}, bf16[2,136,512]{2,1,0:T(8,128)(2,1)S(1)}, u32[]{:S(2)}, u32[]{:S(2)}) collective-permute-start(bf16[2,136,512]{2,1,0:T(8,128)(2,1)S(1)} %collective-permute-done.3.refs_2_), channel_id=1, source_target_pairs={{0,1},{1,0},{2,3},{3,2},{4,5},{5,4},{6,7},{7,6},{8,9},{9,8},{10,11... | collective-permute-start | bytes 835592 | tf_op jit(solution)/shard_map/ppermute | solution.py:432
  22.3 1.6 %collective-permute-start.5 = (bf16[2,136,512]{2,1,0:T(8,128)(2,1)S(1)}, bf16[2,136,512]{2,1,0:T(8,128)(2,1)S(1)}, u32[]{:S(2)}, u32[]{:S(2)}) collective-permute-start(bf16[2,136,512]{2,1,0:T(8,128)(2,1)S(1)} %collective-permute-done.2.refs_1_), channel_id=1, source_target_pairs={{0,1},{1,0},{2,3},{3,2},{4,5},{5,4},{6,7},{7,6},{8,9},{9,8},{10,11... | collective-permute-start | bytes 835592 | tf_op jit(solution)/shard_map/ppermute | solution.py:432
  22.4 1.9 %collective-permute-start.7 = (bf16[2,136,512]{2,1,0:T(8,128)(2,1)S(1)}, bf16[2,136,512]{2,1,0:T(8,128)(2,1)S(1)}, u32[]{:S(2)}, u32[]{:S(2)}) collective-permute-start(bf16[2,136,512]{2,1,0:T(8,128)(2,1)S(1)} %collective-permute-done.1.refs_3_), channel_id=1, source_target_pairs={{0,1},{1,0},{2,3},{3,2},{4,5},{5,4},{6,7},{7,6},{8,9},{9,8},{10,11... | collective-permute-start | bytes 835592 | tf_op jit(solution)/shard_map/ppermute | solution.py:432
  28.1 2.7 %collective-permute-start.8 = (bf16[8,128,512]{2,1,0:T(8,128)(2,1)S(1)}, bf16[8,128,512]{2,1,0:T(8,128)(2,1)S(1)}, u32[]{:S(2)}, u32[]{:S(2)}) collective-permute-start(bf16[8,128,512]{2,1,0:T(8,128)(2,1)S(1)} %get-tuple-element.69), channel_id=1, source_target_pairs={{0,1},{1,0},{2,3},{3,2},{4,5},{5,4},{6,7},{7,6},{8,9},{9,8},{10,11... | collective-permute-start | bytes 3145736 | tf_op jit(solution)/shard_map/ppermute | solution.py:432
  31.0 11.3 %collective-permute-start.9 = (bf16[2,128,512]{2,1,0:T(8,128)(2,1)S(1)}, bf16[2,128,512]{2,1,0:T(8,128)(2,1)S(1)}, u32[]{:S(2)}, u32[]{:S(2)}) collective-permute-start(bf16[2,128,512]{2,1,0:T(8,128)(2,1)S(1)} %get-tuple-element.75), channel_id=1, source_target_pairs={{0,32},{1,5},{2,34},{3,7},{4,36},{5,9},{6,38},{7,11},{8,40},{9,13}... | collective-permute-start | bytes 786440 | tf_op jit(solution)/shard_map/ppermute | solution.py:438
  32.4 10.0 %collective-permute-start.10 = (bf16[2,128,512]{2,1,0:T(8,128)(2,1)S(1)}, bf16[2,128,512]{2,1,0:T(8,128)(2,1)S(1)}, u32[]{:S(2)}, u32[]{:S(2)}) collective-permute-start(bf16[2,128,512]{2,1,0:T(8,128)(2,1)S(1)} %get-tuple-element.76), channel_id=1, source_target_pairs={{0,64},{1,9},{2,66},{3,11},{4,68},{5,13},{6,70},{7,15},{8,72},{9,1... | collective-permute-start | bytes 786440 | tf_op jit(solution)/shard_map/ppermute | solution.py:438
  35.0 7.4 %collective-permute-start.11 = (bf16[2,128,512]{2,1,0:T(8,128)(2,1)S(1)}, bf16[2,128,512]{2,1,0:T(8,128)(2,1)S(1)}, u32[]{:S(2)}, u32[]{:S(2)}) collective-permute-start(bf16[2,128,512]{2,1,0:T(8,128)(2,1)S(1)} %get-tuple-element.77), channel_id=1, source_target_pairs={{0,96},{1,13},{2,98},{3,15},{4,100},{5,1},{6,102},{7,3},{8,104},{9... | collective-permute-start | bytes 786440 | tf_op jit(solution)/shard_map/ppermute | solution.py:438
  36.1 12.3 %collective-permute-start.13 = (f32[128,512]{1,0:T(8,128)S(1)}, f32[128,512]{1,0:T(8,128)S(1)}, u32[]{:S(2)}, u32[]{:S(2)}) collective-permute-start(f32[128,512]{1,0:T(8,128)S(1)} %get-tuple-element.82.embed), channel_id=1, source_target_pairs={{0,16},{1,3},{2,18},{3,1},{4,20},{5,7},{6,22},{7,5},{8,24},{9,11},... | collective-permute-start | bytes 786440 | tf_op jit(solution)/shard_map/ppermute | solution.py:435
  42.6 8.3 %collective-permute-start.12 = (bf16[2,128,512]{2,1,0:T(8,128)(2,1)S(1)}, bf16[2,128,512]{2,1,0:T(8,128)(2,1)S(1)}, u32[]{:S(2)}, u32[]{:S(2)}) collective-permute-start(bf16[2,128,512]{2,1,0:T(8,128)(2,1)S(1)} %get-tuple-element.79.after), channel_id=1, source_target_pairs={{0,16},{1,3},{2,18},{3,1},{4,20},{5,7},{6,22},{7,5},{8,24},{9,11},... | collective-permute-start | bytes 786440 | tf_op jit(solution)/shard_map/ppermute | solution.py:435
  51.0 5.6 %collective-permute-start.16 = (bf16[2,128,512]{2,1,0:T(8,128)(2,1)S(1)}, bf16[2,128,512]{2,1,0:T(8,128)(2,1)S(1)}, u32[]{:S(2)}, u32[]{:S(2)}) collective-permute-start(bf16[2,128,512]{2,1,0:T(8,128)(2,1)S(1)} %get-tuple-element.83.refs_0_), channel_id=1, source_target_pairs={{0,96},{1,13},{2,98},{3,15},{4,100},{5,1},{6,102},{7,3},{8,104},{9... | collective-permute-start | bytes 786440 | tf_op jit(solution)/shard_map/ppermute | solution.py:438
  52.5 9.2 %collective-permute-start.15 = (bf16[2,128,512]{2,1,0:T(8,128)(2,1)S(1)}, bf16[2,128,512]{2,1,0:T(8,128)(2,1)S(1)}, u32[]{:S(2)}, u32[]{:S(2)}) collective-permute-start(bf16[2,128,512]{2,1,0:T(8,128)(2,1)S(1)} %get-tuple-element.83.refs_0_), channel_id=1, source_target_pairs={{0,64},{1,9},{2,66},{3,11},{4,68},{5,13},{6,70},{7,15},{8,72},{9,1... | collective-permute-start | bytes 786440 | tf_op jit(solution)/shard_map/ppermute | solution.py:438
  53.8 9.2 %collective-permute-start.14 = (bf16[2,128,512]{2,1,0:T(8,128)(2,1)S(1)}, bf16[2,128,512]{2,1,0:T(8,128)(2,1)S(1)}, u32[]{:S(2)}, u32[]{:S(2)}) collective-permute-start(bf16[2,128,512]{2,1,0:T(8,128)(2,1)S(1)} %get-tuple-element.83.refs_0_), channel_id=1, source_target_pairs={{0,32},{1,5},{2,34},{3,7},{4,36},{5,9},{6,38},{7,11},{8,40},{9,13}... | collective-permute-start | bytes 786440 | tf_op jit(solution)/shard_map/ppermute | solution.py:438
  54.0 11.4 %collective-permute-start.17 = (bf16[2,128,512]{2,1,0:T(8,128)(2,1)S(1)}, bf16[2,128,512]{2,1,0:T(8,128)(2,1)S(1)}, u32[]{:S(2)}, u32[]{:S(2)}) collective-permute-start(bf16[2,128,512]{2,1,0:T(8,128)(2,1)S(1)} %get-tuple-element.83.refs_0_), channel_id=1, source_target_pairs={{0,1},{1,0},{2,3},{3,2},{4,5},{5,4},{6,7},{7,6},{8,9},{9,8},{10,11... | collective-permute-start | bytes 786440 | tf_op jit(solution)/shard_map/ppermute | solution.py:432
  56.6 8.8 %collective-permute-start.20 = (bf16[2,128,512]{2,1,0:T(8,128)(2,1)S(1)}, bf16[2,128,512]{2,1,0:T(8,128)(2,1)S(1)}, u32[]{:S(2)}, u32[]{:S(2)}) collective-permute-start(bf16[2,128,512]{2,1,0:T(8,128)(2,1)S(1)} %collective-permute-done.16.refs_3_), channel_id=1, source_target_pairs={{0,1},{1,0},{2,3},{3,2},{4,5},{5,4},{6,7},{7,6},{8,9},{9,8},{10,11... | collective-permute-start | bytes 786440 | tf_op jit(solution)/shard_map/ppermute | solution.py:432
  61.7 3.7 %collective-permute-start.19 = (bf16[2,128,512]{2,1,0:T(8,128)(2,1)S(1)}, bf16[2,128,512]{2,1,0:T(8,128)(2,1)S(1)}, u32[]{:S(2)}, u32[]{:S(2)}) collective-permute-start(bf16[2,128,512]{2,1,0:T(8,128)(2,1)S(1)} %collective-permute-done.15.refs_2_), channel_id=1, source_target_pairs={{0,1},{1,0},{2,3},{3,2},{4,5},{5,4},{6,7},{7,6},{8,9},{9,8},{10,11... | collective-permute-start | bytes 786440 | tf_op jit(solution)/shard_map/ppermute | solution.py:432
  63.0 3.6 %collective-permute-start.18 = (bf16[2,128,512]{2,1,0:T(8,128)(2,1)S(1)}, bf16[2,128,512]{2,1,0:T(8,128)(2,1)S(1)}, u32[]{:S(2)}, u32[]{:S(2)}) collective-permute-start(bf16[2,128,512]{2,1,0:T(8,128)(2,1)S(1)} %collective-permute-done.14.refs_1_), channel_id=1, source_target_pairs={{0,1},{1,0},{2,3},{3,2},{4,5},{5,4},{6,7},{7,6},{8,9},{9,8},{10,11... | collective-permute-start | bytes 786440 | tf_op jit(solution)/shard_map/ppermute | solution.py:432
  70.3 2.7 %collective-permute-start.21 = (bf16[8,128,512]{2,1,0:T(8,128)(2,1)S(1)}, bf16[8,128,512]{2,1,0:T(8,128)(2,1)S(1)}, u32[]{:S(2)}, u32[]{:S(2)}) collective-permute-start(bf16[8,128,512]{2,1,0:T(8,128)(2,1)S(1)} %get-tuple-element.94), channel_id=1, source_target_pairs={{0,1},{1,0},{2,3},{3,2},{4,5},{5,4},{6,7},{7,6},{8,9},{9,8},{10,11... | collective-permute-start | bytes 3145736 | tf_op jit(solution)/shard_map/ppermute | solution.py:432
  73.3 6.8 %collective-permute-start.22 = (bf16[2,128,512]{2,1,0:T(8,128)(2,1)S(1)}, bf16[2,128,512]{2,1,0:T(8,128)(2,1)S(1)}, u32[]{:S(2)}, u32[]{:S(2)}) collective-permute-start(bf16[2,128,512]{2,1,0:T(8,128)(2,1)S(1)} %get-tuple-element.96), channel_id=1, source_target_pairs={{0,32},{1,5},{2,34},{3,7},{4,36},{5,9},{6,38},{7,11},{8,40},{9,13}... | collective-permute-start | bytes 786440 | tf_op jit(solution)/shard_map/ppermute | solution.py:438
  74.6 8.6 %collective-permute-start.23 = (bf16[2,128,512]{2,1,0:T(8,128)(2,1)S(1)}, bf16[2,128,512]{2,1,0:T(8,128)(2,1)S(1)}, u32[]{:S(2)}, u32[]{:S(2)}) collective-permute-start(bf16[2,128,512]{2,1,0:T(8,128)(2,1)S(1)} %get-tuple-element.97), channel_id=1, source_target_pairs={{0,64},{1,9},{2,66},{3,11},{4,68},{5,13},{6,70},{7,15},{8,72},{9,1... | collective-permute-start | bytes 786440 | tf_op jit(solution)/shard_map/ppermute | solution.py:438
  76.6 6.8 %collective-permute-start.24 = (bf16[2,128,512]{2,1,0:T(8,128)(2,1)S(1)}, bf16[2,128,512]{2,1,0:T(8,128)(2,1)S(1)}, u32[]{:S(2)}, u32[]{:S(2)}) collective-permute-start(bf16[2,128,512]{2,1,0:T(8,128)(2,1)S(1)} %get-tuple-element.98), channel_id=1, source_target_pairs={{0,96},{1,13},{2,98},{3,15},{4,100},{5,1},{6,102},{7,3},{8,104},{9... | collective-permute-start | bytes 786440 | tf_op jit(solution)/shard_map/ppermute | solution.py:438
  83.6 5.6 %collective-permute-start.25 = (bf16[128,512]{1,0:T(8,128)(2,1)S(1)}, bf16[128,512]{1,0:T(8,128)(2,1)S(1)}, u32[]{:S(2)}, u32[]{:S(2)}) collective-permute-start(bf16[128,512]{1,0:T(8,128)(2,1)S(1)} %get-tuple-element.100), channel_id=1, source_target_pairs={{0,16},{1,3},{2,18},{3,1},{4,20},{5,7},{6,22},{7,5},{8,24},{9,11},... | collective-permute-start | bytes 393224 | tf_op jit(solution)/shard_map/ppermute | solution.py:435
  89.2 2.3 %collective-permute-start.26 = (f32[128,512]{1,0:T(8,128)S(1)}, f32[128,512]{1,0:T(8,128)S(1)}, u32[]{:S(2)}, u32[]{:S(2)}) collective-permute-start(f32[128,512]{1,0:T(8,128)S(1)} %update.3.embed), channel_id=1, source_target_pairs={{0,1},{1,0},{2,3},{3,2},{4,5},{5,4},{6,7},{7,6},{8,9},{9,8},{10,11... | collective-permute-start | bytes 786440 | tf_op jit(solution)/shard_map/ppermute | solution.py:432

commit v5 on v4

--- a/solution.py
+++ b/solution.py
@@ -91,8 +91,10 @@
             for g in range(2):
                 for h in range(2):
                     number = seen[g, h, part, :]
+                    zeros = 0.5 * (sampled[g, h] - number)
                     a[g, h, part, :] = 0.1 * number + 0.25 * a[g, h, part, :]
-                    n[g, h, part, :] = (sampled[g, h] - number).astype(BF16)
+                    b[g, h, part, :] -= zeros
+                    n[g, h, part, :] = zeros.astype(BF16)
             return carry
 
         lax.fori_loop(0, PIECE // STRIP, strip, 0)
@@ -141,33 +143,43 @@
                 pieces += jnp.sum(of_c[k][:, 128:, :].astype(F32), axis=0)
             log_total[...] = jnp.broadcast_to(jnp.log(jnp.sum(pieces, axis=0, keepdims=True)), log_total.shape)
 
+    def body(of_w, of_c, send_rows):
+        assemble(of_w, of_c)
+        held = {}
+        for g in range(2):
+            wg = w[4 * g : 4 * g + 4].reshape(512, 512)
+            for h in range(2):
+                ch = c[:, h * 64 : h * 64 + 64, :].reshape(512, 512)
+                dots = jnp.dot(wg, ch, preferred_element_type=F32)
+                t = dots + jnp.tile(lr[g * 512 : g * 512 + 512, :], (1, 4)) + (lc[h] - log_total[0:1, :])
+                hinge = jnp.tanh(0.5 * t)
+                parts = []
+                for e in range(2):
+                    part = slice(e * 256, e * 256 + 256)
+                    grad = t[part] * a[e][g, h] - b[e][g, h] + n[e][g, h].astype(F32) * hinge[part]
+                    parts.append(grad.astype(BF16))
+                grad = jnp.concatenate(parts, axis=0)
+                grads[h, g * 512 : g * 512 + 512, :] = grad
+                if send_rows:
+                    term = lax.dot_general(grad, ch, NT, preferred_element_type=F32)
+                    if h == 0:
+                        held[g] = term
+                    else:
+                        send[4 * g : 4 * g + 4] = (held[g] + term).reshape(4, 128, 512).astype(BF16)
+                else:
+                    term = lax.dot_general(wg, grad, TN, preferred_element_type=F32)
+                    if g == 0:
+                        held[h] = term
+                    else:
+                        send[:, h * 64 : h * 64 + 64, :] = (held[h] + term).reshape(8, 64, 512).astype(BF16)
+
     @pl.when(role == W_ROLE)
     def _():
-        assemble(own, other)
+        body(own, other, False)
 
     @pl.when(role != W_ROLE)
     def _():
-        assemble(other, own)
-
-    for g in range(2):
-        wg = w[4 * g : 4 * g + 4].reshape(512, 512)
-        for h in range(2):
-            ch = c[:, h * 64 : h * 64 + 64, :].reshape(512, 512)
-            dots = jnp.dot(wg, ch, preferred_element_type=F32)
-            t = dots + jnp.tile(lr[g * 512 : g * 512 + 512, :], (1, 4)) + (lc[h] - log_total[0:1, :])
-            hinge = 0.5 + 0.5 * jnp.tanh(0.5 * t)
-            for e in range(2):
-                part = slice(e * 256, e * 256 + 256)
-                grad = t[part] * a[e][g, h] - b[e][g, h] + n[e][g, h].astype(F32) * hinge[part]
-                grads[h, g * 512 + e * 256 : g * 512 + e * 256 + 256, :] = grad.astype(BF16)
-
-    @pl.when(role == W_ROLE)
-    def _():
-        col_grad(w, c, grads, send)
-
-    @pl.when(role != W_ROLE)
-    def _():
-        row_grad(w, c, grads, send)
+        body(other, own, True)
 
 
 def row_grad(w, c, grads, out):

time: 92.6 us -> 92 us (level)
  starting transfers between devices: 45 us -> 43.5 us
    ppermute x11, starting transfers between devices: 15.8 us -> 14.1 us  [other_core(): return lax.ppermute(x, 'rep', swap)]
  transfers between devices with their start and end apart: 27 -> 27, of which waited for: 14 -> 14; matrix products, arithmetic and copies ran while one was open for 0% -> 0% of each run, Pallas kernels for 18% -> 19%
where the time goes in v5:
time: 92 us; the launch traced here: 91.9 us
  starting transfers between devices  43.5 us (47%)
  Pallas kernels  27.3 us (30%)
  waiting for transfers between devices  20.1 us (22%)
  between operations  0.98 us (1%)
    pallas_call x17, Pallas kernels, run(): call(*(pltpu.with_memory_space_constraint(x, spaces[id(spec)]) if id(spec...  27.3 us
    ppermute x12, starting transfers between devices, ring(): return lax.ppermute(x, AXES, along[k])  18.6 us
    ppermute x11, starting transfers between devices, other_core(): return lax.ppermute(x, 'rep', swap)  14.1 us
    ppermute x4, starting transfers between devices, other_side(): return lax.ppermute(x, AXES, across)  10.7 us
    ppermute x12, waiting for transfers between devices, ring(): return lax.ppermute(x, AXES, along[k])  7.99 us
    ppermute x11, waiting for transfers between devices, other_core(): return lax.ppermute(x, 'rep', swap)  6.16 us
    ppermute x4, waiting for transfers between devices, other_side(): return lax.ppermute(x, AXES, across)  5.92 us
  transfers between devices with their start and end apart: 27, of which 14 were waited for; matrix products, arithmetic and copies ran while one was open for 0% of the time, Pallas kernels for 19%

profile of v5, /device:TPU:1, one launch (start us, length us, event | category | flops | bytes accessed | tf_op | source)
XLA Modules:
  0.0 91.9 jit_solution(615972149288162110)
XLA Ops:
  0.6 1.3 %first_payload.1 = (f32[128,512]{1,0:T(8,128)S(1)}, bf16[136,512]{1,0:T(8,128)(2,1)S(1)}, f32[1024,128]{1,0:T(8,128)S(1)}, f32[2,1,512]{2,1,0:T(1,128)S(1)}) custom-call(s32[1]{0:T(128)} %bitcast.here, f32[128,512]{1,0:T(8,128)} %row_embed.1, f32[64,1024]{1,0:T(8,128)} %col_embed.1, s32[8,128]{1,0:T(8,128)} %bitcast.17, s32[8,128]{1,0:T(8,128)} %bitcast.18), custom_call_target="tpu_custom_call" | custom-call | tf_op jit(solution)/shard_map/first_payload/pallas_call | solution.py:29
  1.9 3.7 %collective-permute-start = (bf16[136,512]{1,0:T(8,128)(2,1)S(1)}, bf16[136,512]{1,0:T(8,128)(2,1)S(1)}, u32[]{:S(2)}, u32[]{:S(2)}) collective-permute-start(bf16[136,512]{1,0:T(8,128)(2,1)S(1)} %get-tuple-element.53.after.mine), channel_id=1, source_target_pairs={{0,16},{1,3},{2,18},{3,1},{4,20},{5,7},{6,22},{7,5},{8,24},{9,11},... | collective-permute-start | bytes 417800 | tf_op jit(solution)/shard_map/ppermute | solution.py:447
  5.6 3.6 %count_factors.4 = (f32[2,2,256,512]{3,2,1,0:T(8,128)S(1)}, f32[2,2,256,512]{3,2,1,0:T(8,128)S(1)}, bf16[2,2,256,512]{3,2,1,0:T(8,128)(2,1)S(1)}, f32[8,128]{1,0:T(8,128)S(1)}) custom-call(s32[2,1,8]{2,1,0:T(1,128)} %bitcast.9, s32[2,1,8]{2,1,0:T(1,128)} %bitcast.13, s32[2,8,512,512]{3,2,1,0:T(8,128)} %counts.7, ...), custom_call_target="tpu_custom_call" | custom-call | flops 3000000000 | bytes 4194304 | tf_op jit(solution)/shard_map/count_factors/pallas_call | solution.py:29
  9.3 0.4 collective-permute-start.4
  9.6 3.1 %collective-permute-start.3 = (bf16[2,136,512]{2,1,0:T(8,128)(2,1)S(1)}, bf16[2,136,512]{2,1,0:T(8,128)(2,1)S(1)}, u32[]{:S(2)}, u32[]{:S(2)}) collective-permute-start(bf16[2,136,512]{2,1,0:T(8,128)(2,1)S(1)} %both_sides.1.after.refs_0_), channel_id=1, source_target_pairs={{0,64},{1,9},{2,66},{3,11},{4,68},{5,13},{6,70},{7,15},{8,72},{9,1... | collective-permute-start | bytes 835592 | tf_op jit(solution)/shard_map/ppermute | solution.py:450
  12.7 0.4 collective-permute-start.2
  13.1 2.3 %collective-permute-start.1 = (bf16[2,136,512]{2,1,0:T(8,128)(2,1)S(1)}, bf16[2,136,512]{2,1,0:T(8,128)(2,1)S(1)}, u32[]{:S(2)}, u32[]{:S(2)}) collective-permute-start(bf16[2,136,512]{2,1,0:T(8,128)(2,1)S(1)} %both_sides.1.after.refs_0_), channel_id=1, source_target_pairs={{0,96},{1,13},{2,98},{3,15},{4,100},{5,1},{6,102},{7,3},{8,104},{9... | collective-permute-start | bytes 835592 | tf_op jit(solution)/shard_map/ppermute | solution.py:450
  15.4 3.6 %count_factors.5 = (f32[2,2,256,512]{3,2,1,0:T(8,128)S(1)}, f32[2,2,256,512]{3,2,1,0:T(8,128)S(1)}, bf16[2,2,256,512]{3,2,1,0:T(8,128)(2,1)S(1)}, f32[8,128]{1,0:T(8,128)S(1)}) custom-call(s32[2,1,8]{2,1,0:T(1,128)} %bitcast.10, s32[2,1,8]{2,1,0:T(1,128)} %bitcast.14, s32[2,8,512,512]{3,2,1,0:T(8,128)} %counts.7, ...), custom_call_target="tpu_custom_call" | custom-call | flops 3000000000 | bytes 4194304 | tf_op jit(solution)/shard_map/count_factors/pallas_call | solution.py:29
  19.1 1.3 %collective-permute-done.1.refs_3_ = bf16[2,136,512]{2,1,0:T(8,128)(2,1)S(1)} collective-permute-done((bf16[2,136,512]{2,1,0:T(8,128)(2,1)S(1)}, bf16[2,136,512]{2,1,0:T(8,128)(2,1)S(1)}, u32[]{:S(2)}, u32[]{:S(2)}) %collective-permute-start.1) | collective-permute-done | bytes 278560 | tf_op jit(solution)/shard_map/ppermute | solution.py:450
  20.3 2.0 %collective-permute-start.6 = (bf16[2,136,512]{2,1,0:T(8,128)(2,1)S(1)}, bf16[2,136,512]{2,1,0:T(8,128)(2,1)S(1)}, u32[]{:S(2)}, u32[]{:S(2)}) collective-permute-start(bf16[2,136,512]{2,1,0:T(8,128)(2,1)S(1)} %collective-permute-done.3.refs_2_), channel_id=1, source_target_pairs={{0,1},{1,0},{2,3},{3,2},{4,5},{5,4},{6,7},{7,6},{8,9},{9,8},{10,11... | collective-permute-start | bytes 835592 | tf_op jit(solution)/shard_map/ppermute | solution.py:444
  22.4 0.4 collective-permute-start.7
  22.8 0.7 collective-permute-done.6.refs_6_
  23.5 0.4 collective-permute-done.5.refs_5_
  23.9 0.4 collective-permute-done.7.refs_7_
  24.3 3.6 %cell_grads.2 = (bf16[8,128,512]{2,1,0:T(8,128)(2,1)S(1)}, bf16[8,128,512]{2,1,0:T(8,128)(2,1)S(1)}, bf16[2,1024,512]{2,1,0:T(8,128)(2,1)S(1)}, bf16[8,128,512]{2,1,0:T(8,128)(2,1)S(1)}, f32[8,512]{1,0:T(8,128)S(1)}) custom-call(s32[1]{0:T(128)} %bitcast.here, f32[8,128]{1,0:T(8,128)S(1)} %get-tuple-element.56.done, ...), custom_call_target="tpu_custom_call" | custom-call | flops 3000000000 | bytes 16777216 | tf_op jit(solution)/shard_map/cell_grads/pallas_call | solution.py:29
  27.9 0.2 collective-permute-start.8
  28.1 1.3 %own_products.2.keep = f32[8,128,512]{2,1,0:T(8,128)S(1)} custom-call(s32[1]{0:T(128)} %bitcast.here, bf16[8,128,512]{2,1,0:T(8,128)(2,1)S(1)} %get-tuple-element.66.w, bf16[8,128,512]{2,1,0:T(8,128)(2,1)S(1)} %get-tuple-element.67.c, bf16[2,1024,512]{2,1,0:T(8,128)(2,1)S(1)} %get-tuple-element.68.grads), custom_call_target="tpu_custom_call" | custom-call | flops 1000000000 | bytes 8388608 | tf_op jit(solution)/shard_map/own_products/pallas_call | solution.py:29
  29.4 1.2 %collective-permute-done.8.extra = bf16[8,128,512]{2,1,0:T(8,128)(2,1)S(1)} collective-permute-done((bf16[8,128,512]{2,1,0:T(8,128)(2,1)S(1)}, bf16[8,128,512]{2,1,0:T(8,128)(2,1)S(1)}, u32[]{:S(2)}, u32[]{:S(2)}) %collective-permute-start.8) | collective-permute-done | bytes 1048608 | tf_op jit(solution)/shard_map/ppermute | solution.py:444
  30.8 1.4 %collective-permute-start.9 = (bf16[2,128,512]{2,1,0:T(8,128)(2,1)S(1)}, bf16[2,128,512]{2,1,0:T(8,128)(2,1)S(1)}, u32[]{:S(2)}, u32[]{:S(2)}) collective-permute-start(bf16[2,128,512]{2,1,0:T(8,128)(2,1)S(1)} %get-tuple-element.75), channel_id=1, source_target_pairs={{0,32},{1,5},{2,34},{3,7},{4,36},{5,9},{6,38},{7,11},{8,40},{9,13}... | collective-permute-start | bytes 786440 | tf_op jit(solution)/shard_map/ppermute | solution.py:450
  32.2 2.6 %collective-permute-start.10 = (bf16[2,128,512]{2,1,0:T(8,128)(2,1)S(1)}, bf16[2,128,512]{2,1,0:T(8,128)(2,1)S(1)}, u32[]{:S(2)}, u32[]{:S(2)}) collective-permute-start(bf16[2,128,512]{2,1,0:T(8,128)(2,1)S(1)} %get-tuple-element.76), channel_id=1, source_target_pairs={{0,64},{1,9},{2,66},{3,11},{4,68},{5,13},{6,70},{7,15},{8,72},{9,1... | collective-permute-start | bytes 786440 | tf_op jit(solution)/shard_map/ppermute | solution.py:450
  34.8 1.1 %collective-permute-start.11 = (bf16[2,128,512]{2,1,0:T(8,128)(2,1)S(1)}, bf16[2,128,512]{2,1,0:T(8,128)(2,1)S(1)}, u32[]{:S(2)}, u32[]{:S(2)}) collective-permute-start(bf16[2,128,512]{2,1,0:T(8,128)(2,1)S(1)} %get-tuple-element.77), channel_id=1, source_target_pairs={{0,96},{1,13},{2,98},{3,15},{4,100},{5,1},{6,102},{7,3},{8,104},{9... | collective-permute-start | bytes 786440 | tf_op jit(solution)/shard_map/ppermute | solution.py:450
  35.9 2.8 %collective-permute-start.13 = (f32[128,512]{1,0:T(8,128)S(1)}, f32[128,512]{1,0:T(8,128)S(1)}, u32[]{:S(2)}, u32[]{:S(2)}) collective-permute-start(f32[128,512]{1,0:T(8,128)S(1)} %get-tuple-element.82.embed), channel_id=1, source_target_pairs={{0,16},{1,3},{2,18},{3,1},{4,20},{5,7},{6,22},{7,5},{8,24},{9,11},... | collective-permute-start | bytes 786440 | tf_op jit(solution)/shard_map/ppermute | solution.py:447
  38.7 3.6 %count_factors.6 = (f32[2,2,256,512]{3,2,1,0:T(8,128)S(1)}, f32[2,2,256,512]{3,2,1,0:T(8,128)S(1)}, bf16[2,2,256,512]{3,2,1,0:T(8,128)(2,1)S(1)}, f32[8,128]{1,0:T(8,128)S(1)}) custom-call(s32[2,1,8]{2,1,0:T(1,128)} %bitcast.11, s32[2,1,8]{2,1,0:T(1,128)} %bitcast.15, s32[2,8,512,512]{3,2,1,0:T(8,128)} %counts.7, ...), custom_call_target="tpu_custom_call" | custom-call | flops 3000000000 | bytes 4194304 | tf_op jit(solution)/shard_map/count_factors/pallas_call | solution.py:29
  42.5 2.2 %collective-permute-start.12 = (bf16[2,128,512]{2,1,0:T(8,128)(2,1)S(1)}, bf16[2,128,512]{2,1,0:T(8,128)(2,1)S(1)}, u32[]{:S(2)}, u32[]{:S(2)}) collective-permute-start(bf16[2,128,512]{2,1,0:T(8,128)(2,1)S(1)} %get-tuple-element.79.after), channel_id=1, source_target_pairs={{0,16},{1,3},{2,18},{3,1},{4,20},{5,7},{6,22},{7,5},{8,24},{9,11},... | collective-permute-start | bytes 786440 | tf_op jit(solution)/shard_map/ppermute | solution.py:447
  44.7 3.6 %count_factors.7 = (f32[2,2,256,512]{3,2,1,0:T(8,128)S(1)}, f32[2,2,256,512]{3,2,1,0:T(8,128)S(1)}, bf16[2,2,256,512]{3,2,1,0:T(8,128)(2,1)S(1)}, f32[8,128]{1,0:T(8,128)S(1)}) custom-call(s32[2,1,8]{2,1,0:T(1,128)} %bitcast.12, s32[2,1,8]{2,1,0:T(1,128)} %bitcast.16, s32[2,8,512,512]{3,2,1,0:T(8,128)} %counts.7, ...), custom_call_target="tpu_custom_call" | custom-call | flops 3000000000 | bytes 4194304 | tf_op jit(solution)/shard_map/count_factors/pallas_call | solution.py:29
  48.4 2.6 %collective-permute-done.12.theirs = bf16[2,128,512]{2,1,0:T(8,128)(2,1)S(1)} collective-permute-done((bf16[2,128,512]{2,1,0:T(8,128)(2,1)S(1)}, bf16[2,128,512]{2,1,0:T(8,128)(2,1)S(1)}, u32[]{:S(2)}, u32[]{:S(2)}) %collective-permute-start.12) | collective-permute-done | bytes 262176 | tf_op jit(solution)/shard_map/ppermute | solution.py:447
  51.1 1.4 %collective-permute-start.16 = (bf16[2,128,512]{2,1,0:T(8,128)(2,1)S(1)}, bf16[2,128,512]{2,1,0:T(8,128)(2,1)S(1)}, u32[]{:S(2)}, u32[]{:S(2)}) collective-permute-start(bf16[2,128,512]{2,1,0:T(8,128)(2,1)S(1)} %get-tuple-element.83.refs_0_), channel_id=1, source_target_pairs={{0,96},{1,13},{2,98},{3,15},{4,100},{5,1},{6,102},{7,3},{8,104},{9... | collective-permute-start | bytes 786440 | tf_op jit(solution)/shard_map/ppermute | solution.py:450
  52.6 1.2 %collective-permute-start.15 = (bf16[2,128,512]{2,1,0:T(8,128)(2,1)S(1)}, bf16[2,128,512]{2,1,0:T(8,128)(2,1)S(1)}, u32[]{:S(2)}, u32[]{:S(2)}) collective-permute-start(bf16[2,128,512]{2,1,0:T(8,128)(2,1)S(1)} %get-tuple-element.83.refs_0_), channel_id=1, source_target_pairs={{0,64},{1,9},{2,66},{3,11},{4,68},{5,13},{6,70},{7,15},{8,72},{9,1... | collective-permute-start | bytes 786440 | tf_op jit(solution)/shard_map/ppermute | solution.py:450
  54.0 1.3 %collective-permute-start.17 = (bf16[2,128,512]{2,1,0:T(8,128)(2,1)S(1)}, bf16[2,128,512]{2,1,0:T(8,128)(2,1)S(1)}, u32[]{:S(2)}, u32[]{:S(2)}) collective-permute-start(bf16[2,128,512]{2,1,0:T(8,128)(2,1)S(1)} %get-tuple-element.83.refs_0_), channel_id=1, source_target_pairs={{0,1},{1,0},{2,3},{3,2},{4,5},{5,4},{6,7},{7,6},{8,9},{9,8},{10,11... | collective-permute-start | bytes 786440 | tf_op jit(solution)/shard_map/ppermute | solution.py:444
  55.3 1.4 %collective-permute-done.16.refs_3_ = bf16[2,128,512]{2,1,0:T(8,128)(2,1)S(1)} collective-permute-done((bf16[2,128,512]{2,1,0:T(8,128)(2,1)S(1)}, bf16[2,128,512]{2,1,0:T(8,128)(2,1)S(1)}, u32[]{:S(2)}, u32[]{:S(2)}) %collective-permute-start.16) | collective-permute-done | bytes 262176 | tf_op jit(solution)/shard_map/ppermute | solution.py:450
  56.7 4.4 %collective-permute-start.20 = (bf16[2,128,512]{2,1,0:T(8,128)(2,1)S(1)}, bf16[2,128,512]{2,1,0:T(8,128)(2,1)S(1)}, u32[]{:S(2)}, u32[]{:S(2)}) collective-permute-start(bf16[2,128,512]{2,1,0:T(8,128)(2,1)S(1)} %collective-permute-done.16.refs_3_), channel_id=1, source_target_pairs={{0,1},{1,0},{2,3},{3,2},{4,5},{5,4},{6,7},{7,6},{8,9},{9,8},{10,11... | collective-permute-start | bytes 786440 | tf_op jit(solution)/shard_map/ppermute | solution.py:444
  61.1 1.2 %collective-permute-start.19 = (bf16[2,128,512]{2,1,0:T(8,128)(2,1)S(1)}, bf16[2,128,512]{2,1,0:T(8,128)(2,1)S(1)}, u32[]{:S(2)}, u32[]{:S(2)}) collective-permute-start(bf16[2,128,512]{2,1,0:T(8,128)(2,1)S(1)} %collective-permute-done.15.refs_2_), channel_id=1, source_target_pairs={{0,1},{1,0},{2,3},{3,2},{4,5},{5,4},{6,7},{7,6},{8,9},{9,8},{10,11... | collective-permute-start | bytes 786440 | tf_op jit(solution)/shard_map/ppermute | solution.py:444
  62.4 2.6 %collective-permute-start.18 = (bf16[2,128,512]{2,1,0:T(8,128)(2,1)S(1)}, bf16[2,128,512]{2,1,0:T(8,128)(2,1)S(1)}, u32[]{:S(2)}, u32[]{:S(2)}) collective-permute-start(bf16[2,128,512]{2,1,0:T(8,128)(2,1)S(1)} %collective-permute-done.14.refs_1_), channel_id=1, source_target_pairs={{0,1},{1,0},{2,3},{3,2},{4,5},{5,4},{6,7},{7,6},{8,9},{9,8},{10,11... | collective-permute-start | bytes 786440 | tf_op jit(solution)/shard_map/ppermute | solution.py:444
  65.1 1.1 %collective-permute-done.18.refs_5_ = bf16[2,128,512]{2,1,0:T(8,128)(2,1)S(1)} collective-permute-done((bf16[2,128,512]{2,1,0:T(8,128)(2,1)S(1)}, bf16[2,128,512]{2,1,0:T(8,128)(2,1)S(1)}, u32[]{:S(2)}, u32[]{:S(2)}) %collective-permute-start.18) | collective-permute-done | bytes 262176 | tf_op jit(solution)/shard_map/ppermute | solution.py:444
  66.2 3.6 %cell_grads.3 = (bf16[8,128,512]{2,1,0:T(8,128)(2,1)S(1)}, bf16[8,128,512]{2,1,0:T(8,128)(2,1)S(1)}, bf16[2,1024,512]{2,1,0:T(8,128)(2,1)S(1)}, bf16[8,128,512]{2,1,0:T(8,128)(2,1)S(1)}) custom-call(s32[1]{0:T(128)} %bitcast.here, f32[8,128]{1,0:T(8,128)S(1)} %get-tuple-element.80.done, bf16[2,128,512]{2,1,0:T(8,128)(2,1)S(1)} %get-tuple-element.83.refs_0_, ...), custom_call_target="tpu_custom_call" | custom-call | flops 3000000000 | bytes 16777216 | tf_op jit(solution)/shard_map/cell_grads/pallas_call | solution.py:29
  69.8 0.3 collective-permute-start.21
  70.0 1.3 %own_products.3.keep = f32[8,128,512]{2,1,0:T(8,128)S(1)} custom-call(s32[1]{0:T(128)} %bitcast.here, bf16[8,128,512]{2,1,0:T(8,128)(2,1)S(1)} %get-tuple-element.91.w, bf16[8,128,512]{2,1,0:T(8,128)(2,1)S(1)} %get-tuple-element.92.c, bf16[2,1024,512]{2,1,0:T(8,128)(2,1)S(1)} %get-tuple-element.93.grads), custom_call_target="tpu_custom_call" | custom-call | flops 1000000000 | bytes 8388608 | tf_op jit(solution)/shard_map/own_products/pallas_call | solution.py:29
  71.3 1.2 %collective-permute-done.21.extra = bf16[8,128,512]{2,1,0:T(8,128)(2,1)S(1)} collective-permute-done((bf16[8,128,512]{2,1,0:T(8,128)(2,1)S(1)}, bf16[8,128,512]{2,1,0:T(8,128)(2,1)S(1)}, u32[]{:S(2)}, u32[]{:S(2)}) %collective-permute-start.21) | collective-permute-done | bytes 1048608 | tf_op jit(solution)/shard_map/ppermute | solution.py:444
  72.7 1.4 %collective-permute-start.22 = (bf16[2,128,512]{2,1,0:T(8,128)(2,1)S(1)}, bf16[2,128,512]{2,1,0:T(8,128)(2,1)S(1)}, u32[]{:S(2)}, u32[]{:S(2)}) collective-permute-start(bf16[2,128,512]{2,1,0:T(8,128)(2,1)S(1)} %get-tuple-element.96), channel_id=1, source_target_pairs={{0,32},{1,5},{2,34},{3,7},{4,36},{5,9},{6,38},{7,11},{8,40},{9,13}... | collective-permute-start | bytes 786440 | tf_op jit(solution)/shard_map/ppermute | solution.py:450
  74.2 2.2 %collective-permute-start.23 = (bf16[2,128,512]{2,1,0:T(8,128)(2,1)S(1)}, bf16[2,128,512]{2,1,0:T(8,128)(2,1)S(1)}, u32[]{:S(2)}, u32[]{:S(2)}) collective-permute-start(bf16[2,128,512]{2,1,0:T(8,128)(2,1)S(1)} %get-tuple-element.97), channel_id=1, source_target_pairs={{0,64},{1,9},{2,66},{3,11},{4,68},{5,13},{6,70},{7,15},{8,72},{9,1... | collective-permute-start | bytes 786440 | tf_op jit(solution)/shard_map/ppermute | solution.py:450
  76.3 1.3 %collective-permute-start.24 = (bf16[2,128,512]{2,1,0:T(8,128)(2,1)S(1)}, bf16[2,128,512]{2,1,0:T(8,128)(2,1)S(1)}, u32[]{:S(2)}, u32[]{:S(2)}) collective-permute-start(bf16[2,128,512]{2,1,0:T(8,128)(2,1)S(1)} %get-tuple-element.98), channel_id=1, source_target_pairs={{0,96},{1,13},{2,98},{3,15},{4,100},{5,1},{6,102},{7,3},{8,104},{9... | collective-permute-start | bytes 786440 | tf_op jit(solution)/shard_map/ppermute | solution.py:450
  77.7 1.8 %collective-permute-done.22.refs_1_ = bf16[2,128,512]{2,1,0:T(8,128)(2,1)S(1)} collective-permute-done((bf16[2,128,512]{2,1,0:T(8,128)(2,1)S(1)}, bf16[2,128,512]{2,1,0:T(8,128)(2,1)S(1)}, u32[]{:S(2)}, u32[]{:S(2)}) %collective-permute-start.22) | collective-permute-done | bytes 262176 | tf_op jit(solution)/shard_map/ppermute | solution.py:450
  79.5 3.4 %collective-permute-done.23.refs_2_ = bf16[2,128,512]{2,1,0:T(8,128)(2,1)S(1)} collective-permute-done((bf16[2,128,512]{2,1,0:T(8,128)(2,1)S(1)}, bf16[2,128,512]{2,1,0:T(8,128)(2,1)S(1)}, u32[]{:S(2)}, u32[]{:S(2)}) %collective-permute-start.23) | collective-permute-done | bytes 262176 | tf_op jit(solution)/shard_map/ppermute | solution.py:450
  83.0 2.1 %collective-permute-start.25 = (bf16[128,512]{1,0:T(8,128)(2,1)S(1)}, bf16[128,512]{1,0:T(8,128)(2,1)S(1)}, u32[]{:S(2)}, u32[]{:S(2)}) collective-permute-start(bf16[128,512]{1,0:T(8,128)(2,1)S(1)} %get-tuple-element.100), channel_id=1, source_target_pairs={{0,16},{1,3},{2,18},{3,1},{4,20},{5,7},{6,22},{7,5},{8,24},{9,11},... | collective-permute-start | bytes 393224 | tf_op jit(solution)/shard_map/ppermute | solution.py:447
  85.1 3.3 %collective-permute-done.25.theirs = bf16[128,512]{1,0:T(8,128)(2,1)S(1)} collective-permute-done((bf16[128,512]{1,0:T(8,128)(2,1)S(1)}, bf16[128,512]{1,0:T(8,128)(2,1)S(1)}, u32[]{:S(2)}, u32[]{:S(2)}) %collective-permute-start.25) | collective-permute-done | bytes 131104 | tf_op jit(solution)/shard_map/ppermute | solution.py:447
  88.5 1.2 %collective-permute-start.26 = (f32[128,512]{1,0:T(8,128)S(1)}, f32[128,512]{1,0:T(8,128)S(1)}, u32[]{:S(2)}, u32[]{:S(2)}) collective-permute-start(f32[128,512]{1,0:T(8,128)S(1)} %update.3.embed), channel_id=1, source_target_pairs={{0,1},{1,0},{2,3},{3,2},{4,5},{5,4},{6,7},{7,6},{8,9},{9,8},{10,11... | collective-permute-start | bytes 786440 | tf_op jit(solution)/shard_map/ppermute | solution.py:444
  89.7 1.2 %collective-permute-done.26.theirs = f32[128,512]{1,0:T(8,128)S(1)} collective-permute-done((f32[128,512]{1,0:T(8,128)S(1)}, f32[128,512]{1,0:T(8,128)S(1)}, u32[]{:S(2)}, u32[]{:S(2)}) %collective-permute-start.26) | collective-permute-done | bytes 262176 | tf_op jit(solution)/shard_map/ppermute | solution.py:444
  90.9 0.8 results.1
  (23 shorter events, 1.3 us)
Async XLA Ops:
  1.9 7.3 %collective-permute-start = (bf16[136,512]{1,0:T(8,128)(2,1)S(1)}, bf16[136,512]{1,0:T(8,128)(2,1)S(1)}, u32[]{:S(2)}, u32[]{:S(2)}) collective-permute-start(bf16[136,512]{1,0:T(8,128)(2,1)S(1)} %get-tuple-element.53.after.mine), channel_id=1, source_target_pairs={{0,16},{1,3},{2,18},{3,1},{4,20},{5,7},{6,22},{7,5},{8,24},{9,11},... | collective-permute-start | bytes 417800 | tf_op jit(solution)/shard_map/ppermute | solution.py:447
  9.3 13.6 %collective-permute-start.4 = (bf16[2,136,512]{2,1,0:T(8,128)(2,1)S(1)}, bf16[2,136,512]{2,1,0:T(8,128)(2,1)S(1)}, u32[]{:S(2)}, u32[]{:S(2)}) collective-permute-start(bf16[2,136,512]{2,1,0:T(8,128)(2,1)S(1)} %both_sides.1.after.refs_0_), channel_id=1, source_target_pairs={{0,1},{1,0},{2,3},{3,2},{4,5},{5,4},{6,7},{7,6},{8,9},{9,8},{10,11... | collective-permute-start | bytes 835592 | tf_op jit(solution)/shard_map/ppermute | solution.py:444
  9.6 10.7 %collective-permute-start.3 = (bf16[2,136,512]{2,1,0:T(8,128)(2,1)S(1)}, bf16[2,136,512]{2,1,0:T(8,128)(2,1)S(1)}, u32[]{:S(2)}, u32[]{:S(2)}) collective-permute-start(bf16[2,136,512]{2,1,0:T(8,128)(2,1)S(1)} %both_sides.1.after.refs_0_), channel_id=1, source_target_pairs={{0,64},{1,9},{2,66},{3,11},{4,68},{5,13},{6,70},{7,15},{8,72},{9,1... | collective-permute-start | bytes 835592 | tf_op jit(solution)/shard_map/ppermute | solution.py:450
  12.7 9.6 %collective-permute-start.2 = (bf16[2,136,512]{2,1,0:T(8,128)(2,1)S(1)}, bf16[2,136,512]{2,1,0:T(8,128)(2,1)S(1)}, u32[]{:S(2)}, u32[]{:S(2)}) collective-permute-start(bf16[2,136,512]{2,1,0:T(8,128)(2,1)S(1)} %both_sides.1.after.refs_0_), channel_id=1, source_target_pairs={{0,32},{1,5},{2,34},{3,7},{4,36},{5,9},{6,38},{7,11},{8,40},{9,13}... | collective-permute-start | bytes 835592 | tf_op jit(solution)/shard_map/ppermute | solution.py:450
  13.1 7.2 %collective-permute-start.1 = (bf16[2,136,512]{2,1,0:T(8,128)(2,1)S(1)}, bf16[2,136,512]{2,1,0:T(8,128)(2,1)S(1)}, u32[]{:S(2)}, u32[]{:S(2)}) collective-permute-start(bf16[2,136,512]{2,1,0:T(8,128)(2,1)S(1)} %both_sides.1.after.refs_0_), channel_id=1, source_target_pairs={{0,96},{1,13},{2,98},{3,15},{4,100},{5,1},{6,102},{7,3},{8,104},{9... | collective-permute-start | bytes 835592 | tf_op jit(solution)/shard_map/ppermute | solution.py:450
  20.3 3.2 %collective-permute-start.6 = (bf16[2,136,512]{2,1,0:T(8,128)(2,1)S(1)}, bf16[2,136,512]{2,1,0:T(8,128)(2,1)S(1)}, u32[]{:S(2)}, u32[]{:S(2)}) collective-permute-start(bf16[2,136,512]{2,1,0:T(8,128)(2,1)S(1)} %collective-permute-done.3.refs_2_), channel_id=1, source_target_pairs={{0,1},{1,0},{2,3},{3,2},{4,5},{5,4},{6,7},{7,6},{8,9},{9,8},{10,11... | collective-permute-start | bytes 835592 | tf_op jit(solution)/shard_map/ppermute | solution.py:444
  22.3 1.6 %collective-permute-start.5 = (bf16[2,136,512]{2,1,0:T(8,128)(2,1)S(1)}, bf16[2,136,512]{2,1,0:T(8,128)(2,1)S(1)}, u32[]{:S(2)}, u32[]{:S(2)}) collective-permute-start(bf16[2,136,512]{2,1,0:T(8,128)(2,1)S(1)} %collective-permute-done.2.refs_1_), channel_id=1, source_target_pairs={{0,1},{1,0},{2,3},{3,2},{4,5},{5,4},{6,7},{7,6},{8,9},{9,8},{10,11... | collective-permute-start | bytes 835592 | tf_op jit(solution)/shard_map/ppermute | solution.py:444
  22.4 1.9 %collective-permute-start.7 = (bf16[2,136,512]{2,1,0:T(8,128)(2,1)S(1)}, bf16[2,136,512]{2,1,0:T(8,128)(2,1)S(1)}, u32[]{:S(2)}, u32[]{:S(2)}) collective-permute-start(bf16[2,136,512]{2,1,0:T(8,128)(2,1)S(1)} %collective-permute-done.1.refs_3_), channel_id=1, source_target_pairs={{0,1},{1,0},{2,3},{3,2},{4,5},{5,4},{6,7},{7,6},{8,9},{9,8},{10,11... | collective-permute-start | bytes 835592 | tf_op jit(solution)/shard_map/ppermute | solution.py:444
  27.9 2.7 %collective-permute-start.8 = (bf16[8,128,512]{2,1,0:T(8,128)(2,1)S(1)}, bf16[8,128,512]{2,1,0:T(8,128)(2,1)S(1)}, u32[]{:S(2)}, u32[]{:S(2)}) collective-permute-start(bf16[8,128,512]{2,1,0:T(8,128)(2,1)S(1)} %get-tuple-element.69), channel_id=1, source_target_pairs={{0,1},{1,0},{2,3},{3,2},{4,5},{5,4},{6,7},{7,6},{8,9},{9,8},{10,11... | collective-permute-start | bytes 3145736 | tf_op jit(solution)/shard_map/ppermute | solution.py:444
  30.8 11.5 %collective-permute-start.9 = (bf16[2,128,512]{2,1,0:T(8,128)(2,1)S(1)}, bf16[2,128,512]{2,1,0:T(8,128)(2,1)S(1)}, u32[]{:S(2)}, u32[]{:S(2)}) collective-permute-start(bf16[2,128,512]{2,1,0:T(8,128)(2,1)S(1)} %get-tuple-element.75), channel_id=1, source_target_pairs={{0,32},{1,5},{2,34},{3,7},{4,36},{5,9},{6,38},{7,11},{8,40},{9,13}... | collective-permute-start | bytes 786440 | tf_op jit(solution)/shard_map/ppermute | solution.py:450
  32.2 10.2 %collective-permute-start.10 = (bf16[2,128,512]{2,1,0:T(8,128)(2,1)S(1)}, bf16[2,128,512]{2,1,0:T(8,128)(2,1)S(1)}, u32[]{:S(2)}, u32[]{:S(2)}) collective-permute-start(bf16[2,128,512]{2,1,0:T(8,128)(2,1)S(1)} %get-tuple-element.76), channel_id=1, source_target_pairs={{0,64},{1,9},{2,66},{3,11},{4,68},{5,13},{6,70},{7,15},{8,72},{9,1... | collective-permute-start | bytes 786440 | tf_op jit(solution)/shard_map/ppermute | solution.py:450
  34.8 7.5 %collective-permute-start.11 = (bf16[2,128,512]{2,1,0:T(8,128)(2,1)S(1)}, bf16[2,128,512]{2,1,0:T(8,128)(2,1)S(1)}, u32[]{:S(2)}, u32[]{:S(2)}) collective-permute-start(bf16[2,128,512]{2,1,0:T(8,128)(2,1)S(1)} %get-tuple-element.77), channel_id=1, source_target_pairs={{0,96},{1,13},{2,98},{3,15},{4,100},{5,1},{6,102},{7,3},{8,104},{9... | collective-permute-start | bytes 786440 | tf_op jit(solution)/shard_map/ppermute | solution.py:450
  35.9 12.5 %collective-permute-start.13 = (f32[128,512]{1,0:T(8,128)S(1)}, f32[128,512]{1,0:T(8,128)S(1)}, u32[]{:S(2)}, u32[]{:S(2)}) collective-permute-start(f32[128,512]{1,0:T(8,128)S(1)} %get-tuple-element.82.embed), channel_id=1, source_target_pairs={{0,16},{1,3},{2,18},{3,1},{4,20},{5,7},{6,22},{7,5},{8,24},{9,11},... | collective-permute-start | bytes 786440 | tf_op jit(solution)/shard_map/ppermute | solution.py:447
  42.5 8.4 %collective-permute-start.12 = (bf16[2,128,512]{2,1,0:T(8,128)(2,1)S(1)}, bf16[2,128,512]{2,1,0:T(8,128)(2,1)S(1)}, u32[]{:S(2)}, u32[]{:S(2)}) collective-permute-start(bf16[2,128,512]{2,1,0:T(8,128)(2,1)S(1)} %get-tuple-element.79.after), channel_id=1, source_target_pairs={{0,16},{1,3},{2,18},{3,1},{4,20},{5,7},{6,22},{7,5},{8,24},{9,11},... | collective-permute-start | bytes 786440 | tf_op jit(solution)/shard_map/ppermute | solution.py:447
  51.1 5.6 %collective-permute-start.16 = (bf16[2,128,512]{2,1,0:T(8,128)(2,1)S(1)}, bf16[2,128,512]{2,1,0:T(8,128)(2,1)S(1)}, u32[]{:S(2)}, u32[]{:S(2)}) collective-permute-start(bf16[2,128,512]{2,1,0:T(8,128)(2,1)S(1)} %get-tuple-element.83.refs_0_), channel_id=1, source_target_pairs={{0,96},{1,13},{2,98},{3,15},{4,100},{5,1},{6,102},{7,3},{8,104},{9... | collective-permute-start | bytes 786440 | tf_op jit(solution)/shard_map/ppermute | solution.py:450
  52.6 8.5 %collective-permute-start.15 = (bf16[2,128,512]{2,1,0:T(8,128)(2,1)S(1)}, bf16[2,128,512]{2,1,0:T(8,128)(2,1)S(1)}, u32[]{:S(2)}, u32[]{:S(2)}) collective-permute-start(bf16[2,128,512]{2,1,0:T(8,128)(2,1)S(1)} %get-tuple-element.83.refs_0_), channel_id=1, source_target_pairs={{0,64},{1,9},{2,66},{3,11},{4,68},{5,13},{6,70},{7,15},{8,72},{9,1... | collective-permute-start | bytes 786440 | tf_op jit(solution)/shard_map/ppermute | solution.py:450
  53.8 8.6 %collective-permute-start.14 = (bf16[2,128,512]{2,1,0:T(8,128)(2,1)S(1)}, bf16[2,128,512]{2,1,0:T(8,128)(2,1)S(1)}, u32[]{:S(2)}, u32[]{:S(2)}) collective-permute-start(bf16[2,128,512]{2,1,0:T(8,128)(2,1)S(1)} %get-tuple-element.83.refs_0_), channel_id=1, source_target_pairs={{0,32},{1,5},{2,34},{3,7},{4,36},{5,9},{6,38},{7,11},{8,40},{9,13}... | collective-permute-start | bytes 786440 | tf_op jit(solution)/shard_map/ppermute | solution.py:450
  54.0 11.0 %collective-permute-start.17 = (bf16[2,128,512]{2,1,0:T(8,128)(2,1)S(1)}, bf16[2,128,512]{2,1,0:T(8,128)(2,1)S(1)}, u32[]{:S(2)}, u32[]{:S(2)}) collective-permute-start(bf16[2,128,512]{2,1,0:T(8,128)(2,1)S(1)} %get-tuple-element.83.refs_0_), channel_id=1, source_target_pairs={{0,1},{1,0},{2,3},{3,2},{4,5},{5,4},{6,7},{7,6},{8,9},{9,8},{10,11... | collective-permute-start | bytes 786440 | tf_op jit(solution)/shard_map/ppermute | solution.py:444
  56.7 8.3 %collective-permute-start.20 = (bf16[2,128,512]{2,1,0:T(8,128)(2,1)S(1)}, bf16[2,128,512]{2,1,0:T(8,128)(2,1)S(1)}, u32[]{:S(2)}, u32[]{:S(2)}) collective-permute-start(bf16[2,128,512]{2,1,0:T(8,128)(2,1)S(1)} %collective-permute-done.16.refs_3_), channel_id=1, source_target_pairs={{0,1},{1,0},{2,3},{3,2},{4,5},{5,4},{6,7},{7,6},{8,9},{9,8},{10,11... | collective-permute-start | bytes 786440 | tf_op jit(solution)/shard_map/ppermute | solution.py:444
  61.1 4.0 %collective-permute-start.19 = (bf16[2,128,512]{2,1,0:T(8,128)(2,1)S(1)}, bf16[2,128,512]{2,1,0:T(8,128)(2,1)S(1)}, u32[]{:S(2)}, u32[]{:S(2)}) collective-permute-start(bf16[2,128,512]{2,1,0:T(8,128)(2,1)S(1)} %collective-permute-done.15.refs_2_), channel_id=1, source_target_pairs={{0,1},{1,0},{2,3},{3,2},{4,5},{5,4},{6,7},{7,6},{8,9},{9,8},{10,11... | collective-permute-start | bytes 786440 | tf_op jit(solution)/shard_map/ppermute | solution.py:444
  62.4 3.8 %collective-permute-start.18 = (bf16[2,128,512]{2,1,0:T(8,128)(2,1)S(1)}, bf16[2,128,512]{2,1,0:T(8,128)(2,1)S(1)}, u32[]{:S(2)}, u32[]{:S(2)}) collective-permute-start(bf16[2,128,512]{2,1,0:T(8,128)(2,1)S(1)} %collective-permute-done.14.refs_1_), channel_id=1, source_target_pairs={{0,1},{1,0},{2,3},{3,2},{4,5},{5,4},{6,7},{7,6},{8,9},{9,8},{10,11... | collective-permute-start | bytes 786440 | tf_op jit(solution)/shard_map/ppermute | solution.py:444
  69.8 2.7 %collective-permute-start.21 = (bf16[8,128,512]{2,1,0:T(8,128)(2,1)S(1)}, bf16[8,128,512]{2,1,0:T(8,128)(2,1)S(1)}, u32[]{:S(2)}, u32[]{:S(2)}) collective-permute-start(bf16[8,128,512]{2,1,0:T(8,128)(2,1)S(1)} %get-tuple-element.94), channel_id=1, source_target_pairs={{0,1},{1,0},{2,3},{3,2},{4,5},{5,4},{6,7},{7,6},{8,9},{9,8},{10,11... | collective-permute-start | bytes 3145736 | tf_op jit(solution)/shard_map/ppermute | solution.py:444
  72.7 6.8 %collective-permute-start.22 = (bf16[2,128,512]{2,1,0:T(8,128)(2,1)S(1)}, bf16[2,128,512]{2,1,0:T(8,128)(2,1)S(1)}, u32[]{:S(2)}, u32[]{:S(2)}) collective-permute-start(bf16[2,128,512]{2,1,0:T(8,128)(2,1)S(1)} %get-tuple-element.96), channel_id=1, source_target_pairs={{0,32},{1,5},{2,34},{3,7},{4,36},{5,9},{6,38},{7,11},{8,40},{9,13}... | collective-permute-start | bytes 786440 | tf_op jit(solution)/shard_map/ppermute | solution.py:450
  74.2 8.7 %collective-permute-start.23 = (bf16[2,128,512]{2,1,0:T(8,128)(2,1)S(1)}, bf16[2,128,512]{2,1,0:T(8,128)(2,1)S(1)}, u32[]{:S(2)}, u32[]{:S(2)}) collective-permute-start(bf16[2,128,512]{2,1,0:T(8,128)(2,1)S(1)} %get-tuple-element.97), channel_id=1, source_target_pairs={{0,64},{1,9},{2,66},{3,11},{4,68},{5,13},{6,70},{7,15},{8,72},{9,1... | collective-permute-start | bytes 786440 | tf_op jit(solution)/shard_map/ppermute | solution.py:450
  76.3 6.6 %collective-permute-start.24 = (bf16[2,128,512]{2,1,0:T(8,128)(2,1)S(1)}, bf16[2,128,512]{2,1,0:T(8,128)(2,1)S(1)}, u32[]{:S(2)}, u32[]{:S(2)}) collective-permute-start(bf16[2,128,512]{2,1,0:T(8,128)(2,1)S(1)} %get-tuple-element.98), channel_id=1, source_target_pairs={{0,96},{1,13},{2,98},{3,15},{4,100},{5,1},{6,102},{7,3},{8,104},{9... | collective-permute-start | bytes 786440 | tf_op jit(solution)/shard_map/ppermute | solution.py:450
  83.0 5.4 %collective-permute-start.25 = (bf16[128,512]{1,0:T(8,128)(2,1)S(1)}, bf16[128,512]{1,0:T(8,128)(2,1)S(1)}, u32[]{:S(2)}, u32[]{:S(2)}) collective-permute-start(bf16[128,512]{1,0:T(8,128)(2,1)S(1)} %get-tuple-element.100), channel_id=1, source_target_pairs={{0,16},{1,3},{2,18},{3,1},{4,20},{5,7},{6,22},{7,5},{8,24},{9,11},... | collective-permute-start | bytes 393224 | tf_op jit(solution)/shard_map/ppermute | solution.py:447
  88.5 2.4 %collective-permute-start.26 = (f32[128,512]{1,0:T(8,128)S(1)}, f32[128,512]{1,0:T(8,128)S(1)}, u32[]{:S(2)}, u32[]{:S(2)}) collective-permute-start(f32[128,512]{1,0:T(8,128)S(1)} %update.3.embed), channel_id=1, source_target_pairs={{0,1},{1,0},{2,3},{3,2},{4,5},{5,4},{6,7},{7,6},{8,9},{9,8},{10,11... | collective-permute-start | bytes 786440 | tf_op jit(solution)/shard_map/ppermute | solution.py:444
